TPU v7x, 32 devices: a whole 2x2x4 slice. The times are simulated.
32 devices in a mesh: groups: 2 (over y), lat: 4 (over z), lev: 2 (over x), tr: 2 (over core).
Axes of the slice: x: 2, y: 2, z: 4, core: 2. Of those that a mesh axis runs over, the one named last changes fastest.
Arguments:
- adjoint_in: float32 [4, 24, 32, 512], P(('groups', 'tr'), 'lev', 'lat'), parts along dimension 0, may hold values from -6 to 6
- courant: float32 [2, 24, 32, 512], P(None, 'lev', 'lat'), may hold values from -0.45 to 0.45
- diffusion: float32 [23, 32, 512], P(None, 'lat', 'lev'), may hold values from 0.3 to 6
- tile_values: float32 [4, 24, 256, 128], P(('groups', 'tr'), 'lev', 'lat'), parts along dimension 0, may hold values from -6 to 6
- tile_region: int32 [512, 1], P(('groups', 'lat')), parts along dimension 0, may hold values from 0 to 3; in each aligned block of 64 rows (0 to 63, 64 to 127, ...) at most 16 rows name the same one
- tile_cell: int32 [512], P(('groups', 'lat')), parts along dimension 0, may hold values from 0 to 31
Outputs:
- adjoint_out: float32 [4, 24, 32, 512], P(('groups', 'tr'), 'lev', 'lat'), parts along dimension 0
- flux_gradient: float32 [4, 32, 512], P(('groups', 'tr'), 'lat', 'lev'), parts along dimension 0
There are 2 independent parts, one for each index of `groups`. A program takes and returns all parts, laid end to end along the dimension named above; an argument that names none is the same for every part. Nothing has to cross between parts.
Inputs may be any that keep to these rules, and one draw needn't show every extreme that they name: `tile_region`: among the tiles of one index of lat (aligned blocks of 64 tiles) at most 16 name any one band, a bound that some block reaches of them.
All inputs are finite; a program needn't handle non-finite values.
Results may differ from a plain program's by a relative error of at most 0.0001.
Values sent between devices are 32-bit elements; how exact they have to be, the bound alone decides.
No kernel may reach another device: no remote copies, remote signals or barrier semaphores. Data moves between devices by JAX's collectives and lax.ppermute only.
A program may use at most 64 MiB of HBM per device.

v0:
```python
import functools

import jax
import jax.numpy as jnp
from jax import lax
from jax.experimental import pallas as pl
from jax.experimental.pallas import tpu as pltpu
from jax.sharding import PartitionSpec as P

STEPS = 6
HALO = STEPS
LANES = 128
F32 = jnp.float32


def call(body, out_shapes, *args, scratch=()):
    spec = pl.BlockSpec(memory_space=pltpu.VMEM)
    return pl.pallas_call(
        body,
        out_shape=[jax.ShapeDtypeStruct(shape, F32) for shape in out_shapes],
        in_specs=[spec] * len(args),
        out_specs=[spec] * len(out_shapes),
        scratch_shapes=[pltpu.VMEM(shape, F32) for shape in scratch],
        compiler_params=pltpu.CompilerParams(vmem_limit_bytes=32 * 1024 * 1024),
    )(*args)


def partner_of(index, turn, count):
    if count & (count - 1) == 0:
        return index ^ turn
    return (index + turn) % count


def source_of(index, turn, count):
    if count & (count - 1) == 0:
        return index ^ turn
    return (index - turn) % count


def rounds(count):
    return [[(b, partner_of(b, turn, count)) for b in range(count)] for turn in range(1, count)]


def band_swaps(bands, first):
    swaps = []
    for b in range(bands):
        partner = b + 1 if (b - first) % 2 == 0 else b - 1
        swaps.append((b, partner if 0 <= partner < bands else b))
    return swaps


class Plan:
    def __init__(self, count, rows, width, devices):
        self.count, self.rows, self.width, self.devices = count, rows, width, devices
        self.levels = count * devices
        self.chunk = width // devices
        self.full = self.chunk // LANES
        self.rest = self.chunk % LANES
        self.window = (self.full + 1) * LANES
        assert self.rest + 2 * HALO <= LANES
        self.middle = (self.rest + LANES) // 2
        self.pitch = -(-(self.rest + 2 * HALO) // 16) * 16
        self.slots = LANES // self.pitch
        self.edge_slots = LANES // 16
        fields = 3 * count
        self.rests_at = fields * self.full
        self.diffusion_at = self.rests_at + -(-fields // self.slots)
        self.diffusion_tiles = -(-self.chunk // LANES)
        self.own_size = self.diffusion_at + (self.levels - 1) * self.diffusion_tiles
        self.sent_size = self.diffusion_at + -(-(self.levels - 1) // self.edge_slots)

    def packed(self, size):
        return size - size // 4 if 4 * HALO == 3 * self.rows else size


def lane_of(rows=8):
    return lax.broadcasted_iota(jnp.int32, (rows, LANES), 1)


def row_of(rows=8):
    return lax.broadcasted_iota(jnp.int32, (rows, LANES), 0)


def turn_lanes(tile, shift):
    return pltpu.roll(tile, shift % LANES, 1) if shift % LANES else tile


def turn_rows(tile, shift):
    rows = tile.shape[0]
    return pltpu.roll(tile, shift % rows, 0) if shift % rows else tile


def pack_lanes(tiles, slots, pitch):
    packed = []
    lane = lane_of(tiles[0].shape[0])
    for begin in range(0, len(tiles), slots):
        total = jnp.zeros_like(tiles[0])
        for slot, tile in enumerate(tiles[begin : begin + slots]):
            moved = turn_lanes(tile, HALO + slot * pitch)
            if slots > 1:
                moved = jnp.where((lane >= slot * pitch) & (lane < (slot + 1) * pitch), moved, total)
            total = moved
        packed.append(total)
    return packed


def unpack_lanes(tile, slot, pitch):
    return turn_lanes(tile, -HALO - slot * pitch)


def window_tiles(plan, ref, index, target):
    if plan.rest == 0:
        def at(column):
            return ref[index + (slice(None), pl.ds(pl.multiple_of(column, LANES), LANES))]

        full = [at(target * plan.chunk + t * LANES) for t in range(plan.full)]
        east = at(lax.rem(target + 1, plan.devices) * plan.chunk)
        west = at(lax.rem(target + plan.devices - 1, plan.devices) * plan.chunk + plan.chunk - LANES)
    else:
        line = pltpu.roll(ref[index], lax.rem(plan.width - target * plan.chunk, plan.width), 1)
        full = [line[:, t * LANES : (t + 1) * LANES] for t in range(plan.full)]
        east = line[:, plan.full * LANES : (plan.full + 1) * LANES]
        west = line[:, plan.width - LANES :]
    return full, jnp.where(lane_of(plan.rows) < plan.middle, east, west)


def field_tiles(plan, field, courant, target):
    tiles, rests = [], []
    for ref, lead in ((field, ()), (courant, (0,)), (courant, (1,))):
        for level in range(plan.count):
            full, rest = window_tiles(plan, ref, lead + (level,), target)
            tiles += full
            rests.append(rest)
    return tiles + pack_lanes(rests, plan.slots, plan.pitch)


def diffusion_tile(plan, diffusion, level, t):
    width = min(LANES, plan.chunk - t * LANES)
    tile = diffusion[level, :, t * LANES : t * LANES + width]
    if width < LANES:
        tile = jnp.concatenate([tile, jnp.zeros((plan.rows, LANES - width), F32)], axis=1)
    return tile


def pack_rows(plan, get, size, north, store):
    first = plan.rows - HALO if north else 0
    row = row_of(plan.rows)
    place = 0
    fours = size // 4 if plan.packed(size) < size else 0
    for four in range(fours):
        tiles = [get(4 * four + j) for j in range(4)]
        for j in range(3):
            extra = turn_rows(tiles[3], HALO - first - 2 * j)
            store(place, jnp.where(row < HALO, turn_rows(tiles[j], -first), extra))
            place += 1
    for index in range(4 * fours, size):
        store(place, turn_rows(get(index), -first))
        place += 1


def unpack_rows(plan, get, size, north, store):
    first = plan.rows - HALO if north else 0
    row = row_of(plan.rows)
    place = 0
    fours = size // 4 if plan.packed(size) < size else 0
    for four in range(fours):
        tiles = [get(place + j) for j in range(3)]
        place += 3
        last = jnp.zeros_like(tiles[0])
        for j in range(3):
            store(4 * four + j, turn_rows(tiles[j], first))
            moved = turn_rows(tiles[j], first + 2 * j - HALO)
            last = jnp.where((row >= first + 2 * j) & (row < first + 2 * j + 2), moved, last)
        store(4 * four + 3, last)
    for index in range(4 * fours, size):
        store(index, turn_rows(get(place), first))
        place += 1


def by_parity(body):
    even = lax.rem(lax.axis_index("lat"), 2) == 0

    @pl.when(even)
    def _():
        body(True)

    @pl.when(jnp.logical_not(even))
    def _():
        body(False)


def pack_body(plan, field, courant, diffusion, own, swap_a, swap_b, *sent):
    me = lax.axis_index("lev")
    tiles = field_tiles(plan, field, courant, me)
    for level in range(plan.levels - 1):
        tiles += [diffusion_tile(plan, diffusion, level, t) for t in range(plan.diffusion_tiles)]
    for index, tile in enumerate(tiles):
        own[index] = tile
    edges = []
    for level in range(plan.levels - 1):
        first = diffusion_tile(plan, diffusion, level, 0)
        last = turn_lanes(diffusion_tile(plan, diffusion, level, plan.diffusion_tiles - 1), -plan.rest)
        edges.append(jnp.where(lane_of(plan.rows) < LANES // 2, first, last))
    edges = pack_lanes(edges, plan.edge_slots, 16)
    for turn in range(1, plan.devices):
        target = partner_of(me, turn, plan.devices)
        for index, tile in enumerate(field_tiles(plan, field, courant, target) + edges):
            sent[turn - 1][index] = tile

    def rows(even):
        for north, swap in ((even, swap_a), (not even, swap_b)):
            pack_rows(plan, lambda i: own[i], plan.own_size, north, swap.__setitem__)

    by_parity(rows)


def forward_rows_body(plan, *refs):
    turns = plan.devices - 1
    got, swap_a, swap_b = refs[:turns], refs[turns], refs[turns + 1]
    size = plan.packed(plan.sent_size)

    def rows(even):
        for north, swap in ((even, swap_a), (not even, swap_b)):
            for turn in range(turns):
                def store(index, tile, base=turn * size, swap=swap):
                    swap[base + index] = tile

                pack_rows(plan, lambda i, turn=turn: got[turn][i], plan.sent_size, north, store)

    by_parity(rows)


def steps_body(plan, bands, *refs):
    turns = plan.devices - 1
    own, early_a, early_b, late_a, late_b = refs[:5]
    got = refs[5 : 5 + turns]
    outs = refs[5 + turns : 5 + turns + plan.devices]
    flux = refs[5 + turns + plan.devices]
    lists, lam, face_e, face_w, lat_e, lat_w, r, a, g = refs[6 + turns + plan.devices :]
    me, band = lax.axis_index("lev"), lax.axis_index("lat")
    rows, levels = plan.rows, plan.levels

    late_size = plan.packed(plan.sent_size)

    def unpack(even):
        for side, from_north in ((1, True), (2, False)):
            early, late = (early_a, late_a) if even == from_north else (early_b, late_b)

            def store(index, tile, base=0, side=side):
                lists[side - 1, base + index] = tile

            unpack_rows(plan, lambda i, e=early: e[i], plan.own_size, not from_north, store)
            for turn in range(turns):
                base = plan.own_size + turn * plan.sent_size
                unpack_rows(
                    plan,
                    lambda i, l=late, t=turn: l[t * late_size + i],
                    plan.sent_size,
                    not from_north,
                    functools.partial(store, base=base),
                )

    by_parity(unpack)

    def tile_of(side, turn, index):
        if side:
            return lists[side - 1, index if turn == 0 else plan.own_size + (turn - 1) * plan.sent_size + index]
        return own[index] if turn == 0 else got[turn - 1][index]

    lane = lane_of(rows)
    for side in range(3):
        at = pl.ds(side * rows, rows)
        for turn in range(plan.devices):
            base = source_of(me, turn, plan.devices) * plan.count if turn else me * plan.count
            for kind, target in enumerate((lam, face_w, lat_w)):
                for level in range(plan.count):
                    item = kind * plan.count + level
                    for t in range(plan.full):
                        target[base + level, at, t * LANES : (t + 1) * LANES] = tile_of(side, turn, item * plan.full + t)
                    rest = tile_of(side, turn, plan.rests_at + item // plan.slots)
                    target[base + level, at, plan.full * LANES :] = unpack_lanes(rest, item % plan.slots, plan.pitch)
        for level in range(levels - 1):
            for t in range(plan.full):
                g[level, at, t * LANES : (t + 1) * LANES] = tile_of(
                    side, 0, plan.diffusion_at + level * plan.diffusion_tiles + t
                )
            east = west = jnp.zeros((rows, LANES), F32)
            for turn in range(1, plan.devices):
                edge = tile_of(side, turn, plan.diffusion_at + level // plan.edge_slots)
                edge = unpack_lanes(edge, level % plan.edge_slots, 16)
                if turns == 1:
                    east = west = edge
                else:
                    source = source_of(me, turn, plan.devices)
                    east = jnp.where(source == lax.rem(me + 1, plan.devices), edge, east)
                    west = jnp.where(source == lax.rem(me + plan.devices - 1, plan.devices), edge, west)
            rest = jnp.where(lane < plan.middle, turn_lanes(east, plan.rest), west)
            if plan.rest:
                mine = tile_of(side, 0, plan.diffusion_at + level * plan.diffusion_tiles + plan.full)
                rest = jnp.where(lane < plan.rest, mine, rest)
            g[level, at, plan.full * LANES :] = rest

    row = lax.broadcasted_iota(jnp.int32, (3 * rows, plan.window), 0)
    closed = ((row == 0) & (band == 0)) | ((row == rows) & (band == bands - 1))
    zero = jnp.zeros((3 * rows, plan.window), F32)
    k_prev = gain = zero
    for level in range(levels):
        south = jnp.where(closed, 0.0, lat_w[level])
        lat_e[level] = jnp.maximum(pltpu.roll(south, 3 * rows - 1, 0), 0.0)
        lat_w[level] = jnp.minimum(south, 0.0)
        west = face_w[level]
        face_e[level] = jnp.maximum(pltpu.roll(west, plan.window - 1, 1), 0.0)
        face_w[level] = jnp.minimum(west, 0.0)
        k_next = g[level] if level < levels - 1 else zero
        inverse = 1.0 / (1.0 + k_prev + k_next - k_prev * gain)
        gain = k_next * inverse
        r[level], a[level], g[level] = inverse, k_prev * inverse, gain
        k_prev = k_next

    flux[...] = jnp.zeros_like(flux)

    def step(_, carry):
        y = zero
        for level in range(levels):
            y = lam[level] * r[level] + a[level] * y
            lam[level] = y
        w = zero
        for level in range(levels - 1, -1, -1):
            w = lam[level] + g[level] * w
            up, down = pltpu.roll(w, 3 * rows - 1, 0), pltpu.roll(w, 1, 0)
            v = w + lat_e[level] * (up - w) + lat_w[level] * (w - down)
            east, west = pltpu.roll(v, plan.window - 1, 1), pltpu.roll(v, 1, 1)
            lam[level] = v + face_e[level] * (east - v) + face_w[level] * (v - west)
        flux[...] += w[:rows, : plan.chunk]
        return carry

    lax.fori_loop(0, STEPS, step, 0)
    flux[...] = flux[...] / STEPS
    for turn in range(plan.devices):
        base = (partner_of(me, turn, plan.devices) if turn else me) * plan.count
        for level in range(plan.count):
            outs[turn][level] = lam[base + level, :rows, : plan.chunk]


def finish_body(plan, regions, *refs):
    parts, buckets, out = refs[: plan.devices], refs[plan.devices : -1], refs[-1]
    count, rows, width = plan.count, plan.rows, plan.width
    me = lax.axis_index("lev")
    cells = jnp.concatenate([bucket[count] for bucket in buckets], axis=0)
    tile = cells.shape[1]
    blocks = width // tile
    lane = lax.broadcasted_iota(jnp.int32, cells.shape, 1)
    place = (lane % rows * blocks + lane // rows).astype(F32)
    hits = jnp.where((cells == place) & (lane < rows * blocks), 1.0, 0.0)
    hits = hits.T[: rows * blocks]
    for level in range(count):
        values = jnp.concatenate([bucket[level] for bucket in buckets], axis=0)
        added = lax.dot_general(
            hits, values, (((1,), (0,)), ((), ())), precision=lax.Precision.HIGHEST, preferred_element_type=F32
        )
        chunks = []
        for q in range(plan.devices):
            piece = parts[0][level]
            for turn in range(1, plan.devices):
                piece = jnp.where(source_of(me, turn, plan.devices) == q, parts[turn][level], piece)
            chunks.append(piece)
        v = jnp.concatenate(chunks, axis=1)
        for block in range(blocks):
            out[level, :, block * tile : (block + 1) * tile] = (
                v[:, block * tile : (block + 1) * tile] + added[block * rows : (block + 1) * rows]
            )


def bucket_body(regions, values, region_column, region_row, cell_column, *outs):
    count, tiles, tile = values.shape
    capacity = outs[0].shape[1]
    band = lax.axis_index("lat")
    earlier = lax.broadcasted_iota(jnp.int32, (tiles, tiles), 0) < lax.broadcasted_iota(jnp.int32, (tiles, tiles), 1)
    same = (region_column[...] == region_row[...]) & earlier
    rank = jnp.sum(jnp.where(same, 1.0, 0.0), axis=0, keepdims=True).astype(jnp.int32)
    slot = lax.broadcasted_iota(jnp.int32, (capacity, tiles), 0)
    cells = jnp.broadcast_to(cell_column[...].astype(F32), (tiles, tile))
    picks = [
        jnp.where((slot == rank) & (region_row[...] == partner_of(band, s, regions)), 1.0, 0.0) for s in range(regions)
    ]
    picks = jnp.concatenate(picks, axis=0)
    for level in range(count + 1):
        got = lax.dot_general(
            picks,
            cells if level == count else values[level],
            (((1,), (0,)), ((), ())),
            precision=lax.Precision.HIGHEST,
            preferred_element_type=F32,
        )
        for s in range(regions):
            outs[s][level] = got[s * capacity : (s + 1) * capacity]


def route_tiles(tile_values, tile_region, tile_cell):
    regions = lax.axis_size("lat")
    count, tiles, tile = tile_values.shape
    outs = call(
        functools.partial(bucket_body, regions),
        [(count + 1, tiles // 4, tile)] * regions,
        tile_values,
        tile_region,
        tile_region.reshape(1, tiles),
        tile_cell.reshape(tiles, 1),
    )
    return [outs[0]] + [lax.ppermute(out, "lat", pairs) for out, pairs in zip(outs[1:], rounds(regions))]


def local(adjoint_in, courant, diffusion, tile_values, tile_region, tile_cell):
    field = adjoint_in[0]
    count, rows, width = field.shape
    devices = lax.axis_size("lev")
    bands = lax.axis_size("lat")
    plan = Plan(count, rows, width, devices)
    swaps_a, swaps_b = band_swaps(bands, 0), band_swaps(bands, 1)
    tile = (rows, LANES)

    early = plan.packed(plan.own_size)
    late = plan.packed(plan.sent_size) * (devices - 1)
    own, early_a, early_b, *sent = call(
        functools.partial(pack_body, plan),
        [(plan.own_size,) + tile] + [(early,) + tile] * 2 + [(plan.sent_size,) + tile] * (devices - 1),
        field,
        courant,
        diffusion,
    )
    got = [lax.ppermute(part, "lev", pairs) for part, pairs in zip(sent, rounds(devices))]
    early_a = lax.ppermute(early_a, "lat", swaps_a)
    early_b = lax.ppermute(early_b, "lat", swaps_b)
    late_a, late_b = call(functools.partial(forward_rows_body, plan), [(late,) + tile] * 2, *got)
    late_a = lax.ppermute(late_a, "lat", swaps_a)
    late_b = lax.ppermute(late_b, "lat", swaps_b)

    whole = (plan.levels, 3 * rows, plan.window)
    lists = (2, plan.own_size + (devices - 1) * plan.sent_size) + tile
    *outs, flux = call(
        functools.partial(steps_body, plan, bands),
        [(count, rows, plan.chunk)] * devices + [(rows, plan.chunk)],
        own,
        early_a,
        early_b,
        late_a,
        late_b,
        *got,
        scratch=[lists] + [whole] * 8,
    )
    parts = [outs[0]] + [lax.ppermute(part, "lev", pairs) for part, pairs in zip(outs[1:], rounds(devices))]
    buckets = route_tiles(tile_values[0], tile_region, tile_cell)
    (out,) = call(functools.partial(finish_body, plan, bands), [(count, rows, width)], *parts, *buckets)
    return out[None], flux[None]


def solution(mesh):
    return jax.shard_map(
        local,
        mesh=mesh,
        in_specs=(
            P(("groups", "tr"), "lev", "lat", None),
            P(None, "lev", "lat", None),
            P(None, "lat", "lev"),
            P(("groups", "tr"), "lev", "lat", None),
            P(("groups", "lat"), None),
            P(("groups", "lat")),
        ),
        out_specs=(P(("groups", "tr"), "lev", "lat", None), P(("groups", "tr"), "lat", "lev")),
        check_vma=False,
    )
```

profile of v0, /device:TPU:16, one launch (start us, length us, event | category | flops | bytes accessed | tf_op | source)
XLA Modules:
  0.0 43.0 jit_solution(4540077994369594430)
XLA Ops:
  0.6 0.0 copy-start
  0.6 1.0 %copy-done = f32[2,12,8,512]{3,2,1,0:T(8,128)S(1)} copy-done((f32[2,12,8,512]{3,2,1,0:T(8,128)S(1)}, f32[2,12,8,512]{3,2,1,0:T(8,128)}, u32[]{:S(2)}) %copy-start) | copy-done | bytes 393240
  1.6 0.9 %copy-done.2 = f32[1,12,8,512]{3,2,1,0:T(8,128)S(1)} copy-done((f32[1,12,8,512]{3,2,1,0:T(8,128)S(1)}, f32[1,12,8,512]{3,2,1,0:T(8,128)}, u32[]{:S(2)}) %copy-start.2) | copy-done | bytes 196632
  2.6 0.9 %copy-done.3 = f32[23,8,256]{2,1,0:T(8,128)S(1)} copy-done((f32[23,8,256]{2,1,0:T(8,128)S(1)}, f32[23,8,256]{2,1,0:T(8,128)}, u32[]{:S(2)}) %copy-start.3) | copy-done | bytes 188440
  3.5 0.4 shard_map.77
  3.9 0.0 copy-start.1
  3.9 1.6 %collective-permute-start.2 = (f32[80,8,128]{2,1,0:T(8,128)S(1)}, f32[80,8,128]{2,1,0:T(8,128)S(1)}, u32[]{:S(2)}, u32[]{:S(2)}) collective-permute-start(f32[80,8,128]{2,1,0:T(8,128)S(1)} %get-tuple-element.18), channel_id=1, source_target_pairs={{0,2},{2,0},{1,3},{3,1},{4,6},{6,4},{5,7},{7,5},{8,10},{10,8},{9,1... | collective-permute-start | bytes 983048 | tf_op jit(solution)/shard_map/ppermute | solution.py:431
  5.4 1.6 %collective-permute-start = (f32[93,8,128]{2,1,0:T(8,128)S(1)}, f32[93,8,128]{2,1,0:T(8,128)S(1)}, u32[]{:S(2)}, u32[]{:S(2)}) collective-permute-start(f32[93,8,128]{2,1,0:T(8,128)S(1)} %get-tuple-element.16), channel_id=1, source_target_pairs={{0,4},{4,0},{8,12},{12,8},{1,5},{5,1},{9,13},{13,9},{2,6},{6,2},{1... | collective-permute-start | bytes 1142792 | tf_op jit(solution)/shard_map/ppermute | solution.py:432
  7.0 1.9 %collective-permute-start.1 = (f32[93,8,128]{2,1,0:T(8,128)S(1)}, f32[93,8,128]{2,1,0:T(8,128)S(1)}, u32[]{:S(2)}, u32[]{:S(2)}) collective-permute-start(f32[93,8,128]{2,1,0:T(8,128)S(1)} %get-tuple-element.17), channel_id=1, source_target_pairs={{0,0},{4,8},{8,4},{12,12},{1,1},{5,9},{9,5},{13,13},{2,2},{6,10},{... | collective-permute-start | bytes 1142792 | tf_op jit(solution)/shard_map/ppermute | solution.py:433
  8.9 4.5 %collective-permute-done.2.refs_0_.refs_5_ = f32[80,8,128]{2,1,0:T(8,128)S(1)} collective-permute-done((f32[80,8,128]{2,1,0:T(8,128)S(1)}, f32[80,8,128]{2,1,0:T(8,128)S(1)}, u32[]{:S(2)}, u32[]{:S(2)}) %collective-permute-start.2) | collective-permute-done | bytes 327712 | tf_op jit(solution)/shard_map/ppermute | solution.py:431
  13.4 0.7 %shard_map.78 = (f32[60,8,128]{2,1,0:T(8,128)}, f32[60,8,128]{2,1,0:T(8,128)S(1)}) custom-call(f32[80,8,128]{2,1,0:T(8,128)S(1)} %collective-permute-done.2.refs_0_.refs_5_), custom_call_target="tpu_custom_call" | custom-call | tf_op jit(solution)/shard_map/pallas_call | solution.py:18
  14.1 1.6 %collective-permute-start.3 = (f32[60,8,128]{2,1,0:T(8,128)}, f32[60,8,128]{2,1,0:T(8,128)S(1)}, u32[]{:S(2)}, u32[]{:S(2)}) collective-permute-start(f32[60,8,128]{2,1,0:T(8,128)} %get-tuple-element.19), channel_id=1, source_target_pairs={{0,4},{4,0},{8,12},{12,8},{1,5},{5,1},{9,13},{13,9},{2,6},{6,2},{1... | collective-permute-start | bytes 737288 | tf_op jit(solution)/shard_map/ppermute | solution.py:435
  15.7 1.9 %collective-permute-start.4 = (f32[60,8,128]{2,1,0:T(8,128)S(1)}, f32[60,8,128]{2,1,0:T(8,128)S(1)}, u32[]{:S(2)}, u32[]{:S(2)}) collective-permute-start(f32[60,8,128]{2,1,0:T(8,128)S(1)} %get-tuple-element.20), channel_id=1, source_target_pairs={{0,0},{4,8},{8,4},{12,12},{1,1},{5,9},{9,5},{13,13},{2,2},{6,10},{... | collective-permute-start | bytes 737288 | tf_op jit(solution)/shard_map/ppermute | solution.py:436
  17.6 0.0 copy-done.4
  17.6 0.1 copy.8.region_column
  17.7 0.7 %copy.9.cell_column = s32[64,1]{1,0:T(8,128)S(1)} copy(s32[64,1]{0,1:T(1,128)} %bitcast.10) | data formatting | bytes 512 | tf_op jit(solution)/shard_map/reshape | solution.py:408
  18.5 0.0 copy-done.1
  18.5 0.6 %shard_map.80 = (f32[13,16,128]{2,1,0:T(8,128)S(1)}, f32[13,16,128]{2,1,0:T(8,128)S(1)}, f32[13,16,128]{2,1,0:T(8,128)S(1)}, f32[13,16,128]{2,1,0:T(8,128)S(1)}) custom-call(f32[12,64,128]{2,1,0:T(8,128)S(1)} %bitcast.6, s32[64,1]{1,0:T(8,128)S(1)} %copy.8.region_column, s32[1,64]{1,0:T(1,128)S(1)} %bitcast.8, s32[64,1]{1,0:T(8,128)S(1)} %copy.9.cell_column), custom_call_target="tpu_custom_call" | custom-call | tf_op jit(solution)/shard_map/pallas_call | solution.py:18
  19.0 0.0 collective-permute-start.6
  19.1 0.0 collective-permute-done.refs_1_
  19.1 3.5 %collective-permute-start.7 = (f32[13,16,128]{2,1,0:T(8,128)S(1)}, f32[13,16,128]{2,1,0:T(8,128)S(1)}, u32[]{:S(2)}, u32[]{:S(2)}) collective-permute-start(f32[13,16,128]{2,1,0:T(8,128)S(1)} %get-tuple-element.25), channel_id=1, source_target_pairs={{0,8},{4,12},{8,0},{12,4},{1,9},{5,13},{9,1},{13,5},{2,10},{6,14},... | collective-permute-start | bytes 319496 | tf_op jit(solution)/shard_map/ppermute | solution.py:410
  22.5 0.0 collective-permute-done.1.refs_2_
  22.6 0.0 collective-permute-start.8
  22.6 0.0 collective-permute-done.3.refs_3_
  22.6 8.5 %collective-permute-done.4.refs_4_ = f32[60,8,128]{2,1,0:T(8,128)S(1)} collective-permute-done((f32[60,8,128]{2,1,0:T(8,128)S(1)}, f32[60,8,128]{2,1,0:T(8,128)S(1)}, u32[]{:S(2)}, u32[]{:S(2)}) %collective-permute-start.4) | collective-permute-done | bytes 245792 | tf_op jit(solution)/shard_map/ppermute | solution.py:436
  31.0 6.2 %shard_map.79 = (f32[12,8,256]{2,1,0:T(8,128)S(1)}, f32[12,8,256]{2,1,0:T(8,128)S(1)}, f32[8,256]{1,0:T(8,128)}) custom-call(f32[123,8,128]{2,1,0:T(8,128)S(1)} %get-tuple-element.15.refs_0_, f32[93,8,128]{2,1,0:T(8,128)S(1)} %collective-permute-done.refs_1_, f32[93,8,128]{2,1,0:T(8,128)S(1)} %collective-permute-done.1.refs_2_, ...), custom_call_target="tpu_custom_call" | custom-call | tf_op jit(solution)/shard_map/pallas_call | solution.py:18
  37.2 1.4 %collective-permute-start.5 = (f32[12,8,256]{2,1,0:T(8,128)S(1)}, f32[12,8,256]{2,1,0:T(8,128)S(1)}, u32[]{:S(2)}, u32[]{:S(2)}) collective-permute-start(f32[12,8,256]{2,1,0:T(8,128)S(1)} %get-tuple-element.22), channel_id=1, source_target_pairs={{0,2},{2,0},{1,3},{3,1},{4,6},{6,4},{5,7},{7,5},{8,10},{10,8},{9,1... | collective-permute-start | bytes 294920 | tf_op jit(solution)/shard_map/ppermute | solution.py:451
  38.6 0.0 collective-permute-done.6.refs_3_
  38.6 0.0 collective-permute-done.7.refs_4_
  38.7 0.0 collective-permute-done.8.refs_5_
  38.7 3.2 %collective-permute-done.5.refs_1_ = f32[12,8,256]{2,1,0:T(8,128)S(1)} collective-permute-done((f32[12,8,256]{2,1,0:T(8,128)S(1)}, f32[12,8,256]{2,1,0:T(8,128)S(1)}, u32[]{:S(2)}, u32[]{:S(2)}) %collective-permute-start.5) | collective-permute-done | bytes 98336 | tf_op jit(solution)/shard_map/ppermute | solution.py:451
  41.8 1.2 %shard_map.81 = f32[12,8,512]{2,1,0:T(8,128)} custom-call(f32[12,8,256]{2,1,0:T(8,128)S(1)} %get-tuple-element.21.refs_0_, f32[12,8,256]{2,1,0:T(8,128)S(1)} %collective-permute-done.5.refs_1_, f32[13,16,128]{2,1,0:T(8,128)S(1)} %get-tuple-element.23.refs_2_, f32[13,16,128]{2,1,0:T(8,128)S(1)} %collective-permute-done.6.refs_3_, ...), custom_call_target="tpu_custom_call" | custom-call | tf_op jit(solution)/shard_map/pallas_call | solution.py:18
  (3 shorter events, 0.0 us)
Async XLA Ops:
  0.6 1.0 %copy-start = (f32[2,12,8,512]{3,2,1,0:T(8,128)S(1)}, f32[2,12,8,512]{3,2,1,0:T(8,128)}, u32[]{:S(2)}) copy-start(f32[2,12,8,512]{3,2,1,0:T(8,128)} %courant.1) | copy-start | bytes 1179652
  1.6 0.9 %copy-start.2 = (f32[1,12,8,512]{3,2,1,0:T(8,128)S(1)}, f32[1,12,8,512]{3,2,1,0:T(8,128)}, u32[]{:S(2)}) copy-start(f32[1,12,8,512]{3,2,1,0:T(8,128)} %param.6) | copy-start | bytes 589828
  2.6 0.9 %copy-start.3 = (f32[23,8,256]{2,1,0:T(8,128)S(1)}, f32[23,8,256]{2,1,0:T(8,128)}, u32[]{:S(2)}) copy-start(f32[23,8,256]{2,1,0:T(8,128)} %diffusion.1) | copy-start | bytes 565252
  3.5 14.1 %copy-start.4 = (s32[64,1]{0,1:T(1,128)S(1)}, s32[64,1]{0,1:T(1,128)}, u32[]{:S(2)}) copy-start(s32[64,1]{0,1:T(1,128)} %param.10) | copy-start | bytes 772
  3.9 14.6 %copy-start.1 = (f32[1,12,64,128]{3,2,1,0:T(8,128)S(1)}, f32[1,12,64,128]{3,2,1,0:T(8,128)}, u32[]{:S(2)}) copy-start(f32[1,12,64,128]{3,2,1,0:T(8,128)} %param.9) | copy-start | bytes 1179652
  3.9 9.5 %collective-permute-start.2 = (f32[80,8,128]{2,1,0:T(8,128)S(1)}, f32[80,8,128]{2,1,0:T(8,128)S(1)}, u32[]{:S(2)}, u32[]{:S(2)}) collective-permute-start(f32[80,8,128]{2,1,0:T(8,128)S(1)} %get-tuple-element.18), channel_id=1, source_target_pairs={{0,2},{2,0},{1,3},{3,1},{4,6},{6,4},{5,7},{7,5},{8,10},{10,8},{9,1... | collective-permute-start | bytes 983048 | tf_op jit(solution)/shard_map/ppermute | solution.py:431
  5.4 13.7 %collective-permute-start = (f32[93,8,128]{2,1,0:T(8,128)S(1)}, f32[93,8,128]{2,1,0:T(8,128)S(1)}, u32[]{:S(2)}, u32[]{:S(2)}) collective-permute-start(f32[93,8,128]{2,1,0:T(8,128)S(1)} %get-tuple-element.16), channel_id=1, source_target_pairs={{0,4},{4,0},{8,12},{12,8},{1,5},{5,1},{9,13},{13,9},{2,6},{6,2},{1... | collective-permute-start | bytes 1142792 | tf_op jit(solution)/shard_map/ppermute | solution.py:432
  7.0 15.6 %collective-permute-start.1 = (f32[93,8,128]{2,1,0:T(8,128)S(1)}, f32[93,8,128]{2,1,0:T(8,128)S(1)}, u32[]{:S(2)}, u32[]{:S(2)}) collective-permute-start(f32[93,8,128]{2,1,0:T(8,128)S(1)} %get-tuple-element.17), channel_id=1, source_target_pairs={{0,0},{4,8},{8,4},{12,12},{1,1},{5,9},{9,5},{13,13},{2,2},{6,10},{... | collective-permute-start | bytes 1142792 | tf_op jit(solution)/shard_map/ppermute | solution.py:433
  14.1 8.4 %collective-permute-start.3 = (f32[60,8,128]{2,1,0:T(8,128)}, f32[60,8,128]{2,1,0:T(8,128)S(1)}, u32[]{:S(2)}, u32[]{:S(2)}) collective-permute-start(f32[60,8,128]{2,1,0:T(8,128)} %get-tuple-element.19), channel_id=1, source_target_pairs={{0,4},{4,0},{8,12},{12,8},{1,5},{5,1},{9,13},{13,9},{2,6},{6,2},{1... | collective-permute-start | bytes 737288 | tf_op jit(solution)/shard_map/ppermute | solution.py:435
  15.7 15.3 %collective-permute-start.4 = (f32[60,8,128]{2,1,0:T(8,128)S(1)}, f32[60,8,128]{2,1,0:T(8,128)S(1)}, u32[]{:S(2)}, u32[]{:S(2)}) collective-permute-start(f32[60,8,128]{2,1,0:T(8,128)S(1)} %get-tuple-element.20), channel_id=1, source_target_pairs={{0,0},{4,8},{8,4},{12,12},{1,1},{5,9},{9,5},{13,13},{2,2},{6,10},{... | collective-permute-start | bytes 737288 | tf_op jit(solution)/shard_map/ppermute | solution.py:436
  19.0 19.6 %collective-permute-start.6 = (f32[13,16,128]{2,1,0:T(8,128)S(1)}, f32[13,16,128]{2,1,0:T(8,128)S(1)}, u32[]{:S(2)}, u32[]{:S(2)}) collective-permute-start(f32[13,16,128]{2,1,0:T(8,128)S(1)} %get-tuple-element.24), channel_id=1, source_target_pairs={{0,4},{4,0},{8,12},{12,8},{1,5},{5,1},{9,13},{13,9},{2,6},{6,2},{1... | collective-permute-start | bytes 319496 | tf_op jit(solution)/shard_map/ppermute | solution.py:410
  19.1 19.6 %collective-permute-start.7 = (f32[13,16,128]{2,1,0:T(8,128)S(1)}, f32[13,16,128]{2,1,0:T(8,128)S(1)}, u32[]{:S(2)}, u32[]{:S(2)}) collective-permute-start(f32[13,16,128]{2,1,0:T(8,128)S(1)} %get-tuple-element.25), channel_id=1, source_target_pairs={{0,8},{4,12},{8,0},{12,4},{1,9},{5,13},{9,1},{13,5},{2,10},{6,14},... | collective-permute-start | bytes 319496 | tf_op jit(solution)/shard_map/ppermute | solution.py:410
  22.6 16.1 %collective-permute-start.8 = (f32[13,16,128]{2,1,0:T(8,128)S(1)}, f32[13,16,128]{2,1,0:T(8,128)S(1)}, u32[]{:S(2)}, u32[]{:S(2)}) collective-permute-start(f32[13,16,128]{2,1,0:T(8,128)S(1)} %get-tuple-element.26), channel_id=1, source_target_pairs={{0,12},{4,8},{8,4},{12,0},{1,13},{5,9},{9,5},{13,1},{2,14},{6,10},... | collective-permute-start | bytes 319496 | tf_op jit(solution)/shard_map/ppermute | solution.py:410
  37.2 4.6 %collective-permute-start.5 = (f32[12,8,256]{2,1,0:T(8,128)S(1)}, f32[12,8,256]{2,1,0:T(8,128)S(1)}, u32[]{:S(2)}, u32[]{:S(2)}) collective-permute-start(f32[12,8,256]{2,1,0:T(8,128)S(1)} %get-tuple-element.22), channel_id=1, source_target_pairs={{0,2},{2,0},{1,3},{3,1},{4,6},{6,4},{5,7},{7,5},{8,10},{10,8},{9,1... | collective-permute-start | bytes 294920 | tf_op jit(solution)/shard_map/ppermute | solution.py:451
where the time goes:
time: 43.3 us; the launch traced here: 43 us
  waiting for transfers between devices  16.1 us (37%)
  starting transfers between devices  13.5 us (31%)
  Pallas kernels  9.05 us (21%)
  local copies, waits for them, and re-layouts  3.69 us (9%)
  between operations  0.71 us (2%)
    pallas_call x5, Pallas kernels, call(): pl.pallas_call(body, out_shape=[jax.ShapeDtypeStruct(shape, F32) for shap...  9.05 us
    ppermute x1, waiting for transfers between devices, local(): late_b = lax.ppermute(late_b, 'lat', swaps_b)  8.46 us
    ppermute x2, waiting for transfers between devices, local(): lax.ppermute(part, 'lev', pairs)  7.64 us
    ppermute x3, starting transfers between devices, route_tiles(): lax.ppermute(out, 'lat', pairs)  3.52 us
    ppermute x2, starting transfers between devices, local(): lax.ppermute(part, 'lev', pairs)  2.99 us
    unnamed x11, local copies, waits for them, and re-layouts  2.95 us
    ppermute x1, starting transfers between devices, local(): late_b = lax.ppermute(late_b, 'lat', swaps_b)  1.91 us
    ppermute x1, starting transfers between devices, local(): early_b = lax.ppermute(early_b, 'lat', swaps_b)  1.91 us
  transfers between devices with their start and end apart: 9, of which 3 were waited for; matrix products, arithmetic and copies ran while one was open for 2% of the time, Pallas kernels for 17%

commit v1 on v0

--- a/solution.py
+++ b/solution.py
@@ -13,14 +13,17 @@
 F32 = jnp.float32
 
 
-def call(body, out_shapes, *args, scratch=()):
+def call(body, out_shapes, *args, scratch=(), semaphores=0, inputs=pltpu.VMEM):
     spec = pl.BlockSpec(memory_space=pltpu.VMEM)
+    shapes = [pltpu.VMEM(shape, F32) for shape in scratch]
+    if semaphores:
+        shapes.append(pltpu.SemaphoreType.DMA((semaphores,)))
     return pl.pallas_call(
         body,
         out_shape=[jax.ShapeDtypeStruct(shape, F32) for shape in out_shapes],
-        in_specs=[spec] * len(args),
+        in_specs=[pl.BlockSpec(memory_space=inputs)] * len(args),
         out_specs=[spec] * len(out_shapes),
-        scratch_shapes=[pltpu.VMEM(shape, F32) for shape in scratch],
+        scratch_shapes=shapes,
         compiler_params=pltpu.CompilerParams(vmem_limit_bytes=32 * 1024 * 1024),
     )(*args)
 
@@ -189,7 +192,17 @@
         body(False)
 
 
-def pack_body(plan, field, courant, diffusion, own, swap_a, swap_b, *sent):
+def pack_body(plan, *refs):
+    sources, (own, swap_a, swap_b), sent = refs[:3], refs[3:6], refs[6:-4]
+    field, courant, diffusion, arrived = refs[-4:]
+    copies = [
+        pltpu.make_async_copy(source, target, arrived.at[i])
+        for i, (source, target) in enumerate(zip(sources, (field, courant, diffusion)))
+    ]
+    for copy in copies:
+        copy.start()
+    for copy in copies:
+        copy.wait()
     me = lax.axis_index("lev")
     tiles = field_tiles(plan, field, courant, me)
     for level in range(plan.levels - 1):
@@ -342,10 +355,9 @@
             outs[turn][level] = lam[base + level, :rows, : plan.chunk]
 
 
-def finish_body(plan, regions, *refs):
-    parts, buckets, out = refs[: plan.devices], refs[plan.devices : -1], refs[-1]
+def sum_body(plan, *refs):
+    buckets, out = refs[:-1], refs[-1]
     count, rows, width = plan.count, plan.rows, plan.width
-    me = lax.axis_index("lev")
     cells = jnp.concatenate([bucket[count] for bucket in buckets], axis=0)
     tile = cells.shape[1]
     blocks = width // tile
@@ -358,17 +370,20 @@
         added = lax.dot_general(
             hits, values, (((1,), (0,)), ((), ())), precision=lax.Precision.HIGHEST, preferred_element_type=F32
         )
-        chunks = []
+        for block in range(blocks):
+            out[level, :, block * tile : (block + 1) * tile] = added[block * rows : (block + 1) * rows]
+
+
+def finish_body(plan, *refs):
+    parts, added, out = refs[: plan.devices], refs[plan.devices], refs[-1]
+    me = lax.axis_index("lev")
+    for level in range(plan.count):
         for q in range(plan.devices):
             piece = parts[0][level]
             for turn in range(1, plan.devices):
                 piece = jnp.where(source_of(me, turn, plan.devices) == q, parts[turn][level], piece)
-            chunks.append(piece)
-        v = jnp.concatenate(chunks, axis=1)
-        for block in range(blocks):
-            out[level, :, block * tile : (block + 1) * tile] = (
-                v[:, block * tile : (block + 1) * tile] + added[block * rows : (block + 1) * rows]
-            )
+            at = slice(q * plan.chunk, (q + 1) * plan.chunk)
+            out[level, :, at] = piece + added[level, :, at]
 
 
 def bucket_body(regions, values, region_column, region_row, cell_column, *outs):
@@ -396,10 +411,10 @@
             outs[s][level] = got[s * capacity : (s + 1) * capacity]
 
 
-def route_tiles(tile_values, tile_region, tile_cell):
+def bucket_tiles(tile_values, tile_region, tile_cell):
     regions = lax.axis_size("lat")
     count, tiles, tile = tile_values.shape
-    outs = call(
+    return call(
         functools.partial(bucket_body, regions),
         [(count + 1, tiles // 4, tile)] * regions,
         tile_values,
@@ -407,8 +422,6 @@
         tile_region.reshape(1, tiles),
         tile_cell.reshape(tiles, 1),
     )
-    return [outs[0]] + [lax.ppermute(out, "lat", pairs) for out, pairs in zip(outs[1:], rounds(regions))]
-
 
 def local(adjoint_in, courant, diffusion, tile_values, tile_region, tile_cell):
     field = adjoint_in[0]
@@ -427,6 +440,9 @@
         field,
         courant,
         diffusion,
+        scratch=[field.shape, courant.shape, diffusion.shape],
+        semaphores=3,
+        inputs=pltpu.HBM,
     )
     got = [lax.ppermute(part, "lev", pairs) for part, pairs in zip(sent, rounds(devices))]
     early_a = lax.ppermute(early_a, "lat", swaps_a)
@@ -434,6 +450,9 @@
     late_a, late_b = call(functools.partial(forward_rows_body, plan), [(late,) + tile] * 2, *got)
     late_a = lax.ppermute(late_a, "lat", swaps_a)
     late_b = lax.ppermute(late_b, "lat", swaps_b)
+    buckets = bucket_tiles(tile_values[0], tile_region, tile_cell)
+    late_a, late_b, *buckets = lax.optimization_barrier((late_a, late_b, *buckets))
+    buckets = [buckets[0]] + [lax.ppermute(part, "lat", pairs) for part, pairs in zip(buckets[1:], rounds(bands))]
 
     whole = (plan.levels, 3 * rows, plan.window)
     lists = (2, plan.own_size + (devices - 1) * plan.sent_size) + tile
@@ -449,8 +468,8 @@
         scratch=[lists] + [whole] * 8,
     )
     parts = [outs[0]] + [lax.ppermute(part, "lev", pairs) for part, pairs in zip(outs[1:], rounds(devices))]
-    buckets = route_tiles(tile_values[0], tile_region, tile_cell)
-    (out,) = call(functools.partial(finish_body, plan, bands), [(count, rows, width)], *parts, *buckets)
+    (added,) = call(functools.partial(sum_body, plan), [(count, rows, width)], *buckets)
+    (out,) = call(functools.partial(finish_body, plan), [(count, rows, width)], *parts, added)
     return out[None], flux[None]
 
 

time: 43.3 us -> 42.1 us (0.972)
  the two profiles are of different devices: /device:TPU:16 before, /device:TPU:0 now
where the time goes in v1:
time: 42.1 us; the launch traced here: 41.9 us
  starting transfers between devices  16.2 us (38%)
  waiting for transfers between devices  11.6 us (28%)
  Pallas kernels  9.74 us (23%)
  local copies, waits for them, and re-layouts  3.69 us (9%)
  between operations  0.7 us (2%)
    pallas_call x6, Pallas kernels, call(): pl.pallas_call(body, out_shape=[jax.ShapeDtypeStruct(shape, F32) for shap...  9.74 us
    ppermute x2, waiting for transfers between devices, local(): lax.ppermute(part, 'lev', pairs)  8.11 us
    ppermute x3, starting transfers between devices, local(): lax.ppermute(part, 'lat', pairs)  7.01 us
    ppermute x2, starting transfers between devices, local(): lax.ppermute(part, 'lev', pairs)  4.44 us
    ppermute x1, waiting for transfers between devices, local(): late_a = lax.ppermute(late_a, 'lat', swaps_a)  3.44 us
    unnamed x11, local copies, waits for them, and re-layouts  2.95 us
    ppermute x1, starting transfers between devices, local(): late_a = lax.ppermute(late_a, 'lat', swaps_a)  1.83 us
    ppermute x1, starting transfers between devices, local(): early_a = lax.ppermute(early_a, 'lat', swaps_a)  1.58 us
  transfers between devices with their start and end apart: 9, of which 3 were waited for; matrix products, arithmetic and copies ran while one was open for 2% of the time, Pallas kernels for 19%

profile of v1, /device:TPU:0, one launch (start us, length us, event | category | flops | bytes accessed | tf_op | source)
XLA Modules:
  0.0 41.9 jit_solution(18015360032878243113)
XLA Ops:
  0.6 0.0 copy-start
  0.6 1.0 %copy-done = f32[2,12,8,512]{3,2,1,0:T(8,128)S(1)} copy-done((f32[2,12,8,512]{3,2,1,0:T(8,128)S(1)}, f32[2,12,8,512]{3,2,1,0:T(8,128)}, u32[]{:S(2)}) %copy-start) | copy-done | bytes 393240
  1.6 0.9 %copy-done.2 = f32[1,12,8,512]{3,2,1,0:T(8,128)S(1)} copy-done((f32[1,12,8,512]{3,2,1,0:T(8,128)S(1)}, f32[1,12,8,512]{3,2,1,0:T(8,128)}, u32[]{:S(2)}) %copy-start.2) | copy-done | bytes 196632
  2.6 0.9 %copy-done.3 = f32[23,8,256]{2,1,0:T(8,128)S(1)} copy-done((f32[23,8,256]{2,1,0:T(8,128)S(1)}, f32[23,8,256]{2,1,0:T(8,128)}, u32[]{:S(2)}) %copy-start.3) | copy-done | bytes 188440
  3.5 1.0 %shard_map.77 = (f32[123,8,128]{2,1,0:T(8,128)S(1)}, f32[93,8,128]{2,1,0:T(8,128)S(1)}, f32[93,8,128]{2,1,0:T(8,128)S(1)}, f32[80,8,128]{2,1,0:T(8,128)S(1)}) custom-call(f32[12,8,512]{2,1,0:T(8,128)S(1)} %bitcast.7, f32[2,12,8,512]{3,2,1,0:T(8,128)S(1)} %copy-done, f32[23,8,256]{2,1,0:T(8,128)S(1)} %copy-done.3), custom_call_target="tpu_custom_call" | custom-call | tf_op jit(solution)/shard_map/pallas_call | solution.py:21
  4.5 0.0 copy-start.1
  4.5 3.0 %collective-permute-start.2 = (f32[80,8,128]{2,1,0:T(8,128)S(1)}, f32[80,8,128]{2,1,0:T(8,128)S(1)}, u32[]{:S(2)}, u32[]{:S(2)}) collective-permute-start(f32[80,8,128]{2,1,0:T(8,128)S(1)} %get-tuple-element.24), channel_id=1, source_target_pairs={{0,2},{2,0},{1,3},{3,1},{4,6},{6,4},{5,7},{7,5},{8,10},{10,8},{9,1... | collective-permute-start | bytes 983048 | tf_op jit(solution)/shard_map/ppermute | solution.py:447
  7.5 1.6 %collective-permute-start = (f32[93,8,128]{2,1,0:T(8,128)S(1)}, f32[93,8,128]{2,1,0:T(8,128)S(1)}, u32[]{:S(2)}, u32[]{:S(2)}) collective-permute-start(f32[93,8,128]{2,1,0:T(8,128)S(1)} %get-tuple-element.22), channel_id=1, source_target_pairs={{0,4},{4,0},{8,12},{12,8},{1,5},{5,1},{9,13},{13,9},{2,6},{6,2},{1... | collective-permute-start | bytes 1142792 | tf_op jit(solution)/shard_map/ppermute | solution.py:448
  9.1 0.7 %collective-permute-start.1 = (f32[93,8,128]{2,1,0:T(8,128)S(1)}, f32[93,8,128]{2,1,0:T(8,128)S(1)}, u32[]{:S(2)}, u32[]{:S(2)}) collective-permute-start(f32[93,8,128]{2,1,0:T(8,128)S(1)} %get-tuple-element.23), channel_id=1, source_target_pairs={{0,0},{4,8},{8,4},{12,12},{1,1},{5,9},{9,5},{13,13},{2,2},{6,10},{... | collective-permute-start | bytes 1142792 | tf_op jit(solution)/shard_map/ppermute | solution.py:449
  9.8 5.4 %collective-permute-done.2.refs_0_.refs_5_ = f32[80,8,128]{2,1,0:T(8,128)S(1)} collective-permute-done((f32[80,8,128]{2,1,0:T(8,128)S(1)}, f32[80,8,128]{2,1,0:T(8,128)S(1)}, u32[]{:S(2)}, u32[]{:S(2)}) %collective-permute-start.2) | collective-permute-done | bytes 327712 | tf_op jit(solution)/shard_map/ppermute | solution.py:447
  15.2 0.7 %shard_map.78 = (f32[60,8,128]{2,1,0:T(8,128)}, f32[60,8,128]{2,1,0:T(8,128)S(1)}) custom-call(f32[80,8,128]{2,1,0:T(8,128)S(1)} %collective-permute-done.2.refs_0_.refs_5_), custom_call_target="tpu_custom_call" | custom-call | tf_op jit(solution)/shard_map/pallas_call | solution.py:21
  16.0 1.8 %collective-permute-start.3 = (f32[60,8,128]{2,1,0:T(8,128)}, f32[60,8,128]{2,1,0:T(8,128)S(1)}, u32[]{:S(2)}, u32[]{:S(2)}) collective-permute-start(f32[60,8,128]{2,1,0:T(8,128)} %get-tuple-element.25), channel_id=1, source_target_pairs={{0,4},{4,0},{8,12},{12,8},{1,5},{5,1},{9,13},{13,9},{2,6},{6,2},{1... | collective-permute-start | bytes 737288 | tf_op jit(solution)/shard_map/ppermute | solution.py:451
  17.8 0.7 %collective-permute-start.4 = (f32[60,8,128]{2,1,0:T(8,128)S(1)}, f32[60,8,128]{2,1,0:T(8,128)S(1)}, u32[]{:S(2)}, u32[]{:S(2)}) collective-permute-start(f32[60,8,128]{2,1,0:T(8,128)S(1)} %get-tuple-element.26), channel_id=1, source_target_pairs={{0,0},{4,8},{8,4},{12,12},{1,1},{5,9},{9,5},{13,13},{2,2},{6,10},{... | collective-permute-start | bytes 737288 | tf_op jit(solution)/shard_map/ppermute | solution.py:452
  18.5 0.0 copy-done.4
  18.5 0.1 copy.8.region_column
  18.6 0.7 %copy.9.cell_column = s32[64,1]{1,0:T(8,128)S(1)} copy(s32[64,1]{0,1:T(1,128)} %bitcast.10) | data formatting | bytes 512 | tf_op jit(solution)/shard_map/reshape | solution.py:423
  19.3 0.6 %shard_map.79 = (f32[13,16,128]{2,1,0:T(8,128)S(1)}, f32[13,16,128]{2,1,0:T(8,128)S(1)}, f32[13,16,128]{2,1,0:T(8,128)S(1)}, f32[13,16,128]{2,1,0:T(8,128)S(1)}) custom-call(f32[12,64,128]{2,1,0:T(8,128)S(1)} %bitcast.6, s32[64,1]{1,0:T(8,128)S(1)} %copy.8.region_column, s32[1,64]{1,0:T(1,128)S(1)} %bitcast.8, s32[64,1]{1,0:T(8,128)S(1)} %copy.9.cell_column), custom_call_target="tpu_custom_call" | custom-call | tf_op jit(solution)/shard_map/pallas_call | solution.py:21
  19.9 3.4 %collective-permute-done.3.refs_3_ = f32[60,8,128]{2,1,0:T(8,128)S(1)} collective-permute-done((f32[60,8,128]{2,1,0:T(8,128)}, f32[60,8,128]{2,1,0:T(8,128)S(1)}, u32[]{:S(2)}, u32[]{:S(2)}) %collective-permute-start.3) | collective-permute-done | bytes 245792 | tf_op jit(solution)/shard_map/ppermute | solution.py:451
  23.3 0.0 collective-permute-done.4.refs_4_
  23.3 4.4 %collective-permute-start.6 = (f32[13,16,128]{2,1,0:T(8,128)S(1)}, f32[13,16,128]{2,1,0:T(8,128)S(1)}, u32[]{:S(2)}, u32[]{:S(2)}) collective-permute-start(f32[13,16,128]{2,1,0:T(8,128)S(1)} %get-tuple-element.36), channel_id=1, source_target_pairs={{0,4},{4,0},{8,12},{12,8},{1,5},{5,1},{9,13},{13,9},{2,6},{6,2},{1... | collective-permute-start | bytes 319496 | tf_op jit(solution)/shard_map/ppermute | solution.py:455
  27.7 1.2 %collective-permute-start.7 = (f32[13,16,128]{2,1,0:T(8,128)S(1)}, f32[13,16,128]{2,1,0:T(8,128)S(1)}, u32[]{:S(2)}, u32[]{:S(2)}) collective-permute-start(f32[13,16,128]{2,1,0:T(8,128)S(1)} %get-tuple-element.37), channel_id=1, source_target_pairs={{0,8},{4,12},{8,0},{12,4},{1,9},{5,13},{9,1},{13,5},{2,10},{6,14},... | collective-permute-start | bytes 319496 | tf_op jit(solution)/shard_map/ppermute | solution.py:455
  28.9 1.5 %collective-permute-start.8 = (f32[13,16,128]{2,1,0:T(8,128)S(1)}, f32[13,16,128]{2,1,0:T(8,128)S(1)}, u32[]{:S(2)}, u32[]{:S(2)}) collective-permute-start(f32[13,16,128]{2,1,0:T(8,128)S(1)} %get-tuple-element.38), channel_id=1, source_target_pairs={{0,12},{4,8},{8,4},{12,0},{1,13},{5,9},{9,5},{13,1},{2,14},{6,10},... | collective-permute-start | bytes 319496 | tf_op jit(solution)/shard_map/ppermute | solution.py:455
  30.3 0.0 collective-permute-done.refs_1_
  30.3 0.0 collective-permute-done.1.refs_2_
  30.3 6.2 %shard_map.80 = (f32[12,8,256]{2,1,0:T(8,128)S(1)}, f32[12,8,256]{2,1,0:T(8,128)S(1)}, f32[8,256]{1,0:T(8,128)}) custom-call(f32[123,8,128]{2,1,0:T(8,128)S(1)} %get-tuple-element.21.refs_0_, f32[93,8,128]{2,1,0:T(8,128)S(1)} %collective-permute-done.refs_1_, f32[93,8,128]{2,1,0:T(8,128)S(1)} %collective-permute-done.1.refs_2_, ...), custom_call_target="tpu_custom_call" | custom-call | tf_op jit(solution)/shard_map/pallas_call | solution.py:21
  36.5 1.4 %collective-permute-start.5 = (f32[12,8,256]{2,1,0:T(8,128)S(1)}, f32[12,8,256]{2,1,0:T(8,128)S(1)}, u32[]{:S(2)}, u32[]{:S(2)}) collective-permute-start(f32[12,8,256]{2,1,0:T(8,128)S(1)} %get-tuple-element.34), channel_id=1, source_target_pairs={{0,2},{2,0},{1,3},{3,1},{4,6},{6,4},{5,7},{7,5},{8,10},{10,8},{9,1... | collective-permute-start | bytes 294920 | tf_op jit(solution)/shard_map/ppermute | solution.py:470
  38.0 0.0 collective-permute-done.6.refs_1_
  38.0 0.0 collective-permute-done.7.refs_2_
  38.0 0.0 collective-permute-done.8.refs_3_
  38.0 0.5 %shard_map.81.refs_2_ = f32[12,8,512]{2,1,0:T(8,128)S(1)} custom-call(f32[13,16,128]{2,1,0:T(8,128)S(1)} %get-tuple-element.35.refs_0_, f32[13,16,128]{2,1,0:T(8,128)S(1)} %collective-permute-done.6.refs_1_, f32[13,16,128]{2,1,0:T(8,128)S(1)} %collective-permute-done.7.refs_2_, f32[13,16,128]{2,1,0:T(8,128)S(1)} %collective-permute-done.8.refs_3_), custom_call_target="tpu_custom_call" | custom-call | tf_op jit(solution)/shard_map/pallas_call | solution.py:21
  38.5 2.7 %collective-permute-done.5.refs_1_ = f32[12,8,256]{2,1,0:T(8,128)S(1)} collective-permute-done((f32[12,8,256]{2,1,0:T(8,128)S(1)}, f32[12,8,256]{2,1,0:T(8,128)S(1)}, u32[]{:S(2)}, u32[]{:S(2)}) %collective-permute-start.5) | collective-permute-done | bytes 98336 | tf_op jit(solution)/shard_map/ppermute | solution.py:470
  41.2 0.7 %shard_map.82 = f32[12,8,512]{2,1,0:T(8,128)} custom-call(f32[12,8,256]{2,1,0:T(8,128)S(1)} %get-tuple-element.33.refs_0_, f32[12,8,256]{2,1,0:T(8,128)S(1)} %collective-permute-done.5.refs_1_, f32[12,8,512]{2,1,0:T(8,128)S(1)} %shard_map.81.refs_2_), custom_call_target="tpu_custom_call" | custom-call | tf_op jit(solution)/shard_map/pallas_call | solution.py:21
  (4 shorter events, 0.0 us)
Async XLA Ops:
  0.6 1.0 %copy-start = (f32[2,12,8,512]{3,2,1,0:T(8,128)S(1)}, f32[2,12,8,512]{3,2,1,0:T(8,128)}, u32[]{:S(2)}) copy-start(f32[2,12,8,512]{3,2,1,0:T(8,128)} %refs_1_.1) | copy-start | bytes 1179652
  1.6 0.9 %copy-start.2 = (f32[1,12,8,512]{3,2,1,0:T(8,128)S(1)}, f32[1,12,8,512]{3,2,1,0:T(8,128)}, u32[]{:S(2)}) copy-start(f32[1,12,8,512]{3,2,1,0:T(8,128)} %param.6) | copy-start | bytes 589828
  2.6 0.9 %copy-start.3 = (f32[23,8,256]{2,1,0:T(8,128)S(1)}, f32[23,8,256]{2,1,0:T(8,128)}, u32[]{:S(2)}) copy-start(f32[23,8,256]{2,1,0:T(8,128)} %refs_2_.1) | copy-start | bytes 565252
  3.5 15.0 %copy-start.4 = (s32[64,1]{0,1:T(1,128)S(1)}, s32[64,1]{0,1:T(1,128)}, u32[]{:S(2)}) copy-start(s32[64,1]{0,1:T(1,128)} %param.10) | copy-start | bytes 772
  4.5 14.8 %copy-start.1 = (f32[1,12,64,128]{3,2,1,0:T(8,128)S(1)}, f32[1,12,64,128]{3,2,1,0:T(8,128)}, u32[]{:S(2)}) copy-start(f32[1,12,64,128]{3,2,1,0:T(8,128)} %param.9) | copy-start | bytes 1179652
  4.5 10.7 %collective-permute-start.2 = (f32[80,8,128]{2,1,0:T(8,128)S(1)}, f32[80,8,128]{2,1,0:T(8,128)S(1)}, u32[]{:S(2)}, u32[]{:S(2)}) collective-permute-start(f32[80,8,128]{2,1,0:T(8,128)S(1)} %get-tuple-element.24), channel_id=1, source_target_pairs={{0,2},{2,0},{1,3},{3,1},{4,6},{6,4},{5,7},{7,5},{8,10},{10,8},{9,1... | collective-permute-start | bytes 983048 | tf_op jit(solution)/shard_map/ppermute | solution.py:447
  7.5 22.8 %collective-permute-start = (f32[93,8,128]{2,1,0:T(8,128)S(1)}, f32[93,8,128]{2,1,0:T(8,128)S(1)}, u32[]{:S(2)}, u32[]{:S(2)}) collective-permute-start(f32[93,8,128]{2,1,0:T(8,128)S(1)} %get-tuple-element.22), channel_id=1, source_target_pairs={{0,4},{4,0},{8,12},{12,8},{1,5},{5,1},{9,13},{13,9},{2,6},{6,2},{1... | collective-permute-start | bytes 1142792 | tf_op jit(solution)/shard_map/ppermute | solution.py:448
  9.1 21.2 %collective-permute-start.1 = (f32[93,8,128]{2,1,0:T(8,128)S(1)}, f32[93,8,128]{2,1,0:T(8,128)S(1)}, u32[]{:S(2)}, u32[]{:S(2)}) collective-permute-start(f32[93,8,128]{2,1,0:T(8,128)S(1)} %get-tuple-element.23), channel_id=1, source_target_pairs={{0,0},{4,8},{8,4},{12,12},{1,1},{5,9},{9,5},{13,13},{2,2},{6,10},{... | collective-permute-start | bytes 1142792 | tf_op jit(solution)/shard_map/ppermute | solution.py:449
  16.0 7.4 %collective-permute-start.3 = (f32[60,8,128]{2,1,0:T(8,128)}, f32[60,8,128]{2,1,0:T(8,128)S(1)}, u32[]{:S(2)}, u32[]{:S(2)}) collective-permute-start(f32[60,8,128]{2,1,0:T(8,128)} %get-tuple-element.25), channel_id=1, source_target_pairs={{0,4},{4,0},{8,12},{12,8},{1,5},{5,1},{9,13},{13,9},{2,6},{6,2},{1... | collective-permute-start | bytes 737288 | tf_op jit(solution)/shard_map/ppermute | solution.py:451
  17.8 5.5 %collective-permute-start.4 = (f32[60,8,128]{2,1,0:T(8,128)S(1)}, f32[60,8,128]{2,1,0:T(8,128)S(1)}, u32[]{:S(2)}, u32[]{:S(2)}) collective-permute-start(f32[60,8,128]{2,1,0:T(8,128)S(1)} %get-tuple-element.26), channel_id=1, source_target_pairs={{0,0},{4,8},{8,4},{12,12},{1,1},{5,9},{9,5},{13,13},{2,2},{6,10},{... | collective-permute-start | bytes 737288 | tf_op jit(solution)/shard_map/ppermute | solution.py:452
  23.3 14.6 %collective-permute-start.6 = (f32[13,16,128]{2,1,0:T(8,128)S(1)}, f32[13,16,128]{2,1,0:T(8,128)S(1)}, u32[]{:S(2)}, u32[]{:S(2)}) collective-permute-start(f32[13,16,128]{2,1,0:T(8,128)S(1)} %get-tuple-element.36), channel_id=1, source_target_pairs={{0,4},{4,0},{8,12},{12,8},{1,5},{5,1},{9,13},{13,9},{2,6},{6,2},{1... | collective-permute-start | bytes 319496 | tf_op jit(solution)/shard_map/ppermute | solution.py:455
  27.7 10.3 %collective-permute-start.7 = (f32[13,16,128]{2,1,0:T(8,128)S(1)}, f32[13,16,128]{2,1,0:T(8,128)S(1)}, u32[]{:S(2)}, u32[]{:S(2)}) collective-permute-start(f32[13,16,128]{2,1,0:T(8,128)S(1)} %get-tuple-element.37), channel_id=1, source_target_pairs={{0,8},{4,12},{8,0},{12,4},{1,9},{5,13},{9,1},{13,5},{2,10},{6,14},... | collective-permute-start | bytes 319496 | tf_op jit(solution)/shard_map/ppermute | solution.py:455
  28.9 9.1 %collective-permute-start.8 = (f32[13,16,128]{2,1,0:T(8,128)S(1)}, f32[13,16,128]{2,1,0:T(8,128)S(1)}, u32[]{:S(2)}, u32[]{:S(2)}) collective-permute-start(f32[13,16,128]{2,1,0:T(8,128)S(1)} %get-tuple-element.38), channel_id=1, source_target_pairs={{0,12},{4,8},{8,4},{12,0},{1,13},{5,9},{9,5},{13,1},{2,14},{6,10},... | collective-permute-start | bytes 319496 | tf_op jit(solution)/shard_map/ppermute | solution.py:455
  36.5 4.6 %collective-permute-start.5 = (f32[12,8,256]{2,1,0:T(8,128)S(1)}, f32[12,8,256]{2,1,0:T(8,128)S(1)}, u32[]{:S(2)}, u32[]{:S(2)}) collective-permute-start(f32[12,8,256]{2,1,0:T(8,128)S(1)} %get-tuple-element.34), channel_id=1, source_target_pairs={{0,2},{2,0},{1,3},{3,1},{4,6},{6,4},{5,7},{7,5},{8,10},{10,8},{9,1... | collective-permute-start | bytes 294920 | tf_op jit(solution)/shard_map/ppermute | solution.py:470

commit v2 on v1

--- a/solution.py
+++ b/solution.py
@@ -15,6 +15,8 @@
 
 def call(body, out_shapes, *args, scratch=(), semaphores=0, inputs=pltpu.VMEM):
     spec = pl.BlockSpec(memory_space=pltpu.VMEM)
+    if inputs == pltpu.HBM:
+        args = [pltpu.with_memory_space_constraint(arg, pltpu.HBM) for arg in args]
     shapes = [pltpu.VMEM(shape, F32) for shape in scratch]
     if semaphores:
         shapes.append(pltpu.SemaphoreType.DMA((semaphores,)))
@@ -45,11 +47,8 @@
 
 
 def band_swaps(bands, first):
-    swaps = []
-    for b in range(bands):
-        partner = b + 1 if (b - first) % 2 == 0 else b - 1
-        swaps.append((b, partner if 0 <= partner < bands else b))
-    return swaps
+    pairs = [(b, b + 1) for b in range(first, bands - 1, 2)]
+    return pairs + [(b, a) for a, b in pairs]
 
 
 class Plan:
@@ -445,11 +444,11 @@
         inputs=pltpu.HBM,
     )
     got = [lax.ppermute(part, "lev", pairs) for part, pairs in zip(sent, rounds(devices))]
+    early_b = lax.ppermute(early_b, "lat", swaps_b)
     early_a = lax.ppermute(early_a, "lat", swaps_a)
-    early_b = lax.ppermute(early_b, "lat", swaps_b)
     late_a, late_b = call(functools.partial(forward_rows_body, plan), [(late,) + tile] * 2, *got)
+    late_b = lax.ppermute(late_b, "lat", swaps_b)
     late_a = lax.ppermute(late_a, "lat", swaps_a)
-    late_b = lax.ppermute(late_b, "lat", swaps_b)
     buckets = bucket_tiles(tile_values[0], tile_region, tile_cell)
     late_a, late_b, *buckets = lax.optimization_barrier((late_a, late_b, *buckets))
     buckets = [buckets[0]] + [lax.ppermute(part, "lat", pairs) for part, pairs in zip(buckets[1:], rounds(bands))]

time: 42.1 us -> 39.7 us (0.943)
  local copies, waits for them, and re-layouts: 3.69 us -> 0.85 us
  Pallas kernels: 9.74 us -> 10.2 us
    unnamed x11 -> x5, local copies, waits for them, and re-layouts: 2.95 us -> 0.11 us
    pallas_call x6, Pallas kernels: 9.74 us -> 10.2 us  [call(): pl.pallas_call(body, out_shape=[jax.ShapeDtypeStruct(shape, F32) for shap...]
  transfers between devices with their start and end apart: 9 -> 9, of which waited for: 3 -> 3; matrix products, arithmetic and copies ran while one was open for 2% -> 2% of each run, Pallas kernels for 19% -> 20%
where the time goes in v2:
time: 39.7 us; the launch traced here: 39.5 us
  starting transfers between devices  16.2 us (41%)
  waiting for transfers between devices  11.6 us (29%)
  Pallas kernels  10.2 us (26%)
  local copies, waits for them, and re-layouts  0.85 us (2%)
  between operations  0.69 us (2%)
    pallas_call x6, Pallas kernels, call(): pl.pallas_call(body, out_shape=[jax.ShapeDtypeStruct(shape, F32) for shap...  10.2 us
    ppermute x2, waiting for transfers between devices, local(): lax.ppermute(part, 'lev', pairs)  8.11 us
    ppermute x3, starting transfers between devices, local(): lax.ppermute(part, 'lat', pairs)  7.01 us
    ppermute x2, starting transfers between devices, local(): lax.ppermute(part, 'lev', pairs)  4.43 us
    ppermute x1, waiting for transfers between devices, local(): late_a = lax.ppermute(late_a, 'lat', swaps_a)  3.43 us
    ppermute x1, starting transfers between devices, local(): late_a = lax.ppermute(late_a, 'lat', swaps_a)  1.83 us
    ppermute x1, starting transfers between devices, local(): early_a = lax.ppermute(early_a, 'lat', swaps_a)  1.58 us
  transfers between devices with their start and end apart: 9, of which 3 were waited for; matrix products, arithmetic and copies ran while one was open for 2% of the time, Pallas kernels for 20%

profile of v2, /device:TPU:0, one launch (start us, length us, event | category | flops | bytes accessed | tf_op | source)
XLA Modules:
  0.0 39.5 jit_solution(1334447920976660624)
XLA Ops:
  0.6 0.0 copy-start.1
  0.6 1.5 %shard_map.77 = (f32[123,8,128]{2,1,0:T(8,128)S(1)}, f32[93,8,128]{2,1,0:T(8,128)S(1)}, f32[93,8,128]{2,1,0:T(8,128)S(1)}, f32[80,8,128]{2,1,0:T(8,128)S(1)}) custom-call(f32[12,8,512]{2,1,0:T(8,128)} %bitcast.8, f32[2,12,8,512]{3,2,1,0:T(8,128)} %refs_1_.1, f32[23,8,256]{2,1,0:T(8,128)} %refs_2_.1), custom_call_target="tpu_custom_call" | custom-call | tf_op jit(solution)/shard_map/pallas_call | solution.py:23
  2.2 0.0 copy-start
  2.2 3.0 %collective-permute-start.2 = (f32[80,8,128]{2,1,0:T(8,128)S(1)}, f32[80,8,128]{2,1,0:T(8,128)S(1)}, u32[]{:S(2)}, u32[]{:S(2)}) collective-permute-start(f32[80,8,128]{2,1,0:T(8,128)S(1)} %get-tuple-element.24), channel_id=1, source_target_pairs={{0,2},{2,0},{1,3},{3,1},{4,6},{6,4},{5,7},{7,5},{8,10},{10,8},{9,1... | collective-permute-start | bytes 983048 | tf_op jit(solution)/shard_map/ppermute | solution.py:446
  5.2 1.6 %collective-permute-start = (f32[93,8,128]{2,1,0:T(8,128)S(1)}, f32[93,8,128]{2,1,0:T(8,128)S(1)}, u32[]{:S(2)}, u32[]{:S(2)}) collective-permute-start(f32[93,8,128]{2,1,0:T(8,128)S(1)} %get-tuple-element.22), channel_id=1, source_target_pairs={{0,4},{8,12},{4,0},{12,8},{1,5},{9,13},{5,1},{13,9},{2,6},{10,14},... | collective-permute-start | bytes 1142792 | tf_op jit(solution)/shard_map/ppermute | solution.py:448
  6.8 0.7 %collective-permute-start.1 = (f32[93,8,128]{2,1,0:T(8,128)S(1)}, f32[93,8,128]{2,1,0:T(8,128)S(1)}, u32[]{:S(2)}, u32[]{:S(2)}) collective-permute-start(f32[93,8,128]{2,1,0:T(8,128)S(1)} %get-tuple-element.23), channel_id=1, source_target_pairs={{4,8},{8,4},{5,9},{9,5},{6,10},{10,6},{7,11},{11,7},{20,24},{24,20... | collective-permute-start | bytes 1142792 | tf_op jit(solution)/shard_map/ppermute | solution.py:447
  7.4 5.4 %collective-permute-done.2.refs_0_.refs_5_ = f32[80,8,128]{2,1,0:T(8,128)S(1)} collective-permute-done((f32[80,8,128]{2,1,0:T(8,128)S(1)}, f32[80,8,128]{2,1,0:T(8,128)S(1)}, u32[]{:S(2)}, u32[]{:S(2)}) %collective-permute-start.2) | collective-permute-done | bytes 327712 | tf_op jit(solution)/shard_map/ppermute | solution.py:446
  12.9 0.7 %shard_map.78 = (f32[60,8,128]{2,1,0:T(8,128)}, f32[60,8,128]{2,1,0:T(8,128)S(1)}) custom-call(f32[80,8,128]{2,1,0:T(8,128)S(1)} %collective-permute-done.2.refs_0_.refs_5_), custom_call_target="tpu_custom_call" | custom-call | tf_op jit(solution)/shard_map/pallas_call | solution.py:23
  13.6 1.8 %collective-permute-start.3 = (f32[60,8,128]{2,1,0:T(8,128)}, f32[60,8,128]{2,1,0:T(8,128)S(1)}, u32[]{:S(2)}, u32[]{:S(2)}) collective-permute-start(f32[60,8,128]{2,1,0:T(8,128)} %get-tuple-element.25), channel_id=1, source_target_pairs={{0,4},{8,12},{4,0},{12,8},{1,5},{9,13},{5,1},{13,9},{2,6},{10,14},... | collective-permute-start | bytes 737288 | tf_op jit(solution)/shard_map/ppermute | solution.py:451
  15.4 0.7 %collective-permute-start.4 = (f32[60,8,128]{2,1,0:T(8,128)S(1)}, f32[60,8,128]{2,1,0:T(8,128)S(1)}, u32[]{:S(2)}, u32[]{:S(2)}) collective-permute-start(f32[60,8,128]{2,1,0:T(8,128)S(1)} %get-tuple-element.26), channel_id=1, source_target_pairs={{4,8},{8,4},{5,9},{9,5},{6,10},{10,6},{7,11},{11,7},{20,24},{24,20... | collective-permute-start | bytes 737288 | tf_op jit(solution)/shard_map/ppermute | solution.py:450
  16.1 0.0 copy-done.1
  16.1 0.1 copy.8.region_column
  16.2 0.7 %copy.9.cell_column = s32[64,1]{1,0:T(8,128)S(1)} copy(s32[64,1]{0,1:T(1,128)} %bitcast.10) | data formatting | bytes 512 | tf_op jit(solution)/shard_map/reshape | solution.py:422
  17.0 0.0 copy-done
  17.0 0.6 %shard_map.79 = (f32[13,16,128]{2,1,0:T(8,128)S(1)}, f32[13,16,128]{2,1,0:T(8,128)S(1)}, f32[13,16,128]{2,1,0:T(8,128)S(1)}, f32[13,16,128]{2,1,0:T(8,128)S(1)}) custom-call(f32[12,64,128]{2,1,0:T(8,128)S(1)} %bitcast.6, s32[64,1]{1,0:T(8,128)S(1)} %copy.8.region_column, s32[1,64]{1,0:T(1,128)S(1)} %bitcast.7, s32[64,1]{1,0:T(8,128)S(1)} %copy.9.cell_column), custom_call_target="tpu_custom_call" | custom-call | tf_op jit(solution)/shard_map/pallas_call | solution.py:23
  17.5 3.4 %collective-permute-done.3.refs_3_ = f32[60,8,128]{2,1,0:T(8,128)S(1)} collective-permute-done((f32[60,8,128]{2,1,0:T(8,128)}, f32[60,8,128]{2,1,0:T(8,128)S(1)}, u32[]{:S(2)}, u32[]{:S(2)}) %collective-permute-start.3) | collective-permute-done | bytes 245792 | tf_op jit(solution)/shard_map/ppermute | solution.py:451
  21.0 0.0 collective-permute-done.4.refs_4_
  21.0 4.4 %collective-permute-start.6 = (f32[13,16,128]{2,1,0:T(8,128)S(1)}, f32[13,16,128]{2,1,0:T(8,128)S(1)}, u32[]{:S(2)}, u32[]{:S(2)}) collective-permute-start(f32[13,16,128]{2,1,0:T(8,128)S(1)} %get-tuple-element.36), channel_id=1, source_target_pairs={{0,4},{4,0},{8,12},{12,8},{1,5},{5,1},{9,13},{13,9},{2,6},{6,2},{1... | collective-permute-start | bytes 319496 | tf_op jit(solution)/shard_map/ppermute | solution.py:454
  25.4 1.2 %collective-permute-start.7 = (f32[13,16,128]{2,1,0:T(8,128)S(1)}, f32[13,16,128]{2,1,0:T(8,128)S(1)}, u32[]{:S(2)}, u32[]{:S(2)}) collective-permute-start(f32[13,16,128]{2,1,0:T(8,128)S(1)} %get-tuple-element.37), channel_id=1, source_target_pairs={{0,8},{4,12},{8,0},{12,4},{1,9},{5,13},{9,1},{13,5},{2,10},{6,14},... | collective-permute-start | bytes 319496 | tf_op jit(solution)/shard_map/ppermute | solution.py:454
  26.5 1.5 %collective-permute-start.8 = (f32[13,16,128]{2,1,0:T(8,128)S(1)}, f32[13,16,128]{2,1,0:T(8,128)S(1)}, u32[]{:S(2)}, u32[]{:S(2)}) collective-permute-start(f32[13,16,128]{2,1,0:T(8,128)S(1)} %get-tuple-element.38), channel_id=1, source_target_pairs={{0,12},{4,8},{8,4},{12,0},{1,13},{5,9},{9,5},{13,1},{2,14},{6,10},... | collective-permute-start | bytes 319496 | tf_op jit(solution)/shard_map/ppermute | solution.py:454
  28.0 0.0 collective-permute-done.refs_1_
  28.0 0.0 collective-permute-done.1.refs_2_
  28.0 6.2 %shard_map.80 = (f32[12,8,256]{2,1,0:T(8,128)S(1)}, f32[12,8,256]{2,1,0:T(8,128)S(1)}, f32[8,256]{1,0:T(8,128)}) custom-call(f32[123,8,128]{2,1,0:T(8,128)S(1)} %get-tuple-element.21.refs_0_, f32[93,8,128]{2,1,0:T(8,128)S(1)} %collective-permute-done.refs_1_, f32[93,8,128]{2,1,0:T(8,128)S(1)} %collective-permute-done.1.refs_2_, ...), custom_call_target="tpu_custom_call" | custom-call | tf_op jit(solution)/shard_map/pallas_call | solution.py:23
  34.2 1.4 %collective-permute-start.5 = (f32[12,8,256]{2,1,0:T(8,128)S(1)}, f32[12,8,256]{2,1,0:T(8,128)S(1)}, u32[]{:S(2)}, u32[]{:S(2)}) collective-permute-start(f32[12,8,256]{2,1,0:T(8,128)S(1)} %get-tuple-element.34), channel_id=1, source_target_pairs={{0,2},{2,0},{1,3},{3,1},{4,6},{6,4},{5,7},{7,5},{8,10},{10,8},{9,1... | collective-permute-start | bytes 294920 | tf_op jit(solution)/shard_map/ppermute | solution.py:469
  35.6 0.0 collective-permute-done.6.refs_1_
  35.6 0.0 collective-permute-done.7.refs_2_
  35.6 0.0 collective-permute-done.8.refs_3_
  35.6 0.5 %shard_map.81.refs_2_ = f32[12,8,512]{2,1,0:T(8,128)S(1)} custom-call(f32[13,16,128]{2,1,0:T(8,128)S(1)} %get-tuple-element.35.refs_0_, f32[13,16,128]{2,1,0:T(8,128)S(1)} %collective-permute-done.6.refs_1_, f32[13,16,128]{2,1,0:T(8,128)S(1)} %collective-permute-done.7.refs_2_, f32[13,16,128]{2,1,0:T(8,128)S(1)} %collective-permute-done.8.refs_3_), custom_call_target="tpu_custom_call" | custom-call | tf_op jit(solution)/shard_map/pallas_call | solution.py:23
  36.1 2.7 %collective-permute-done.5.refs_1_ = f32[12,8,256]{2,1,0:T(8,128)S(1)} collective-permute-done((f32[12,8,256]{2,1,0:T(8,128)S(1)}, f32[12,8,256]{2,1,0:T(8,128)S(1)}, u32[]{:S(2)}, u32[]{:S(2)}) %collective-permute-start.5) | collective-permute-done | bytes 98336 | tf_op jit(solution)/shard_map/ppermute | solution.py:469
  38.8 0.7 %shard_map.82 = f32[12,8,512]{2,1,0:T(8,128)} custom-call(f32[12,8,256]{2,1,0:T(8,128)S(1)} %get-tuple-element.33.refs_0_, f32[12,8,256]{2,1,0:T(8,128)S(1)} %collective-permute-done.5.refs_1_, f32[12,8,512]{2,1,0:T(8,128)S(1)} %shard_map.81.refs_2_), custom_call_target="tpu_custom_call" | custom-call | tf_op jit(solution)/shard_map/pallas_call | solution.py:23
Async XLA Ops:
  0.6 15.5 %copy-start.1 = (s32[64,1]{0,1:T(1,128)S(1)}, s32[64,1]{0,1:T(1,128)}, u32[]{:S(2)}) copy-start(s32[64,1]{0,1:T(1,128)} %param.10) | copy-start | bytes 772
  2.2 14.8 %copy-start = (f32[1,12,64,128]{3,2,1,0:T(8,128)S(1)}, f32[1,12,64,128]{3,2,1,0:T(8,128)}, u32[]{:S(2)}) copy-start(f32[1,12,64,128]{3,2,1,0:T(8,128)} %param.9) | copy-start | bytes 1179652
  2.2 10.7 %collective-permute-start.2 = (f32[80,8,128]{2,1,0:T(8,128)S(1)}, f32[80,8,128]{2,1,0:T(8,128)S(1)}, u32[]{:S(2)}, u32[]{:S(2)}) collective-permute-start(f32[80,8,128]{2,1,0:T(8,128)S(1)} %get-tuple-element.24), channel_id=1, source_target_pairs={{0,2},{2,0},{1,3},{3,1},{4,6},{6,4},{5,7},{7,5},{8,10},{10,8},{9,1... | collective-permute-start | bytes 983048 | tf_op jit(solution)/shard_map/ppermute | solution.py:446
  5.2 22.8 %collective-permute-start = (f32[93,8,128]{2,1,0:T(8,128)S(1)}, f32[93,8,128]{2,1,0:T(8,128)S(1)}, u32[]{:S(2)}, u32[]{:S(2)}) collective-permute-start(f32[93,8,128]{2,1,0:T(8,128)S(1)} %get-tuple-element.22), channel_id=1, source_target_pairs={{0,4},{8,12},{4,0},{12,8},{1,5},{9,13},{5,1},{13,9},{2,6},{10,14},... | collective-permute-start | bytes 1142792 | tf_op jit(solution)/shard_map/ppermute | solution.py:448
  6.8 21.2 %collective-permute-start.1 = (f32[93,8,128]{2,1,0:T(8,128)S(1)}, f32[93,8,128]{2,1,0:T(8,128)S(1)}, u32[]{:S(2)}, u32[]{:S(2)}) collective-permute-start(f32[93,8,128]{2,1,0:T(8,128)S(1)} %get-tuple-element.23), channel_id=1, source_target_pairs={{4,8},{8,4},{5,9},{9,5},{6,10},{10,6},{7,11},{11,7},{20,24},{24,20... | collective-permute-start | bytes 1142792 | tf_op jit(solution)/shard_map/ppermute | solution.py:447
  13.6 7.4 %collective-permute-start.3 = (f32[60,8,128]{2,1,0:T(8,128)}, f32[60,8,128]{2,1,0:T(8,128)S(1)}, u32[]{:S(2)}, u32[]{:S(2)}) collective-permute-start(f32[60,8,128]{2,1,0:T(8,128)} %get-tuple-element.25), channel_id=1, source_target_pairs={{0,4},{8,12},{4,0},{12,8},{1,5},{9,13},{5,1},{13,9},{2,6},{10,14},... | collective-permute-start | bytes 737288 | tf_op jit(solution)/shard_map/ppermute | solution.py:451
  15.4 5.5 %collective-permute-start.4 = (f32[60,8,128]{2,1,0:T(8,128)S(1)}, f32[60,8,128]{2,1,0:T(8,128)S(1)}, u32[]{:S(2)}, u32[]{:S(2)}) collective-permute-start(f32[60,8,128]{2,1,0:T(8,128)S(1)} %get-tuple-element.26), channel_id=1, source_target_pairs={{4,8},{8,4},{5,9},{9,5},{6,10},{10,6},{7,11},{11,7},{20,24},{24,20... | collective-permute-start | bytes 737288 | tf_op jit(solution)/shard_map/ppermute | solution.py:450
  21.0 14.6 %collective-permute-start.6 = (f32[13,16,128]{2,1,0:T(8,128)S(1)}, f32[13,16,128]{2,1,0:T(8,128)S(1)}, u32[]{:S(2)}, u32[]{:S(2)}) collective-permute-start(f32[13,16,128]{2,1,0:T(8,128)S(1)} %get-tuple-element.36), channel_id=1, source_target_pairs={{0,4},{4,0},{8,12},{12,8},{1,5},{5,1},{9,13},{13,9},{2,6},{6,2},{1... | collective-permute-start | bytes 319496 | tf_op jit(solution)/shard_map/ppermute | solution.py:454
  25.4 10.3 %collective-permute-start.7 = (f32[13,16,128]{2,1,0:T(8,128)S(1)}, f32[13,16,128]{2,1,0:T(8,128)S(1)}, u32[]{:S(2)}, u32[]{:S(2)}) collective-permute-start(f32[13,16,128]{2,1,0:T(8,128)S(1)} %get-tuple-element.37), channel_id=1, source_target_pairs={{0,8},{4,12},{8,0},{12,4},{1,9},{5,13},{9,1},{13,5},{2,10},{6,14},... | collective-permute-start | bytes 319496 | tf_op jit(solution)/shard_map/ppermute | solution.py:454
  26.5 9.1 %collective-permute-start.8 = (f32[13,16,128]{2,1,0:T(8,128)S(1)}, f32[13,16,128]{2,1,0:T(8,128)S(1)}, u32[]{:S(2)}, u32[]{:S(2)}) collective-permute-start(f32[13,16,128]{2,1,0:T(8,128)S(1)} %get-tuple-element.38), channel_id=1, source_target_pairs={{0,12},{4,8},{8,4},{12,0},{1,13},{5,9},{9,5},{13,1},{2,14},{6,10},... | collective-permute-start | bytes 319496 | tf_op jit(solution)/shard_map/ppermute | solution.py:454
  34.2 4.6 %collective-permute-start.5 = (f32[12,8,256]{2,1,0:T(8,128)S(1)}, f32[12,8,256]{2,1,0:T(8,128)S(1)}, u32[]{:S(2)}, u32[]{:S(2)}) collective-permute-start(f32[12,8,256]{2,1,0:T(8,128)S(1)} %get-tuple-element.34), channel_id=1, source_target_pairs={{0,2},{2,0},{1,3},{3,1},{4,6},{6,4},{5,7},{7,5},{8,10},{10,8},{9,1... | collective-permute-start | bytes 294920 | tf_op jit(solution)/shard_map/ppermute | solution.py:469

commit v3 on v1

--- a/solution.py
+++ b/solution.py
@@ -15,6 +15,8 @@
 
 def call(body, out_shapes, *args, scratch=(), semaphores=0, inputs=pltpu.VMEM):
     spec = pl.BlockSpec(memory_space=pltpu.VMEM)
+    if inputs == pltpu.HBM:
+        args = [pltpu.with_memory_space_constraint(arg, pltpu.HBM) for arg in args]
     shapes = [pltpu.VMEM(shape, F32) for shape in scratch]
     if semaphores:
         shapes.append(pltpu.SemaphoreType.DMA((semaphores,)))
@@ -24,7 +26,7 @@
         in_specs=[pl.BlockSpec(memory_space=inputs)] * len(args),
         out_specs=[spec] * len(out_shapes),
         scratch_shapes=shapes,
-        compiler_params=pltpu.CompilerParams(vmem_limit_bytes=32 * 1024 * 1024),
+        compiler_params=pltpu.CompilerParams(vmem_limit_bytes=16 * 1024 * 1024),
     )(*args)
 
 
@@ -44,11 +46,15 @@
     return [[(b, partner_of(b, turn, count)) for b in range(count)] for turn in range(1, count)]
 
 
-def band_swaps(bands, first):
+def band_swaps(bands, tracers, first):
     swaps = []
     for b in range(bands):
         partner = b + 1 if (b - first) % 2 == 0 else b - 1
-        swaps.append((b, partner if 0 <= partner < bands else b))
+        for t in range(tracers):
+            if 0 <= partner < bands:
+                swaps.append((b * tracers + t, partner * tracers + t))
+            else:
+                swaps.append((b * tracers + t, b * tracers + (t ^ 1 if tracers % 2 == 0 else t)))
     return swaps
 
 
@@ -147,37 +153,33 @@
 
 def pack_rows(plan, get, size, north, store):
     first = plan.rows - HALO if north else 0
+    gap = 0 if north else HALO
     row = row_of(plan.rows)
-    place = 0
+    kept = (row >= first) & (row < first + HALO)
     fours = size // 4 if plan.packed(size) < size else 0
     for four in range(fours):
-        tiles = [get(4 * four + j) for j in range(4)]
+        last = get(4 * four + 3)
         for j in range(3):
-            extra = turn_rows(tiles[3], HALO - first - 2 * j)
-            store(place, jnp.where(row < HALO, turn_rows(tiles[j], -first), extra))
-            place += 1
+            store(3 * four + j, jnp.where(kept, get(4 * four + j), turn_rows(last, gap - first - 2 * j)))
     for index in range(4 * fours, size):
-        store(place, turn_rows(get(index), -first))
-        place += 1
+        store(index - fours, get(index))
 
 
 def unpack_rows(plan, get, size, north, store):
     first = plan.rows - HALO if north else 0
+    gap = 0 if north else HALO
     row = row_of(plan.rows)
-    place = 0
     fours = size // 4 if plan.packed(size) < size else 0
     for four in range(fours):
-        tiles = [get(place + j) for j in range(3)]
-        place += 3
-        last = jnp.zeros_like(tiles[0])
+        last = None
         for j in range(3):
-            store(4 * four + j, turn_rows(tiles[j], first))
-            moved = turn_rows(tiles[j], first + 2 * j - HALO)
-            last = jnp.where((row >= first + 2 * j) & (row < first + 2 * j + 2), moved, last)
+            tile = get(3 * four + j)
+            store(4 * four + j, tile)
+            moved = turn_rows(tile, first + 2 * j - gap)
+            last = moved if last is None else jnp.where(row >= first + 2 * j, moved, last)
         store(4 * four + 3, last)
     for index in range(4 * fours, size):
-        store(index, turn_rows(get(place), first))
-        place += 1
+        store(index, get(index - fours))
 
 
 def by_parity(body):
@@ -243,107 +245,189 @@
     by_parity(rows)
 
 
+def place_fields(plan, base, get, targets):
+    for kind, (target, at) in enumerate(targets):
+        for level in range(plan.count):
+            item = kind * plan.count + level
+            for t in range(plan.full):
+                target[base + level, at, t * LANES : (t + 1) * LANES] = get(item * plan.full + t)
+            rest = get(plan.rests_at + item // plan.slots)
+            target[base + level, at, plan.full * LANES :] = unpack_lanes(rest, item % plan.slots, plan.pitch)
+
+
+def place_diffusion(plan, at, get, target):
+    for level in range(plan.levels - 1):
+        for t in range(plan.full):
+            target[level, at, t * LANES : (t + 1) * LANES] = get(plan.diffusion_at + level * plan.diffusion_tiles + t)
+
+
+def place_diffusion_rest(plan, me, at, mine, get, target):
+    lane = lane_of(plan.rows)
+    for level in range(plan.levels - 1):
+        east = west = None
+        for turn in range(1, plan.devices):
+            edge = get(turn, plan.diffusion_at + level // plan.edge_slots)
+            edge = unpack_lanes(edge, level % plan.edge_slots, 16)
+            source = source_of(me, turn, plan.devices)
+            if east is None:
+                east = west = edge
+            else:
+                east = jnp.where(source == lax.rem(me + 1, plan.devices), edge, east)
+                west = jnp.where(source == lax.rem(me + plan.devices - 1, plan.devices), edge, west)
+        rest = jnp.where(lane < plan.middle, turn_lanes(east, plan.rest), west)
+        target[level, at] = jnp.where(lane < plan.rest, mine(level), rest) if plan.rest else rest
+
+
+def column_factors(plan, r, a, g):
+    k_prev = gain = zero = jnp.zeros(g.shape[1:], F32)
+    for level in range(plan.levels):
+        k_next = g[level] if level < plan.levels - 1 else zero
+        inverse = 1.0 / (1.0 + k_prev + k_next - k_prev * gain)
+        gain = k_next * inverse
+        r[level], a[level], g[level] = inverse, k_prev * inverse, gain
+        k_prev = k_next
+
+
+def split_zonal(plan, level, face_e, face_w):
+    west = face_w[level]
+    face_e[level] = jnp.maximum(pltpu.roll(west, plan.window - 1, 1), 0.0)
+    face_w[level] = jnp.minimum(west, 0.0)
+
+
+def sides(plan, even, swap_a, swap_b, begin):
+    return (
+        (True, slice(begin, begin + plan.rows), swap_a if even else swap_b),
+        (False, slice(begin + plan.rows, begin + 2 * plan.rows), swap_b if even else swap_a),
+    )
+
+
+def early_shapes(plan):
+    rows, window, full = plan.rows, plan.window, plan.full * LANES
+    shapes = [(plan.levels, rows, window)] * 4 + [(plan.count, 2 * rows, window)] * 4
+    shapes += [(plan.levels, rows, LANES)] * 3
+    shapes += [(plan.levels, 3 * rows, full)] * 3 if full else []
+    return shapes + ([(plan.levels, 2 * rows, LANES)] if plan.rest else [])
+
+
+def early_body(plan, *refs):
+    turns = plan.devices - 1
+    own, swap_a, swap_b = refs[:3]
+    lists = [own, *refs[3 : 3 + turns]]
+    outs, unpacked = refs[3 + turns : -1], refs[-1]
+    lam, face_e, face_w, lat = outs[:4]
+    halo_lam, halo_e, halo_w, halo_lat = outs[4:8]
+    rest_factors, full_factors = outs[8:11], outs[11:14]
+    me = lax.axis_index("lev")
+    rows = plan.rows
+    at = slice(0, rows)
+    for turn in range(plan.devices):
+        base = (source_of(me, turn, plan.devices) if turn else me) * plan.count
+        place_fields(plan, base, lists[turn].__getitem__, ((lam, at), (face_w, at), (lat, at)))
+    if plan.full:
+        place_diffusion(plan, at, own.__getitem__, full_factors[2])
+
+    def mine(level):
+        return own[plan.diffusion_at + level * plan.diffusion_tiles + plan.full]
+
+    place_diffusion_rest(plan, me, at, mine, lambda turn, index: lists[turn][index], rest_factors[2])
+
+    def halos(even):
+        for north, at, swap in sides(plan, even, swap_a, swap_b, 0):
+            unpack_rows(plan, swap.__getitem__, plan.own_size, not north, unpacked.__setitem__)
+            place_fields(plan, 0, unpacked.__getitem__, ((halo_lam, at), (halo_w, at), (halo_lat, at)))
+            if plan.full:
+                below = slice(at.start + rows, at.stop + rows)
+                place_diffusion(plan, below, unpacked.__getitem__, full_factors[2])
+            if plan.rest:
+                for level in range(plan.levels - 1):
+                    outs[-1][level, at] = unpacked[plan.diffusion_at + level * plan.diffusion_tiles + plan.full]
+
+    by_parity(halos)
+    for level in range(plan.levels):
+        split_zonal(plan, level, face_e, face_w)
+    for level in range(plan.count):
+        split_zonal(plan, level, halo_e, halo_w)
+    column_factors(plan, *rest_factors)
+    if plan.full:
+        column_factors(plan, *full_factors)
+
+
 def steps_body(plan, bands, *refs):
     turns = plan.devices - 1
-    own, early_a, early_b, late_a, late_b = refs[:5]
-    got = refs[5 : 5 + turns]
-    outs = refs[5 + turns : 5 + turns + plan.devices]
-    flux = refs[5 + turns + plan.devices]
-    lists, lam, face_e, face_w, lat_e, lat_w, r, a, g = refs[6 + turns + plan.devices :]
+    state = len(early_shapes(plan))
+    own_lam, own_e, own_w, own_lat, early_lam, early_e, early_w, early_lat = refs[:8]
+    own_factors, full_factors, left = refs[8:11], refs[11:14], refs[state - 1]
+    swap_a, swap_b = refs[state : state + 2]
+    outs = refs[state + 2 : state + 2 + plan.devices]
+    flux, lam, halo_e, halo_w, lat_e, lat_w, *rest_factors, unpacked = refs[state + 2 + plan.devices :]
     me, band = lax.axis_index("lev"), lax.axis_index("lat")
     rows, levels = plan.rows, plan.levels
-
-    late_size = plan.packed(plan.sent_size)
-
-    def unpack(even):
-        for side, from_north in ((1, True), (2, False)):
-            early, late = (early_a, late_a) if even == from_north else (early_b, late_b)
-
-            def store(index, tile, base=0, side=side):
-                lists[side - 1, base + index] = tile
-
-            unpack_rows(plan, lambda i, e=early: e[i], plan.own_size, not from_north, store)
+    packed = plan.packed(plan.sent_size)
+
+    for level in range(levels):
+        lam[level, :rows] = own_lam[level]
+        lat_w[level, :rows] = own_lat[level]
+    for level in range(plan.count):
+        at = me * plan.count + level
+        lam[at, rows:] = early_lam[level]
+        lat_w[at, rows:] = early_lat[level]
+        halo_e[at], halo_w[at] = early_e[level], early_w[level]
+
+    def halos(even):
+        for north, at, swap in sides(plan, even, swap_a, swap_b, rows):
+            above = slice(at.start - rows, at.stop - rows)
             for turn in range(turns):
-                base = plan.own_size + turn * plan.sent_size
-                unpack_rows(
-                    plan,
-                    lambda i, l=late, t=turn: l[t * late_size + i],
-                    plan.sent_size,
-                    not from_north,
-                    functools.partial(store, base=base),
-                )
-
-    by_parity(unpack)
-
-    def tile_of(side, turn, index):
-        if side:
-            return lists[side - 1, index if turn == 0 else plan.own_size + (turn - 1) * plan.sent_size + index]
-        return own[index] if turn == 0 else got[turn - 1][index]
-
-    lane = lane_of(rows)
-    for side in range(3):
-        at = pl.ds(side * rows, rows)
-        for turn in range(plan.devices):
-            base = source_of(me, turn, plan.devices) * plan.count if turn else me * plan.count
-            for kind, target in enumerate((lam, face_w, lat_w)):
-                for level in range(plan.count):
-                    item = kind * plan.count + level
-                    for t in range(plan.full):
-                        target[base + level, at, t * LANES : (t + 1) * LANES] = tile_of(side, turn, item * plan.full + t)
-                    rest = tile_of(side, turn, plan.rests_at + item // plan.slots)
-                    target[base + level, at, plan.full * LANES :] = unpack_lanes(rest, item % plan.slots, plan.pitch)
-        for level in range(levels - 1):
-            for t in range(plan.full):
-                g[level, at, t * LANES : (t + 1) * LANES] = tile_of(
-                    side, 0, plan.diffusion_at + level * plan.diffusion_tiles + t
-                )
-            east = west = jnp.zeros((rows, LANES), F32)
+                def get(index, base=turn * packed, swap=swap):
+                    return swap[base + index]
+
+                def store(index, tile, base=turn * plan.sent_size):
+                    unpacked[base + index] = tile
+
+                unpack_rows(plan, get, plan.sent_size, not north, store)
+
+            def tile_of(turn, index):
+                return unpacked[(turn - 1) * plan.sent_size + index]
+
             for turn in range(1, plan.devices):
-                edge = tile_of(side, turn, plan.diffusion_at + level // plan.edge_slots)
-                edge = unpack_lanes(edge, level % plan.edge_slots, 16)
-                if turns == 1:
-                    east = west = edge
-                else:
-                    source = source_of(me, turn, plan.devices)
-                    east = jnp.where(source == lax.rem(me + 1, plan.devices), edge, east)
-                    west = jnp.where(source == lax.rem(me + plan.devices - 1, plan.devices), edge, west)
-            rest = jnp.where(lane < plan.middle, turn_lanes(east, plan.rest), west)
-            if plan.rest:
-                mine = tile_of(side, 0, plan.diffusion_at + level * plan.diffusion_tiles + plan.full)
-                rest = jnp.where(lane < plan.rest, mine, rest)
-            g[level, at, plan.full * LANES :] = rest
-
+                base = source_of(me, turn, plan.devices) * plan.count
+                get = functools.partial(tile_of, turn)
+                place_fields(plan, base, get, ((lam, at), (halo_w, above), (lat_w, at)))
+            place_diffusion_rest(plan, me, above, lambda level, above=above: left[level, above], tile_of, rest_factors[2])
+
+    by_parity(halos)
+    for turn in range(1, plan.devices):
+        base = source_of(me, turn, plan.devices) * plan.count
+        for level in range(plan.count):
+            split_zonal(plan, base + level, halo_e, halo_w)
     row = lax.broadcasted_iota(jnp.int32, (3 * rows, plan.window), 0)
     closed = ((row == 0) & (band == 0)) | ((row == rows) & (band == bands - 1))
-    zero = jnp.zeros((3 * rows, plan.window), F32)
-    k_prev = gain = zero
     for level in range(levels):
         south = jnp.where(closed, 0.0, lat_w[level])
         lat_e[level] = jnp.maximum(pltpu.roll(south, 3 * rows - 1, 0), 0.0)
         lat_w[level] = jnp.minimum(south, 0.0)
-        west = face_w[level]
-        face_e[level] = jnp.maximum(pltpu.roll(west, plan.window - 1, 1), 0.0)
-        face_w[level] = jnp.minimum(west, 0.0)
-        k_next = g[level] if level < levels - 1 else zero
-        inverse = 1.0 / (1.0 + k_prev + k_next - k_prev * gain)
-        gain = k_next * inverse
-        r[level], a[level], g[level] = inverse, k_prev * inverse, gain
-        k_prev = k_next
+    column_factors(plan, *rest_factors)
 
     flux[...] = jnp.zeros_like(flux)
+    zero = jnp.zeros((3 * rows, plan.window), F32)
+
+    def factor(kind, level):
+        rest = jnp.concatenate([own_factors[kind][level], rest_factors[kind][level]], axis=0)
+        return jnp.concatenate([full_factors[kind][level], rest], axis=1) if plan.full else rest
 
     def step(_, carry):
         y = zero
         for level in range(levels):
-            y = lam[level] * r[level] + a[level] * y
+            y = lam[level] * factor(0, level) + factor(1, level) * y
             lam[level] = y
         w = zero
         for level in range(levels - 1, -1, -1):
-            w = lam[level] + g[level] * w
+            w = lam[level] + factor(2, level) * w
             up, down = pltpu.roll(w, 3 * rows - 1, 0), pltpu.roll(w, 1, 0)
             v = w + lat_e[level] * (up - w) + lat_w[level] * (w - down)
             east, west = pltpu.roll(v, plan.window - 1, 1), pltpu.roll(v, 1, 1)
-            lam[level] = v + face_e[level] * (east - v) + face_w[level] * (v - west)
+            face_e = jnp.concatenate([own_e[level], halo_e[level]], axis=0)
+            face_w = jnp.concatenate([own_w[level], halo_w[level]], axis=0)
+            lam[level] = v + face_e * (east - v) + face_w * (v - west)
         flux[...] += w[:rows, : plan.chunk]
         return carry
 
@@ -429,7 +513,8 @@
     devices = lax.axis_size("lev")
     bands = lax.axis_size("lat")
     plan = Plan(count, rows, width, devices)
-    swaps_a, swaps_b = band_swaps(bands, 0), band_swaps(bands, 1)
+    tracers = lax.axis_size("tr")
+    swaps_a, swaps_b = band_swaps(bands, tracers, 0), band_swaps(bands, tracers, 1)
     tile = (rows, LANES)
 
     early = plan.packed(plan.own_size)
@@ -445,27 +530,34 @@
         inputs=pltpu.HBM,
     )
     got = [lax.ppermute(part, "lev", pairs) for part, pairs in zip(sent, rounds(devices))]
-    early_a = lax.ppermute(early_a, "lat", swaps_a)
-    early_b = lax.ppermute(early_b, "lat", swaps_b)
+    early_b = lax.ppermute(early_b, ("lat", "tr"), swaps_b)
+    early_a = lax.ppermute(early_a, ("lat", "tr"), swaps_a)
     late_a, late_b = call(functools.partial(forward_rows_body, plan), [(late,) + tile] * 2, *got)
-    late_a = lax.ppermute(late_a, "lat", swaps_a)
-    late_b = lax.ppermute(late_b, "lat", swaps_b)
+    late_b = lax.ppermute(late_b, ("lat", "tr"), swaps_b)
+    late_a = lax.ppermute(late_a, ("lat", "tr"), swaps_a)
+    state = call(
+        functools.partial(early_body, plan),
+        early_shapes(plan),
+        own,
+        early_a,
+        early_b,
+        *got,
+        scratch=[(plan.own_size,) + tile],
+    )
     buckets = bucket_tiles(tile_values[0], tile_region, tile_cell)
-    late_a, late_b, *buckets = lax.optimization_barrier((late_a, late_b, *buckets))
+    late_a, late_b, state, buckets = lax.optimization_barrier((late_a, late_b, state, buckets))
     buckets = [buckets[0]] + [lax.ppermute(part, "lat", pairs) for part, pairs in zip(buckets[1:], rounds(bands))]
 
-    whole = (plan.levels, 3 * rows, plan.window)
-    lists = (2, plan.own_size + (devices - 1) * plan.sent_size) + tile
+    whole, halo = (plan.levels, 3 * rows, plan.window), (plan.levels, 2 * rows, plan.window)
     *outs, flux = call(
         functools.partial(steps_body, plan, bands),
         [(count, rows, plan.chunk)] * devices + [(rows, plan.chunk)],
-        own,
-        early_a,
-        early_b,
+        *state,
         late_a,
         late_b,
-        *got,
-        scratch=[lists] + [whole] * 8,
+        scratch=[whole, halo, halo, whole, whole]
+        + [(plan.levels, 2 * rows, LANES)] * 3
+        + [((devices - 1) * plan.sent_size,) + tile],
     )
     parts = [outs[0]] + [lax.ppermute(part, "lev", pairs) for part, pairs in zip(outs[1:], rounds(devices))]
     (added,) = call(functools.partial(sum_body, plan), [(count, rows, width)], *buckets)

time: 42.1 us -> 37.7 us (0.90)
  starting transfers between devices: 16.2 us -> 13 us
  local copies, waits for them, and re-layouts: 3.69 us -> 0.85 us
  Pallas kernels: 9.74 us -> 10.8 us
  waiting for transfers between devices: 11.6 us -> 12.3 us
    unnamed x11 -> x5, local copies, waits for them, and re-layouts: 2.95 us -> 0.11 us
    ppermute x3, starting transfers between devices: 7.01 us -> 5.12 us  [local(): lax.ppermute(part, 'lat', pairs)]
    ppermute x4, starting transfers between devices: 4.74 us -> 3.4 us  [the longest x1 1.82 us: local(): late_a = lax.ppermute(late_a, ('lat', 'tr'), swaps_a)]
    pallas_call x6 -> x7, Pallas kernels: 9.74 us -> 10.8 us  [call(): pl.pallas_call(body, out_shape=[jax.ShapeDtypeStruct(shape, F32) for shap...]
    ppermute x2, waiting for transfers between devices: 8.11 us -> 8.78 us  [local(): lax.ppermute(part, 'lev', pairs)]
  transfers between devices with their start and end apart: 9 -> 9, of which waited for: 3 -> 3; matrix products, arithmetic and copies ran while one was open for 2% -> 2% of each run, Pallas kernels for 19% -> 23%
where the time goes in v3:
time: 37.7 us; the launch traced here: 37.6 us
  starting transfers between devices  13 us (34%)
  waiting for transfers between devices  12.3 us (33%)
  Pallas kernels  10.8 us (29%)
  local copies, waits for them, and re-layouts  0.85 us (2%)
  between operations  0.69 us (2%)
    pallas_call x7, Pallas kernels, call(): pl.pallas_call(body, out_shape=[jax.ShapeDtypeStruct(shape, F32) for shap...  10.8 us
    ppermute x2, waiting for transfers between devices, local(): lax.ppermute(part, 'lev', pairs)  8.78 us
    ppermute x3, starting transfers between devices, local(): lax.ppermute(part, 'lat', pairs)  5.12 us
    ppermute x2, starting transfers between devices, local(): lax.ppermute(part, 'lev', pairs)  4.44 us
    ppermute x1, waiting for transfers between devices, local(): late_a = lax.ppermute(late_a, ('lat', 'tr'), swaps_a)  3.46 us
    ppermute x1, starting transfers between devices, local(): late_a = lax.ppermute(late_a, ('lat', 'tr'), swaps_a)  1.82 us
    ppermute x1, starting transfers between devices, local(): early_a = lax.ppermute(early_a, ('lat', 'tr'), swaps_a)  1.58 us
  transfers between devices with their start and end apart: 9, of which 3 were waited for; matrix products, arithmetic and copies ran while one was open for 2% of the time, Pallas kernels for 23%

profile of v3, /device:TPU:0, one launch (start us, length us, event | category | flops | bytes accessed | tf_op | source)
XLA Modules:
  0.0 37.6 jit_solution(4361792623778142874)
XLA Ops:
  0.6 0.0 copy-start.1
  0.6 1.5 %shard_map.77 = (f32[123,8,128]{2,1,0:T(8,128)S(1)}, f32[93,8,128]{2,1,0:T(8,128)S(1)}, f32[93,8,128]{2,1,0:T(8,128)S(1)}, f32[80,8,128]{2,1,0:T(8,128)S(1)}) custom-call(f32[12,8,512]{2,1,0:T(8,128)} %bitcast.8, f32[2,12,8,512]{3,2,1,0:T(8,128)} %refs_1_.1, f32[23,8,256]{2,1,0:T(8,128)} %refs_2_.1), custom_call_target="tpu_custom_call" | custom-call | tf_op jit(solution)/shard_map/pallas_call | solution.py:23
  2.2 0.0 copy-start
  2.2 3.0 %collective-permute-start = (f32[80,8,128]{2,1,0:T(8,128)S(1)}, f32[80,8,128]{2,1,0:T(8,128)S(1)}, u32[]{:S(2)}, u32[]{:S(2)}) collective-permute-start(f32[80,8,128]{2,1,0:T(8,128)S(1)} %get-tuple-element.49), channel_id=1, source_target_pairs={{0,2},{2,0},{1,3},{3,1},{4,6},{6,4},{5,7},{7,5},{8,10},{10,8},{9,1... | collective-permute-start | bytes 983048 | tf_op jit(solution)/shard_map/ppermute | solution.py:532
  5.2 1.6 %collective-permute-start.3 = (f32[93,8,128]{2,1,0:T(8,128)S(1)}, f32[93,8,128]{2,1,0:T(8,128)S(1)}, u32[]{:S(2)}, u32[]{:S(2)}) collective-permute-start(f32[93,8,128]{2,1,0:T(8,128)S(1)} %get-tuple-element.53), channel_id=1, source_target_pairs={{0,4},{1,5},{4,0},{5,1},{8,12},{9,13},{12,8},{13,9},{2,6},{3,7},{6... | collective-permute-start | bytes 1142792 | tf_op jit(solution)/shard_map/ppermute | solution.py:534
  6.7 0.0 collective-permute-start.4
  6.7 6.1 %collective-permute-done.refs_0_.refs_3_ = f32[80,8,128]{2,1,0:T(8,128)S(1)} collective-permute-done((f32[80,8,128]{2,1,0:T(8,128)S(1)}, f32[80,8,128]{2,1,0:T(8,128)S(1)}, u32[]{:S(2)}, u32[]{:S(2)}) %collective-permute-start) | collective-permute-done | bytes 327712 | tf_op jit(solution)/shard_map/ppermute | solution.py:532
  12.9 0.7 %shard_map.78 = (f32[60,8,128]{2,1,0:T(8,128)}, f32[60,8,128]{2,1,0:T(8,128)S(1)}) custom-call(f32[80,8,128]{2,1,0:T(8,128)S(1)} %collective-permute-done.refs_0_.refs_3_), custom_call_target="tpu_custom_call" | custom-call | tf_op jit(solution)/shard_map/pallas_call | solution.py:23
  13.6 1.8 %collective-permute-start.1 = (f32[60,8,128]{2,1,0:T(8,128)}, f32[60,8,128]{2,1,0:T(8,128)S(1)}, u32[]{:S(2)}, u32[]{:S(2)}) collective-permute-start(f32[60,8,128]{2,1,0:T(8,128)} %get-tuple-element.50), channel_id=1, source_target_pairs={{0,4},{1,5},{4,0},{5,1},{8,12},{9,13},{12,8},{13,9},{2,6},{3,7},{6... | collective-permute-start | bytes 737288 | tf_op jit(solution)/shard_map/ppermute | solution.py:537
  15.4 0.0 collective-permute-start.2
  15.5 0.0 copy-done.1
  15.5 0.1 copy.8.region_column
  15.6 0.7 %copy.9.cell_column = s32[64,1]{1,0:T(8,128)S(1)} copy(s32[64,1]{0,1:T(1,128)} %bitcast.10) | data formatting | bytes 512 | tf_op jit(solution)/shard_map/reshape | solution.py:507
  16.3 0.0 copy-done
  16.3 0.6 %shard_map.80 = (f32[13,16,128]{2,1,0:T(8,128)S(1)}, f32[13,16,128]{2,1,0:T(8,128)S(1)}, f32[13,16,128]{2,1,0:T(8,128)S(1)}, f32[13,16,128]{2,1,0:T(8,128)S(1)}) custom-call(f32[12,64,128]{2,1,0:T(8,128)S(1)} %bitcast.6, s32[64,1]{1,0:T(8,128)S(1)} %copy.8.region_column, s32[1,64]{1,0:T(1,128)S(1)} %bitcast.7, s32[64,1]{1,0:T(8,128)S(1)} %copy.9.cell_column), custom_call_target="tpu_custom_call" | custom-call | tf_op jit(solution)/shard_map/pallas_call | solution.py:23
  16.9 0.0 collective-permute-done.3.refs_1_
  16.9 0.0 collective-permute-done.4.refs_2_
  16.9 0.6 %shard_map.79 = (f32[24,8,384]{2,1,0:T(8,128)S(1)}, f32[24,8,384]{2,1,0:T(8,128)S(1)}, f32[24,8,384]{2,1,0:T(8,128)S(1)}, f32[24,8,384]{2,1,0:T(8,128)S(1)}, f32...) custom-call(f32[123,8,128]{2,1,0:T(8,128)S(1)} %get-tuple-element.52, ...), custom_call_target="tpu_custom_call" | custom-call | tf_op jit(solution)/shard_map/pallas_call | solution.py:23
  17.5 3.5 %collective-permute-done.1.refs_14_ = f32[60,8,128]{2,1,0:T(8,128)S(1)} collective-permute-done((f32[60,8,128]{2,1,0:T(8,128)}, f32[60,8,128]{2,1,0:T(8,128)S(1)}, u32[]{:S(2)}, u32[]{:S(2)}) %collective-permute-start.1) | collective-permute-done | bytes 245792 | tf_op jit(solution)/shard_map/ppermute | solution.py:537
  21.0 0.0 collective-permute-done.2.refs_15_
  21.0 2.5 %collective-permute-start.6 = (f32[13,16,128]{2,1,0:T(8,128)S(1)}, f32[13,16,128]{2,1,0:T(8,128)S(1)}, u32[]{:S(2)}, u32[]{:S(2)}) collective-permute-start(f32[13,16,128]{2,1,0:T(8,128)S(1)} %get-tuple-element.92), channel_id=1, source_target_pairs={{0,4},{4,0},{8,12},{12,8},{1,5},{5,1},{9,13},{13,9},{2,6},{6,2},{1... | collective-permute-start | bytes 319496 | tf_op jit(solution)/shard_map/ppermute | solution.py:549
  23.5 1.6 %collective-permute-start.7 = (f32[13,16,128]{2,1,0:T(8,128)S(1)}, f32[13,16,128]{2,1,0:T(8,128)S(1)}, u32[]{:S(2)}, u32[]{:S(2)}) collective-permute-start(f32[13,16,128]{2,1,0:T(8,128)S(1)} %get-tuple-element.93), channel_id=1, source_target_pairs={{0,8},{4,12},{8,0},{12,4},{1,9},{5,13},{9,1},{13,5},{2,10},{6,14},... | collective-permute-start | bytes 319496 | tf_op jit(solution)/shard_map/ppermute | solution.py:549
  25.1 1.0 %collective-permute-start.8 = (f32[13,16,128]{2,1,0:T(8,128)S(1)}, f32[13,16,128]{2,1,0:T(8,128)S(1)}, u32[]{:S(2)}, u32[]{:S(2)}) collective-permute-start(f32[13,16,128]{2,1,0:T(8,128)S(1)} %get-tuple-element.94), channel_id=1, source_target_pairs={{0,12},{4,8},{8,4},{12,0},{1,13},{5,9},{9,5},{13,1},{2,14},{6,10},... | collective-permute-start | bytes 319496 | tf_op jit(solution)/shard_map/ppermute | solution.py:549
  26.1 6.1 %shard_map.81 = (f32[12,8,256]{2,1,0:T(8,128)S(1)}, f32[12,8,256]{2,1,0:T(8,128)S(1)}, f32[8,256]{1,0:T(8,128)}) custom-call(f32[24,8,384]{2,1,0:T(8,128)S(1)} %get-tuple-element.73.refs_0_, f32[24,8,384]{2,1,0:T(8,128)S(1)} %get-tuple-element.74.refs_1_, f32[24,8,384]{2,1,0:T(8,128)S(1)} %get-tuple-element.75.refs_2_, ...), custom_call_target="tpu_custom_call" | custom-call | tf_op jit(solution)/shard_map/pallas_call | solution.py:23
  32.2 1.4 %collective-permute-start.5 = (f32[12,8,256]{2,1,0:T(8,128)S(1)}, f32[12,8,256]{2,1,0:T(8,128)S(1)}, u32[]{:S(2)}, u32[]{:S(2)}) collective-permute-start(f32[12,8,256]{2,1,0:T(8,128)S(1)} %get-tuple-element.90), channel_id=1, source_target_pairs={{0,2},{2,0},{1,3},{3,1},{4,6},{6,4},{5,7},{7,5},{8,10},{10,8},{9,1... | collective-permute-start | bytes 294920 | tf_op jit(solution)/shard_map/ppermute | solution.py:562
  33.7 0.0 collective-permute-done.6.refs_1_
  33.7 0.0 collective-permute-done.7.refs_2_
  33.7 0.0 collective-permute-done.8.refs_3_
  33.7 0.5 %shard_map.82.refs_2_ = f32[12,8,512]{2,1,0:T(8,128)S(1)} custom-call(f32[13,16,128]{2,1,0:T(8,128)S(1)} %get-tuple-element.91.refs_0_, f32[13,16,128]{2,1,0:T(8,128)S(1)} %collective-permute-done.6.refs_1_, f32[13,16,128]{2,1,0:T(8,128)S(1)} %collective-permute-done.7.refs_2_, f32[13,16,128]{2,1,0:T(8,128)S(1)} %collective-permute-done.8.refs_3_), custom_call_target="tpu_custom_call" | custom-call | tf_op jit(solution)/shard_map/pallas_call | solution.py:23
  34.2 2.6 %collective-permute-done.5.refs_1_ = f32[12,8,256]{2,1,0:T(8,128)S(1)} collective-permute-done((f32[12,8,256]{2,1,0:T(8,128)S(1)}, f32[12,8,256]{2,1,0:T(8,128)S(1)}, u32[]{:S(2)}, u32[]{:S(2)}) %collective-permute-start.5) | collective-permute-done | bytes 98336 | tf_op jit(solution)/shard_map/ppermute | solution.py:562
  36.9 0.7 %shard_map.83 = f32[12,8,512]{2,1,0:T(8,128)} custom-call(f32[12,8,256]{2,1,0:T(8,128)S(1)} %get-tuple-element.89.refs_0_, f32[12,8,256]{2,1,0:T(8,128)S(1)} %collective-permute-done.5.refs_1_, f32[12,8,512]{2,1,0:T(8,128)S(1)} %shard_map.82.refs_2_), custom_call_target="tpu_custom_call" | custom-call | tf_op jit(solution)/shard_map/pallas_call | solution.py:23
Async XLA Ops:
  0.6 14.8 %copy-start.1 = (s32[64,1]{0,1:T(1,128)S(1)}, s32[64,1]{0,1:T(1,128)}, u32[]{:S(2)}) copy-start(s32[64,1]{0,1:T(1,128)} %param.10) | copy-start | bytes 772
  2.2 14.1 %copy-start = (f32[1,12,64,128]{3,2,1,0:T(8,128)S(1)}, f32[1,12,64,128]{3,2,1,0:T(8,128)}, u32[]{:S(2)}) copy-start(f32[1,12,64,128]{3,2,1,0:T(8,128)} %param.9) | copy-start | bytes 1179652
  2.2 10.7 %collective-permute-start = (f32[80,8,128]{2,1,0:T(8,128)S(1)}, f32[80,8,128]{2,1,0:T(8,128)S(1)}, u32[]{:S(2)}, u32[]{:S(2)}) collective-permute-start(f32[80,8,128]{2,1,0:T(8,128)S(1)} %get-tuple-element.49), channel_id=1, source_target_pairs={{0,2},{2,0},{1,3},{3,1},{4,6},{6,4},{5,7},{7,5},{8,10},{10,8},{9,1... | collective-permute-start | bytes 983048 | tf_op jit(solution)/shard_map/ppermute | solution.py:532
  5.2 11.7 %collective-permute-start.3 = (f32[93,8,128]{2,1,0:T(8,128)S(1)}, f32[93,8,128]{2,1,0:T(8,128)S(1)}, u32[]{:S(2)}, u32[]{:S(2)}) collective-permute-start(f32[93,8,128]{2,1,0:T(8,128)S(1)} %get-tuple-element.53), channel_id=1, source_target_pairs={{0,4},{1,5},{4,0},{5,1},{8,12},{9,13},{12,8},{13,9},{2,6},{3,7},{6... | collective-permute-start | bytes 1142792 | tf_op jit(solution)/shard_map/ppermute | solution.py:534
  6.7 10.1 %collective-permute-start.4 = (f32[93,8,128]{2,1,0:T(8,128)S(1)}, f32[93,8,128]{2,1,0:T(8,128)S(1)}, u32[]{:S(2)}, u32[]{:S(2)}) collective-permute-start(f32[93,8,128]{2,1,0:T(8,128)S(1)} %get-tuple-element.54), channel_id=1, source_target_pairs={{0,1},{1,0},{4,8},{5,9},{8,4},{9,5},{12,13},{13,12},{2,3},{3,2},{6... | collective-permute-start | bytes 1142792 | tf_op jit(solution)/shard_map/ppermute | solution.py:533
  13.6 7.4 %collective-permute-start.1 = (f32[60,8,128]{2,1,0:T(8,128)}, f32[60,8,128]{2,1,0:T(8,128)S(1)}, u32[]{:S(2)}, u32[]{:S(2)}) collective-permute-start(f32[60,8,128]{2,1,0:T(8,128)} %get-tuple-element.50), channel_id=1, source_target_pairs={{0,4},{1,5},{4,0},{5,1},{8,12},{9,13},{12,8},{13,9},{2,6},{3,7},{6... | collective-permute-start | bytes 737288 | tf_op jit(solution)/shard_map/ppermute | solution.py:537
  15.4 5.5 %collective-permute-start.2 = (f32[60,8,128]{2,1,0:T(8,128)S(1)}, f32[60,8,128]{2,1,0:T(8,128)S(1)}, u32[]{:S(2)}, u32[]{:S(2)}) collective-permute-start(f32[60,8,128]{2,1,0:T(8,128)S(1)} %get-tuple-element.51), channel_id=1, source_target_pairs={{0,1},{1,0},{4,8},{5,9},{8,4},{9,5},{12,13},{13,12},{2,3},{3,2},{6... | collective-permute-start | bytes 737288 | tf_op jit(solution)/shard_map/ppermute | solution.py:536
  21.0 12.7 %collective-permute-start.6 = (f32[13,16,128]{2,1,0:T(8,128)S(1)}, f32[13,16,128]{2,1,0:T(8,128)S(1)}, u32[]{:S(2)}, u32[]{:S(2)}) collective-permute-start(f32[13,16,128]{2,1,0:T(8,128)S(1)} %get-tuple-element.92), channel_id=1, source_target_pairs={{0,4},{4,0},{8,12},{12,8},{1,5},{5,1},{9,13},{13,9},{2,6},{6,2},{1... | collective-permute-start | bytes 319496 | tf_op jit(solution)/shard_map/ppermute | solution.py:549
  23.5 10.2 %collective-permute-start.7 = (f32[13,16,128]{2,1,0:T(8,128)S(1)}, f32[13,16,128]{2,1,0:T(8,128)S(1)}, u32[]{:S(2)}, u32[]{:S(2)}) collective-permute-start(f32[13,16,128]{2,1,0:T(8,128)S(1)} %get-tuple-element.93), channel_id=1, source_target_pairs={{0,8},{4,12},{8,0},{12,4},{1,9},{5,13},{9,1},{13,5},{2,10},{6,14},... | collective-permute-start | bytes 319496 | tf_op jit(solution)/shard_map/ppermute | solution.py:549
  25.1 8.6 %collective-permute-start.8 = (f32[13,16,128]{2,1,0:T(8,128)S(1)}, f32[13,16,128]{2,1,0:T(8,128)S(1)}, u32[]{:S(2)}, u32[]{:S(2)}) collective-permute-start(f32[13,16,128]{2,1,0:T(8,128)S(1)} %get-tuple-element.94), channel_id=1, source_target_pairs={{0,12},{4,8},{8,4},{12,0},{1,13},{5,9},{9,5},{13,1},{2,14},{6,10},... | collective-permute-start | bytes 319496 | tf_op jit(solution)/shard_map/ppermute | solution.py:549
  32.2 4.6 %collective-permute-start.5 = (f32[12,8,256]{2,1,0:T(8,128)S(1)}, f32[12,8,256]{2,1,0:T(8,128)S(1)}, u32[]{:S(2)}, u32[]{:S(2)}) collective-permute-start(f32[12,8,256]{2,1,0:T(8,128)S(1)} %get-tuple-element.90), channel_id=1, source_target_pairs={{0,2},{2,0},{1,3},{3,1},{4,6},{6,4},{5,7},{7,5},{8,10},{10,8},{9,1... | collective-permute-start | bytes 294920 | tf_op jit(solution)/shard_map/ppermute | solution.py:562

commit v4 on v3

--- a/solution.py
+++ b/solution.py
@@ -545,7 +545,7 @@
         scratch=[(plan.own_size,) + tile],
     )
     buckets = bucket_tiles(tile_values[0], tile_region, tile_cell)
-    late_a, late_b, state, buckets = lax.optimization_barrier((late_a, late_b, state, buckets))
+    state, buckets = lax.optimization_barrier((state, buckets))
     buckets = [buckets[0]] + [lax.ppermute(part, "lat", pairs) for part, pairs in zip(buckets[1:], rounds(bands))]
 
     whole, halo = (plan.levels, 3 * rows, plan.window), (plan.levels, 2 * rows, plan.window)

time: 37.7 us -> 38.1 us (1.011)
  the two profiles are of different devices: /device:TPU:0 before, /device:TPU:16 now
where the time goes in v4:
time: 38.1 us; the launch traced here: 37.9 us
  waiting for transfers between devices  15.9 us (42%)
  Pallas kernels  10.8 us (28%)
  starting transfers between devices  9.68 us (25%)
  local copies, waits for them, and re-layouts  0.85 us (2%)
  between operations  0.69 us (2%)
    pallas_call x7, Pallas kernels, call(): pl.pallas_call(body, out_shape=[jax.ShapeDtypeStruct(shape, F32) for shap...  10.8 us
    ppermute x2, waiting for transfers between devices, local(): lax.ppermute(part, 'lev', pairs)  9.08 us
    ppermute x1, waiting for transfers between devices, local(): late_b = lax.ppermute(late_b, ('lat', 'tr'), swaps_b)  5.58 us
    ppermute x3, starting transfers between devices, local(): lax.ppermute(part, 'lat', pairs)  3.58 us
    ppermute x2, starting transfers between devices, local(): lax.ppermute(part, 'lev', pairs)  2.95 us
    ppermute x1, starting transfers between devices, local(): early_a = lax.ppermute(early_a, ('lat', 'tr'), swaps_a)  1.58 us
    ppermute x1, starting transfers between devices, local(): late_a = lax.ppermute(late_a, ('lat', 'tr'), swaps_a)  1.57 us
    ppermute x1, waiting for transfers between devices, local(): late_a = lax.ppermute(late_a, ('lat', 'tr'), swaps_a)  1.23 us
  transfers between devices with their start and end apart: 9, of which 4 were waited for; matrix products, arithmetic and copies ran while one was open for 2% of the time, Pallas kernels for 23%

profile of v4, /device:TPU:16, one launch (start us, length us, event | category | flops | bytes accessed | tf_op | source)
XLA Modules:
  0.0 37.9 jit_solution(8979357660092959668)
XLA Ops:
  0.6 0.0 copy-start.1
  0.6 1.5 %shard_map.77 = (f32[123,8,128]{2,1,0:T(8,128)S(1)}, f32[93,8,128]{2,1,0:T(8,128)S(1)}, f32[93,8,128]{2,1,0:T(8,128)S(1)}, f32[80,8,128]{2,1,0:T(8,128)S(1)}) custom-call(f32[12,8,512]{2,1,0:T(8,128)} %bitcast.8, f32[2,12,8,512]{3,2,1,0:T(8,128)} %refs_1_.1, f32[23,8,256]{2,1,0:T(8,128)} %refs_2_.1), custom_call_target="tpu_custom_call" | custom-call | tf_op jit(solution)/shard_map/pallas_call | solution.py:23
  2.2 0.0 copy-start
  2.2 1.6 %collective-permute-start.2 = (f32[80,8,128]{2,1,0:T(8,128)S(1)}, f32[80,8,128]{2,1,0:T(8,128)S(1)}, u32[]{:S(2)}, u32[]{:S(2)}) collective-permute-start(f32[80,8,128]{2,1,0:T(8,128)S(1)} %get-tuple-element.50), channel_id=1, source_target_pairs={{0,2},{2,0},{1,3},{3,1},{4,6},{6,4},{5,7},{7,5},{8,10},{10,8},{9,1... | collective-permute-start | bytes 983048 | tf_op jit(solution)/shard_map/ppermute | solution.py:532
  3.7 1.6 %collective-permute-start = (f32[93,8,128]{2,1,0:T(8,128)S(1)}, f32[93,8,128]{2,1,0:T(8,128)S(1)}, u32[]{:S(2)}, u32[]{:S(2)}) collective-permute-start(f32[93,8,128]{2,1,0:T(8,128)S(1)} %get-tuple-element.48), channel_id=1, source_target_pairs={{0,4},{1,5},{4,0},{5,1},{8,12},{9,13},{12,8},{13,9},{2,6},{3,7},{6... | collective-permute-start | bytes 1142792 | tf_op jit(solution)/shard_map/ppermute | solution.py:534
  5.3 0.0 collective-permute-start.1
  5.3 6.4 %collective-permute-done.2.refs_3_.refs_0_ = f32[80,8,128]{2,1,0:T(8,128)S(1)} collective-permute-done((f32[80,8,128]{2,1,0:T(8,128)S(1)}, f32[80,8,128]{2,1,0:T(8,128)S(1)}, u32[]{:S(2)}, u32[]{:S(2)}) %collective-permute-start.2) | collective-permute-done | bytes 327712 | tf_op jit(solution)/shard_map/ppermute | solution.py:532
  11.7 0.7 %shard_map.80 = (f32[60,8,128]{2,1,0:T(8,128)}, f32[60,8,128]{2,1,0:T(8,128)S(1)}) custom-call(f32[80,8,128]{2,1,0:T(8,128)S(1)} %collective-permute-done.2.refs_3_.refs_0_), custom_call_target="tpu_custom_call" | custom-call | tf_op jit(solution)/shard_map/pallas_call | solution.py:23
  12.4 1.6 %collective-permute-start.3 = (f32[60,8,128]{2,1,0:T(8,128)}, f32[60,8,128]{2,1,0:T(8,128)S(1)}, u32[]{:S(2)}, u32[]{:S(2)}) collective-permute-start(f32[60,8,128]{2,1,0:T(8,128)} %get-tuple-element.83), channel_id=1, source_target_pairs={{0,4},{1,5},{4,0},{5,1},{8,12},{9,13},{12,8},{13,9},{2,6},{3,7},{6... | collective-permute-start | bytes 737288 | tf_op jit(solution)/shard_map/ppermute | solution.py:537
  14.0 0.0 collective-permute-start.4
  14.0 0.0 copy-done.1
  14.0 0.1 copy.8.region_column
  14.1 0.7 %copy.9.cell_column = s32[64,1]{1,0:T(8,128)S(1)} copy(s32[64,1]{0,1:T(1,128)} %bitcast.10) | data formatting | bytes 512 | tf_op jit(solution)/shard_map/reshape | solution.py:507
  14.8 0.0 copy-done
  14.9 0.6 %shard_map.79 = (f32[13,16,128]{2,1,0:T(8,128)S(1)}, f32[13,16,128]{2,1,0:T(8,128)S(1)}, f32[13,16,128]{2,1,0:T(8,128)S(1)}, f32[13,16,128]{2,1,0:T(8,128)S(1)}) custom-call(f32[12,64,128]{2,1,0:T(8,128)S(1)} %bitcast.6, s32[64,1]{1,0:T(8,128)S(1)} %copy.8.region_column, s32[1,64]{1,0:T(1,128)S(1)} %bitcast.7, s32[64,1]{1,0:T(8,128)S(1)} %copy.9.cell_column), custom_call_target="tpu_custom_call" | custom-call | tf_op jit(solution)/shard_map/pallas_call | solution.py:23
  15.4 0.0 collective-permute-done.refs_1_
  15.4 0.0 collective-permute-done.1.refs_2_
  15.4 0.6 %shard_map.78 = (f32[24,8,384]{2,1,0:T(8,128)S(1)}, f32[24,8,384]{2,1,0:T(8,128)S(1)}, f32[24,8,384]{2,1,0:T(8,128)S(1)}, f32[24,8,384]{2,1,0:T(8,128)S(1)}, f32...) custom-call(f32[123,8,128]{2,1,0:T(8,128)S(1)} %get-tuple-element.47, ...), custom_call_target="tpu_custom_call" | custom-call | tf_op jit(solution)/shard_map/pallas_call | solution.py:23
  16.1 0.5 %collective-permute-start.6 = (f32[13,16,128]{2,1,0:T(8,128)S(1)}, f32[13,16,128]{2,1,0:T(8,128)S(1)}, u32[]{:S(2)}, u32[]{:S(2)}) collective-permute-start(f32[13,16,128]{2,1,0:T(8,128)S(1)} %get-tuple-element.88), channel_id=1, source_target_pairs={{0,4},{4,0},{8,12},{12,8},{1,5},{5,1},{9,13},{13,9},{2,6},{6,2},{1... | collective-permute-start | bytes 319496 | tf_op jit(solution)/shard_map/ppermute | solution.py:549
  16.6 3.0 %collective-permute-start.7 = (f32[13,16,128]{2,1,0:T(8,128)S(1)}, f32[13,16,128]{2,1,0:T(8,128)S(1)}, u32[]{:S(2)}, u32[]{:S(2)}) collective-permute-start(f32[13,16,128]{2,1,0:T(8,128)S(1)} %get-tuple-element.89), channel_id=1, source_target_pairs={{0,8},{4,12},{8,0},{12,4},{1,9},{5,13},{9,1},{13,5},{2,10},{6,14},... | collective-permute-start | bytes 319496 | tf_op jit(solution)/shard_map/ppermute | solution.py:549
  19.6 0.0 collective-permute-start.8
  19.7 1.2 %collective-permute-done.3.refs_14_ = f32[60,8,128]{2,1,0:T(8,128)S(1)} collective-permute-done((f32[60,8,128]{2,1,0:T(8,128)}, f32[60,8,128]{2,1,0:T(8,128)S(1)}, u32[]{:S(2)}, u32[]{:S(2)}) %collective-permute-start.3) | collective-permute-done | bytes 245792 | tf_op jit(solution)/shard_map/ppermute | solution.py:537
  20.9 5.6 %collective-permute-done.4.refs_15_ = f32[60,8,128]{2,1,0:T(8,128)S(1)} collective-permute-done((f32[60,8,128]{2,1,0:T(8,128)S(1)}, f32[60,8,128]{2,1,0:T(8,128)S(1)}, u32[]{:S(2)}, u32[]{:S(2)}) %collective-permute-start.4) | collective-permute-done | bytes 245792 | tf_op jit(solution)/shard_map/ppermute | solution.py:536
  26.5 6.1 %shard_map.81 = (f32[12,8,256]{2,1,0:T(8,128)S(1)}, f32[12,8,256]{2,1,0:T(8,128)S(1)}, f32[8,256]{1,0:T(8,128)}) custom-call(f32[24,8,384]{2,1,0:T(8,128)S(1)} %get-tuple-element.69.refs_0_, f32[24,8,384]{2,1,0:T(8,128)S(1)} %get-tuple-element.70.refs_1_, f32[24,8,384]{2,1,0:T(8,128)S(1)} %get-tuple-element.71.refs_2_, ...), custom_call_target="tpu_custom_call" | custom-call | tf_op jit(solution)/shard_map/pallas_call | solution.py:23
  32.6 1.4 %collective-permute-start.5 = (f32[12,8,256]{2,1,0:T(8,128)S(1)}, f32[12,8,256]{2,1,0:T(8,128)S(1)}, u32[]{:S(2)}, u32[]{:S(2)}) collective-permute-start(f32[12,8,256]{2,1,0:T(8,128)S(1)} %get-tuple-element.86), channel_id=1, source_target_pairs={{0,2},{2,0},{1,3},{3,1},{4,6},{6,4},{5,7},{7,5},{8,10},{10,8},{9,1... | collective-permute-start | bytes 294920 | tf_op jit(solution)/shard_map/ppermute | solution.py:562
  34.0 0.0 collective-permute-done.6.refs_1_
  34.0 0.0 collective-permute-done.7.refs_2_
  34.0 0.0 collective-permute-done.8.refs_3_
  34.0 0.5 %shard_map.82.refs_2_ = f32[12,8,512]{2,1,0:T(8,128)S(1)} custom-call(f32[13,16,128]{2,1,0:T(8,128)S(1)} %get-tuple-element.87.refs_0_, f32[13,16,128]{2,1,0:T(8,128)S(1)} %collective-permute-done.6.refs_1_, f32[13,16,128]{2,1,0:T(8,128)S(1)} %collective-permute-done.7.refs_2_, f32[13,16,128]{2,1,0:T(8,128)S(1)} %collective-permute-done.8.refs_3_), custom_call_target="tpu_custom_call" | custom-call | tf_op jit(solution)/shard_map/pallas_call | solution.py:23
  34.5 2.7 %collective-permute-done.5.refs_1_ = f32[12,8,256]{2,1,0:T(8,128)S(1)} collective-permute-done((f32[12,8,256]{2,1,0:T(8,128)S(1)}, f32[12,8,256]{2,1,0:T(8,128)S(1)}, u32[]{:S(2)}, u32[]{:S(2)}) %collective-permute-start.5) | collective-permute-done | bytes 98336 | tf_op jit(solution)/shard_map/ppermute | solution.py:562
  37.2 0.7 %shard_map.83 = f32[12,8,512]{2,1,0:T(8,128)} custom-call(f32[12,8,256]{2,1,0:T(8,128)S(1)} %get-tuple-element.85.refs_0_, f32[12,8,256]{2,1,0:T(8,128)S(1)} %collective-permute-done.5.refs_1_, f32[12,8,512]{2,1,0:T(8,128)S(1)} %shard_map.82.refs_2_), custom_call_target="tpu_custom_call" | custom-call | tf_op jit(solution)/shard_map/pallas_call | solution.py:23
Async XLA Ops:
  0.6 13.4 %copy-start.1 = (s32[64,1]{0,1:T(1,128)S(1)}, s32[64,1]{0,1:T(1,128)}, u32[]{:S(2)}) copy-start(s32[64,1]{0,1:T(1,128)} %param.10) | copy-start | bytes 772
  2.2 12.7 %copy-start = (f32[1,12,64,128]{3,2,1,0:T(8,128)S(1)}, f32[1,12,64,128]{3,2,1,0:T(8,128)}, u32[]{:S(2)}) copy-start(f32[1,12,64,128]{3,2,1,0:T(8,128)} %param.9) | copy-start | bytes 1179652
  2.2 9.5 %collective-permute-start.2 = (f32[80,8,128]{2,1,0:T(8,128)S(1)}, f32[80,8,128]{2,1,0:T(8,128)S(1)}, u32[]{:S(2)}, u32[]{:S(2)}) collective-permute-start(f32[80,8,128]{2,1,0:T(8,128)S(1)} %get-tuple-element.50), channel_id=1, source_target_pairs={{0,2},{2,0},{1,3},{3,1},{4,6},{6,4},{5,7},{7,5},{8,10},{10,8},{9,1... | collective-permute-start | bytes 983048 | tf_op jit(solution)/shard_map/ppermute | solution.py:532
  3.7 11.7 %collective-permute-start = (f32[93,8,128]{2,1,0:T(8,128)S(1)}, f32[93,8,128]{2,1,0:T(8,128)S(1)}, u32[]{:S(2)}, u32[]{:S(2)}) collective-permute-start(f32[93,8,128]{2,1,0:T(8,128)S(1)} %get-tuple-element.48), channel_id=1, source_target_pairs={{0,4},{1,5},{4,0},{5,1},{8,12},{9,13},{12,8},{13,9},{2,6},{3,7},{6... | collective-permute-start | bytes 1142792 | tf_op jit(solution)/shard_map/ppermute | solution.py:534
  5.3 10.1 %collective-permute-start.1 = (f32[93,8,128]{2,1,0:T(8,128)S(1)}, f32[93,8,128]{2,1,0:T(8,128)S(1)}, u32[]{:S(2)}, u32[]{:S(2)}) collective-permute-start(f32[93,8,128]{2,1,0:T(8,128)S(1)} %get-tuple-element.49), channel_id=1, source_target_pairs={{0,1},{1,0},{4,8},{5,9},{8,4},{9,5},{12,13},{13,12},{2,3},{3,2},{6... | collective-permute-start | bytes 1142792 | tf_op jit(solution)/shard_map/ppermute | solution.py:533
  12.4 8.5 %collective-permute-start.3 = (f32[60,8,128]{2,1,0:T(8,128)}, f32[60,8,128]{2,1,0:T(8,128)S(1)}, u32[]{:S(2)}, u32[]{:S(2)}) collective-permute-start(f32[60,8,128]{2,1,0:T(8,128)} %get-tuple-element.83), channel_id=1, source_target_pairs={{0,4},{1,5},{4,0},{5,1},{8,12},{9,13},{12,8},{13,9},{2,6},{3,7},{6... | collective-permute-start | bytes 737288 | tf_op jit(solution)/shard_map/ppermute | solution.py:537
  14.0 12.5 %collective-permute-start.4 = (f32[60,8,128]{2,1,0:T(8,128)S(1)}, f32[60,8,128]{2,1,0:T(8,128)S(1)}, u32[]{:S(2)}, u32[]{:S(2)}) collective-permute-start(f32[60,8,128]{2,1,0:T(8,128)S(1)} %get-tuple-element.84), channel_id=1, source_target_pairs={{0,1},{1,0},{4,8},{5,9},{8,4},{9,5},{12,13},{13,12},{2,3},{3,2},{6... | collective-permute-start | bytes 737288 | tf_op jit(solution)/shard_map/ppermute | solution.py:536
  16.1 17.9 %collective-permute-start.6 = (f32[13,16,128]{2,1,0:T(8,128)S(1)}, f32[13,16,128]{2,1,0:T(8,128)S(1)}, u32[]{:S(2)}, u32[]{:S(2)}) collective-permute-start(f32[13,16,128]{2,1,0:T(8,128)S(1)} %get-tuple-element.88), channel_id=1, source_target_pairs={{0,4},{4,0},{8,12},{12,8},{1,5},{5,1},{9,13},{13,9},{2,6},{6,2},{1... | collective-permute-start | bytes 319496 | tf_op jit(solution)/shard_map/ppermute | solution.py:549
  16.6 17.4 %collective-permute-start.7 = (f32[13,16,128]{2,1,0:T(8,128)S(1)}, f32[13,16,128]{2,1,0:T(8,128)S(1)}, u32[]{:S(2)}, u32[]{:S(2)}) collective-permute-start(f32[13,16,128]{2,1,0:T(8,128)S(1)} %get-tuple-element.89), channel_id=1, source_target_pairs={{0,8},{4,12},{8,0},{12,4},{1,9},{5,13},{9,1},{13,5},{2,10},{6,14},... | collective-permute-start | bytes 319496 | tf_op jit(solution)/shard_map/ppermute | solution.py:549
  19.6 14.4 %collective-permute-start.8 = (f32[13,16,128]{2,1,0:T(8,128)S(1)}, f32[13,16,128]{2,1,0:T(8,128)S(1)}, u32[]{:S(2)}, u32[]{:S(2)}) collective-permute-start(f32[13,16,128]{2,1,0:T(8,128)S(1)} %get-tuple-element.90), channel_id=1, source_target_pairs={{0,12},{4,8},{8,4},{12,0},{1,13},{5,9},{9,5},{13,1},{2,14},{6,10},... | collective-permute-start | bytes 319496 | tf_op jit(solution)/shard_map/ppermute | solution.py:549
  32.6 4.6 %collective-permute-start.5 = (f32[12,8,256]{2,1,0:T(8,128)S(1)}, f32[12,8,256]{2,1,0:T(8,128)S(1)}, u32[]{:S(2)}, u32[]{:S(2)}) collective-permute-start(f32[12,8,256]{2,1,0:T(8,128)S(1)} %get-tuple-element.86), channel_id=1, source_target_pairs={{0,2},{2,0},{1,3},{3,1},{4,6},{6,4},{5,7},{7,5},{8,10},{10,8},{9,1... | collective-permute-start | bytes 294920 | tf_op jit(solution)/shard_map/ppermute | solution.py:562

commit v5 on v3

--- a/solution.py
+++ b/solution.py
@@ -13,7 +13,7 @@
 F32 = jnp.float32
 
 
-def call(body, out_shapes, *args, scratch=(), semaphores=0, inputs=pltpu.VMEM):
+def call(body, out_shapes, *args, scratch=(), semaphores=0, inputs=pltpu.VMEM, keep=False):
     spec = pl.BlockSpec(memory_space=pltpu.VMEM)
     if inputs == pltpu.HBM:
         args = [pltpu.with_memory_space_constraint(arg, pltpu.HBM) for arg in args]
@@ -22,7 +22,7 @@
         shapes.append(pltpu.SemaphoreType.DMA((semaphores,)))
     return pl.pallas_call(
         body,
-        out_shape=[jax.ShapeDtypeStruct(shape, F32) for shape in out_shapes],
+        out_shape=[pltpu.VMEM(shape, F32) if keep else jax.ShapeDtypeStruct(shape, F32) for shape in out_shapes],
         in_specs=[pl.BlockSpec(memory_space=inputs)] * len(args),
         out_specs=[spec] * len(out_shapes),
         scratch_shapes=shapes,
@@ -305,7 +305,7 @@
     rows, window, full = plan.rows, plan.window, plan.full * LANES
     shapes = [(plan.levels, rows, window)] * 4 + [(plan.count, 2 * rows, window)] * 4
     shapes += [(plan.levels, rows, LANES)] * 3
-    shapes += [(plan.levels, 3 * rows, full)] * 3 if full else []
+    shapes += [(plan.levels, 3 * rows, full)] * 3 + [(plan.levels, rows, full)] * 3 if full else []
     return shapes + ([(plan.levels, 2 * rows, LANES)] if plan.rest else [])
 
 
@@ -350,13 +350,20 @@
     column_factors(plan, *rest_factors)
     if plan.full:
         column_factors(plan, *full_factors)
+        for narrow, factors in zip(outs[14:17], full_factors):
+            for level in range(plan.levels):
+                narrow[level] = near_rows(plan, factors[level, rows : 2 * rows], factors[level, 2 * rows :])
+
+
+def near_rows(plan, north, south):
+    return jnp.where(lax.broadcasted_iota(jnp.int32, north.shape, 0) < plan.rows // 2, north, south)
 
 
 def steps_body(plan, bands, *refs):
     turns = plan.devices - 1
     state = len(early_shapes(plan))
     own_lam, own_e, own_w, own_lat, early_lam, early_e, early_w, early_lat = refs[:8]
-    own_factors, full_factors, left = refs[8:11], refs[11:14], refs[state - 1]
+    own_factors, full_factors, narrow_factors, left = refs[8:11], refs[11:14], refs[14:17], refs[state - 1]
     swap_a, swap_b = refs[state : state + 2]
     outs = refs[state + 2 : state + 2 + plan.devices]
     flux, lam, halo_e, halo_w, lat_e, lat_w, *rest_factors, unpacked = refs[state + 2 + plan.devices :]
@@ -408,30 +415,40 @@
     column_factors(plan, *rest_factors)
 
     flux[...] = jnp.zeros_like(flux)
-    zero = jnp.zeros((3 * rows, plan.window), F32)
-
-    def factor(kind, level):
-        rest = jnp.concatenate([own_factors[kind][level], rest_factors[kind][level]], axis=0)
-        return jnp.concatenate([full_factors[kind][level], rest], axis=1) if plan.full else rest
-
-    def step(_, carry):
-        y = zero
+
+    def factor(kind, level, height):
+        rest = jnp.concatenate([own_factors[kind][level], rest_factors[kind][level, : height - rows]], axis=0)
+        if not plan.full:
+            return rest
+        if height == 3 * rows:
+            full = full_factors[kind][level]
+        else:
+            full = jnp.concatenate([full_factors[kind][level, :rows], narrow_factors[kind][level]], axis=0)
+        return jnp.concatenate([full, rest], axis=1)
+
+    def step(height, _, carry):
+        y = w = jnp.zeros((height, plan.window), F32)
         for level in range(levels):
-            y = lam[level] * factor(0, level) + factor(1, level) * y
-            lam[level] = y
-        w = zero
+            y = lam[level, :height] * factor(0, level, height) + factor(1, level, height) * y
+            lam[level, :height] = y
         for level in range(levels - 1, -1, -1):
-            w = lam[level] + factor(2, level) * w
-            up, down = pltpu.roll(w, 3 * rows - 1, 0), pltpu.roll(w, 1, 0)
-            v = w + lat_e[level] * (up - w) + lat_w[level] * (w - down)
+            w = lam[level, :height] + factor(2, level, height) * w
+            up, down = pltpu.roll(w, height - 1, 0), pltpu.roll(w, 1, 0)
+            v = w + lat_e[level, :height] * (up - w) + lat_w[level, :height] * (w - down)
             east, west = pltpu.roll(v, plan.window - 1, 1), pltpu.roll(v, 1, 1)
-            face_e = jnp.concatenate([own_e[level], halo_e[level]], axis=0)
-            face_w = jnp.concatenate([own_w[level], halo_w[level]], axis=0)
-            lam[level] = v + face_e * (east - v) + face_w * (v - west)
+            face_e = jnp.concatenate([own_e[level], halo_e[level, : height - rows]], axis=0)
+            face_w = jnp.concatenate([own_w[level], halo_w[level, : height - rows]], axis=0)
+            lam[level, :height] = v + face_e * (east - v) + face_w * (v - west)
         flux[...] += w[:rows, : plan.chunk]
         return carry
 
-    lax.fori_loop(0, STEPS, step, 0)
+    wide = max(0, HALO - rows // 2)
+    lax.fori_loop(0, wide, functools.partial(step, 3 * rows), 0)
+    for level in range(levels):
+        for ref, begin in ((lam, rows), (lat_e, rows), (lat_w, rows), (halo_e, 0), (halo_w, 0), *((f, 0) for f in rest_factors)):
+            north, south = ref[level, begin : begin + rows], ref[level, begin + rows : begin + 2 * rows]
+            ref[level, begin : begin + rows] = near_rows(plan, north, south)
+    lax.fori_loop(wide, STEPS, functools.partial(step, 2 * rows), 0)
     flux[...] = flux[...] / STEPS
     for turn in range(plan.devices):
         base = (partner_of(me, turn, plan.devices) if turn else me) * plan.count
@@ -532,7 +549,7 @@
     got = [lax.ppermute(part, "lev", pairs) for part, pairs in zip(sent, rounds(devices))]
     early_b = lax.ppermute(early_b, ("lat", "tr"), swaps_b)
     early_a = lax.ppermute(early_a, ("lat", "tr"), swaps_a)
-    late_a, late_b = call(functools.partial(forward_rows_body, plan), [(late,) + tile] * 2, *got)
+    late_a, late_b = call(functools.partial(forward_rows_body, plan), [(late,) + tile] * 2, *got, keep=True)
     late_b = lax.ppermute(late_b, ("lat", "tr"), swaps_b)
     late_a = lax.ppermute(late_a, ("lat", "tr"), swaps_a)
     state = call(

time: 37.7 us -> 36.7 us (0.973)
  Pallas kernels: 10.8 us -> 9.82 us
    pallas_call x7, Pallas kernels: 10.8 us -> 9.82 us  [call(): pl.pallas_call(body, out_shape=[pltpu.VMEM(shape, F32) if keep else jax.S...]
  transfers between devices with their start and end apart: 9 -> 9, of which waited for: 3 -> 4; matrix products, arithmetic and copies ran while one was open for 2% -> 2% of each run, Pallas kernels for 23% -> 21%
where the time goes in v5:
time: 36.7 us; the launch traced here: 36.5 us
  starting transfers between devices  13 us (35%)
  waiting for transfers between devices  12.2 us (33%)
  Pallas kernels  9.82 us (27%)
  local copies, waits for them, and re-layouts  0.85 us (2%)
  between operations  0.69 us (2%)
    pallas_call x7, Pallas kernels, call(): pl.pallas_call(body, out_shape=[pltpu.VMEM(shape, F32) if keep else jax.S...  9.82 us
    ppermute x2, waiting for transfers between devices, local(): lax.ppermute(part, 'lev', pairs)  8.7 us
    ppermute x3, starting transfers between devices, local(): lax.ppermute(part, 'lat', pairs)  5.12 us
    ppermute x2, starting transfers between devices, local(): lax.ppermute(part, 'lev', pairs)  4.44 us
    ppermute x1, waiting for transfers between devices, local(): late_a = lax.ppermute(late_a, ('lat', 'tr'), swaps_a)  3.42 us
    ppermute x1, starting transfers between devices, local(): late_a = lax.ppermute(late_a, ('lat', 'tr'), swaps_a)  1.82 us
    ppermute x1, starting transfers between devices, local(): early_a = lax.ppermute(early_a, ('lat', 'tr'), swaps_a)  1.58 us
    reshape x1, local copies, waits for them, and re-layouts, bucket_tiles(): tile_cell.reshape(tiles, 1)  0.74 us
  transfers between devices with their start and end apart: 9, of which 4 were waited for; matrix products, arithmetic and copies ran while one was open for 2% of the time, Pallas kernels for 21%

profile of v5, /device:TPU:0, one launch (start us, length us, event | category | flops | bytes accessed | tf_op | source)
XLA Modules:
  0.0 36.5 jit_solution(12659805680527990199)
XLA Ops:
  0.6 0.0 copy-start.1
  0.6 1.5 %shard_map.77 = (f32[123,8,128]{2,1,0:T(8,128)S(1)}, f32[93,8,128]{2,1,0:T(8,128)S(1)}, f32[93,8,128]{2,1,0:T(8,128)S(1)}, f32[80,8,128]{2,1,0:T(8,128)S(1)}) custom-call(f32[12,8,512]{2,1,0:T(8,128)} %bitcast.8, f32[2,12,8,512]{3,2,1,0:T(8,128)} %refs_1_.1, f32[23,8,256]{2,1,0:T(8,128)} %refs_2_.1), custom_call_target="tpu_custom_call" | custom-call | tf_op jit(solution)/shard_map/pallas_call | solution.py:23
  2.2 0.0 copy-start
  2.2 3.0 %collective-permute-start = (f32[80,8,128]{2,1,0:T(8,128)S(1)}, f32[80,8,128]{2,1,0:T(8,128)S(1)}, u32[]{:S(2)}, u32[]{:S(2)}) collective-permute-start(f32[80,8,128]{2,1,0:T(8,128)S(1)} %get-tuple-element.55), channel_id=1, source_target_pairs={{0,2},{2,0},{1,3},{3,1},{4,6},{6,4},{5,7},{7,5},{8,10},{10,8},{9,1... | collective-permute-start | bytes 983048 | tf_op jit(solution)/shard_map/ppermute | solution.py:549
  5.2 1.6 %collective-permute-start.3 = (f32[93,8,128]{2,1,0:T(8,128)S(1)}, f32[93,8,128]{2,1,0:T(8,128)S(1)}, u32[]{:S(2)}, u32[]{:S(2)}) collective-permute-start(f32[93,8,128]{2,1,0:T(8,128)S(1)} %get-tuple-element.59), channel_id=1, source_target_pairs={{0,4},{1,5},{4,0},{5,1},{8,12},{9,13},{12,8},{13,9},{2,6},{3,7},{6... | collective-permute-start | bytes 1142792 | tf_op jit(solution)/shard_map/ppermute | solution.py:551
  6.7 0.0 collective-permute-start.4
  6.7 6.1 %collective-permute-done.refs_0_.refs_3_ = f32[80,8,128]{2,1,0:T(8,128)S(1)} collective-permute-done((f32[80,8,128]{2,1,0:T(8,128)S(1)}, f32[80,8,128]{2,1,0:T(8,128)S(1)}, u32[]{:S(2)}, u32[]{:S(2)}) %collective-permute-start) | collective-permute-done | bytes 327712 | tf_op jit(solution)/shard_map/ppermute | solution.py:549
  12.9 0.7 %shard_map.78 = (f32[60,8,128]{2,1,0:T(8,128)}, f32[60,8,128]{2,1,0:T(8,128)S(1)}) custom-call(f32[80,8,128]{2,1,0:T(8,128)S(1)} %collective-permute-done.refs_0_.refs_3_), custom_call_target="tpu_custom_call" | custom-call | tf_op jit(solution)/shard_map/pallas_call | solution.py:23
  13.6 1.8 %collective-permute-start.1 = (f32[60,8,128]{2,1,0:T(8,128)}, f32[60,8,128]{2,1,0:T(8,128)S(1)}, u32[]{:S(2)}, u32[]{:S(2)}) collective-permute-start(f32[60,8,128]{2,1,0:T(8,128)} %get-tuple-element.56), channel_id=1, source_target_pairs={{0,4},{1,5},{4,0},{5,1},{8,12},{9,13},{12,8},{13,9},{2,6},{3,7},{6... | collective-permute-start | bytes 737288 | tf_op jit(solution)/shard_map/ppermute | solution.py:554
  15.4 0.0 collective-permute-start.2
  15.5 0.0 copy-done.1
  15.5 0.1 copy.8.region_column
  15.6 0.7 %copy.9.cell_column = s32[64,1]{1,0:T(8,128)S(1)} copy(s32[64,1]{0,1:T(1,128)} %bitcast.10) | data formatting | bytes 512 | tf_op jit(solution)/shard_map/reshape | solution.py:524
  16.3 0.0 copy-done
  16.3 0.6 %shard_map.80 = (f32[13,16,128]{2,1,0:T(8,128)S(1)}, f32[13,16,128]{2,1,0:T(8,128)S(1)}, f32[13,16,128]{2,1,0:T(8,128)S(1)}, f32[13,16,128]{2,1,0:T(8,128)S(1)}) custom-call(f32[12,64,128]{2,1,0:T(8,128)S(1)} %bitcast.6, s32[64,1]{1,0:T(8,128)S(1)} %copy.8.region_column, s32[1,64]{1,0:T(1,128)S(1)} %bitcast.7, s32[64,1]{1,0:T(8,128)S(1)} %copy.9.cell_column), custom_call_target="tpu_custom_call" | custom-call | tf_op jit(solution)/shard_map/pallas_call | solution.py:23
  16.9 0.0 collective-permute-done.3.refs_1_
  16.9 0.0 collective-permute-done.4.refs_2_
  16.9 0.7 %shard_map.79 = (f32[24,8,384]{2,1,0:T(8,128)S(1)}, f32[24,8,384]{2,1,0:T(8,128)S(1)}, f32[24,8,384]{2,1,0:T(8,128)S(1)}, f32[24,8,384]{2,1,0:T(8,128)S(1)}, f32...) custom-call(f32[123,8,128]{2,1,0:T(8,128)S(1)} %get-tuple-element.58, ...), custom_call_target="tpu_custom_call" | custom-call | tf_op jit(solution)/shard_map/pallas_call | solution.py:23
  17.6 3.4 %collective-permute-done.1.refs_17_ = f32[60,8,128]{2,1,0:T(8,128)S(1)} collective-permute-done((f32[60,8,128]{2,1,0:T(8,128)}, f32[60,8,128]{2,1,0:T(8,128)S(1)}, u32[]{:S(2)}, u32[]{:S(2)}) %collective-permute-start.1) | collective-permute-done | bytes 245792 | tf_op jit(solution)/shard_map/ppermute | solution.py:554
  21.0 0.0 collective-permute-done.2.refs_18_
  21.0 2.5 %collective-permute-start.6 = (f32[13,16,128]{2,1,0:T(8,128)S(1)}, f32[13,16,128]{2,1,0:T(8,128)S(1)}, u32[]{:S(2)}, u32[]{:S(2)}) collective-permute-start(f32[13,16,128]{2,1,0:T(8,128)S(1)} %get-tuple-element.104), channel_id=1, source_target_pairs={{0,4},{4,0},{8,12},{12,8},{1,5},{5,1},{9,13},{13,9},{2,6},{6,2},{1... | collective-permute-start | bytes 319496 | tf_op jit(solution)/shard_map/ppermute | solution.py:566
  23.5 1.6 %collective-permute-start.7 = (f32[13,16,128]{2,1,0:T(8,128)S(1)}, f32[13,16,128]{2,1,0:T(8,128)S(1)}, u32[]{:S(2)}, u32[]{:S(2)}) collective-permute-start(f32[13,16,128]{2,1,0:T(8,128)S(1)} %get-tuple-element.105), channel_id=1, source_target_pairs={{0,8},{4,12},{8,0},{12,4},{1,9},{5,13},{9,1},{13,5},{2,10},{6,14},... | collective-permute-start | bytes 319496 | tf_op jit(solution)/shard_map/ppermute | solution.py:566
  25.1 1.0 %collective-permute-start.8 = (f32[13,16,128]{2,1,0:T(8,128)S(1)}, f32[13,16,128]{2,1,0:T(8,128)S(1)}, u32[]{:S(2)}, u32[]{:S(2)}) collective-permute-start(f32[13,16,128]{2,1,0:T(8,128)S(1)} %get-tuple-element.106), channel_id=1, source_target_pairs={{0,12},{4,8},{8,4},{12,0},{1,13},{5,9},{9,5},{13,1},{2,14},{6,10},... | collective-permute-start | bytes 319496 | tf_op jit(solution)/shard_map/ppermute | solution.py:566
  26.1 5.1 %shard_map.81 = (f32[12,8,256]{2,1,0:T(8,128)S(1)}, f32[12,8,256]{2,1,0:T(8,128)S(1)}, f32[8,256]{1,0:T(8,128)}) custom-call(f32[24,8,384]{2,1,0:T(8,128)S(1)} %get-tuple-element.82.refs_0_, f32[24,8,384]{2,1,0:T(8,128)S(1)} %get-tuple-element.83.refs_1_, f32[24,8,384]{2,1,0:T(8,128)S(1)} %get-tuple-element.84.refs_2_, ...), custom_call_target="tpu_custom_call" | custom-call | tf_op jit(solution)/shard_map/pallas_call | solution.py:23
  31.2 1.4 %collective-permute-start.5 = (f32[12,8,256]{2,1,0:T(8,128)S(1)}, f32[12,8,256]{2,1,0:T(8,128)S(1)}, u32[]{:S(2)}, u32[]{:S(2)}) collective-permute-start(f32[12,8,256]{2,1,0:T(8,128)S(1)} %get-tuple-element.102), channel_id=1, source_target_pairs={{0,2},{2,0},{1,3},{3,1},{4,6},{6,4},{5,7},{7,5},{8,10},{10,8},{9,1... | collective-permute-start | bytes 294920 | tf_op jit(solution)/shard_map/ppermute | solution.py:579
  32.7 0.0 collective-permute-done.6.refs_1_
  32.7 0.1 collective-permute-done.7.refs_2_
  32.7 0.0 collective-permute-done.8.refs_3_
  32.7 0.5 %shard_map.82.refs_2_ = f32[12,8,512]{2,1,0:T(8,128)S(1)} custom-call(f32[13,16,128]{2,1,0:T(8,128)S(1)} %get-tuple-element.103.refs_0_, f32[13,16,128]{2,1,0:T(8,128)S(1)} %collective-permute-done.6.refs_1_, f32[13,16,128]{2,1,0:T(8,128)S(1)} %collective-permute-done.7.refs_2_, f32[13,16,128]{2,1,0:T(8,128)S(1)} %collective-permute-done.8.refs_3_), custom_call_target="tpu_custom_call" | custom-call | tf_op jit(solution)/shard_map/pallas_call | solution.py:23
  33.3 2.6 %collective-permute-done.5.refs_1_ = f32[12,8,256]{2,1,0:T(8,128)S(1)} collective-permute-done((f32[12,8,256]{2,1,0:T(8,128)S(1)}, f32[12,8,256]{2,1,0:T(8,128)S(1)}, u32[]{:S(2)}, u32[]{:S(2)}) %collective-permute-start.5) | collective-permute-done | bytes 98336 | tf_op jit(solution)/shard_map/ppermute | solution.py:579
  35.8 0.7 %shard_map.83 = f32[12,8,512]{2,1,0:T(8,128)} custom-call(f32[12,8,256]{2,1,0:T(8,128)S(1)} %get-tuple-element.101.refs_0_, f32[12,8,256]{2,1,0:T(8,128)S(1)} %collective-permute-done.5.refs_1_, f32[12,8,512]{2,1,0:T(8,128)S(1)} %shard_map.82.refs_2_), custom_call_target="tpu_custom_call" | custom-call | tf_op jit(solution)/shard_map/pallas_call | solution.py:23
Async XLA Ops:
  0.6 14.8 %copy-start.1 = (s32[64,1]{0,1:T(1,128)S(1)}, s32[64,1]{0,1:T(1,128)}, u32[]{:S(2)}) copy-start(s32[64,1]{0,1:T(1,128)} %param.10) | copy-start | bytes 772
  2.2 14.1 %copy-start = (f32[1,12,64,128]{3,2,1,0:T(8,128)S(1)}, f32[1,12,64,128]{3,2,1,0:T(8,128)}, u32[]{:S(2)}) copy-start(f32[1,12,64,128]{3,2,1,0:T(8,128)} %param.9) | copy-start | bytes 1179652
  2.2 10.7 %collective-permute-start = (f32[80,8,128]{2,1,0:T(8,128)S(1)}, f32[80,8,128]{2,1,0:T(8,128)S(1)}, u32[]{:S(2)}, u32[]{:S(2)}) collective-permute-start(f32[80,8,128]{2,1,0:T(8,128)S(1)} %get-tuple-element.55), channel_id=1, source_target_pairs={{0,2},{2,0},{1,3},{3,1},{4,6},{6,4},{5,7},{7,5},{8,10},{10,8},{9,1... | collective-permute-start | bytes 983048 | tf_op jit(solution)/shard_map/ppermute | solution.py:549
  5.2 11.7 %collective-permute-start.3 = (f32[93,8,128]{2,1,0:T(8,128)S(1)}, f32[93,8,128]{2,1,0:T(8,128)S(1)}, u32[]{:S(2)}, u32[]{:S(2)}) collective-permute-start(f32[93,8,128]{2,1,0:T(8,128)S(1)} %get-tuple-element.59), channel_id=1, source_target_pairs={{0,4},{1,5},{4,0},{5,1},{8,12},{9,13},{12,8},{13,9},{2,6},{3,7},{6... | collective-permute-start | bytes 1142792 | tf_op jit(solution)/shard_map/ppermute | solution.py:551
  6.7 10.1 %collective-permute-start.4 = (f32[93,8,128]{2,1,0:T(8,128)S(1)}, f32[93,8,128]{2,1,0:T(8,128)S(1)}, u32[]{:S(2)}, u32[]{:S(2)}) collective-permute-start(f32[93,8,128]{2,1,0:T(8,128)S(1)} %get-tuple-element.60), channel_id=1, source_target_pairs={{0,1},{1,0},{4,8},{5,9},{8,4},{9,5},{12,13},{13,12},{2,3},{3,2},{6... | collective-permute-start | bytes 1142792 | tf_op jit(solution)/shard_map/ppermute | solution.py:550
  13.6 7.4 %collective-permute-start.1 = (f32[60,8,128]{2,1,0:T(8,128)}, f32[60,8,128]{2,1,0:T(8,128)S(1)}, u32[]{:S(2)}, u32[]{:S(2)}) collective-permute-start(f32[60,8,128]{2,1,0:T(8,128)} %get-tuple-element.56), channel_id=1, source_target_pairs={{0,4},{1,5},{4,0},{5,1},{8,12},{9,13},{12,8},{13,9},{2,6},{3,7},{6... | collective-permute-start | bytes 737288 | tf_op jit(solution)/shard_map/ppermute | solution.py:554
  15.4 5.5 %collective-permute-start.2 = (f32[60,8,128]{2,1,0:T(8,128)S(1)}, f32[60,8,128]{2,1,0:T(8,128)S(1)}, u32[]{:S(2)}, u32[]{:S(2)}) collective-permute-start(f32[60,8,128]{2,1,0:T(8,128)S(1)} %get-tuple-element.57), channel_id=1, source_target_pairs={{0,1},{1,0},{4,8},{5,9},{8,4},{9,5},{12,13},{13,12},{2,3},{3,2},{6... | collective-permute-start | bytes 737288 | tf_op jit(solution)/shard_map/ppermute | solution.py:553
  21.0 11.7 %collective-permute-start.6 = (f32[13,16,128]{2,1,0:T(8,128)S(1)}, f32[13,16,128]{2,1,0:T(8,128)S(1)}, u32[]{:S(2)}, u32[]{:S(2)}) collective-permute-start(f32[13,16,128]{2,1,0:T(8,128)S(1)} %get-tuple-element.104), channel_id=1, source_target_pairs={{0,4},{4,0},{8,12},{12,8},{1,5},{5,1},{9,13},{13,9},{2,6},{6,2},{1... | collective-permute-start | bytes 319496 | tf_op jit(solution)/shard_map/ppermute | solution.py:566
  23.5 9.3 %collective-permute-start.7 = (f32[13,16,128]{2,1,0:T(8,128)S(1)}, f32[13,16,128]{2,1,0:T(8,128)S(1)}, u32[]{:S(2)}, u32[]{:S(2)}) collective-permute-start(f32[13,16,128]{2,1,0:T(8,128)S(1)} %get-tuple-element.105), channel_id=1, source_target_pairs={{0,8},{4,12},{8,0},{12,4},{1,9},{5,13},{9,1},{13,5},{2,10},{6,14},... | collective-permute-start | bytes 319496 | tf_op jit(solution)/shard_map/ppermute | solution.py:566
  25.1 7.7 %collective-permute-start.8 = (f32[13,16,128]{2,1,0:T(8,128)S(1)}, f32[13,16,128]{2,1,0:T(8,128)S(1)}, u32[]{:S(2)}, u32[]{:S(2)}) collective-permute-start(f32[13,16,128]{2,1,0:T(8,128)S(1)} %get-tuple-element.106), channel_id=1, source_target_pairs={{0,12},{4,8},{8,4},{12,0},{1,13},{5,9},{9,5},{13,1},{2,14},{6,10},... | collective-permute-start | bytes 319496 | tf_op jit(solution)/shard_map/ppermute | solution.py:566
  31.2 4.6 %collective-permute-start.5 = (f32[12,8,256]{2,1,0:T(8,128)S(1)}, f32[12,8,256]{2,1,0:T(8,128)S(1)}, u32[]{:S(2)}, u32[]{:S(2)}) collective-permute-start(f32[12,8,256]{2,1,0:T(8,128)S(1)} %get-tuple-element.102), channel_id=1, source_target_pairs={{0,2},{2,0},{1,3},{3,1},{4,6},{6,4},{5,7},{7,5},{8,10},{10,8},{9,1... | collective-permute-start | bytes 294920 | tf_op jit(solution)/shard_map/ppermute | solution.py:579

commit v6 on v5

--- a/solution.py
+++ b/solution.py
@@ -195,7 +195,7 @@
 
 
 def pack_body(plan, *refs):
-    sources, (own, swap_a, swap_b), sent = refs[:3], refs[3:6], refs[6:-4]
+    sources, own, sent = refs[:3], refs[3], refs[4:-4]
     field, courant, diffusion, arrived = refs[-4:]
     copies = [
         pltpu.make_async_copy(source, target, arrived.at[i])
@@ -222,9 +222,11 @@
         for index, tile in enumerate(field_tiles(plan, field, courant, target) + edges):
             sent[turn - 1][index] = tile
 
+
+def pack_rows_body(plan, own, swap_a, swap_b):
     def rows(even):
         for north, swap in ((even, swap_a), (not even, swap_b)):
-            pack_rows(plan, lambda i: own[i], plan.own_size, north, swap.__setitem__)
+            pack_rows(plan, own.__getitem__, plan.own_size, north, swap.__setitem__)
 
     by_parity(rows)
 
@@ -426,29 +428,32 @@
             full = jnp.concatenate([full_factors[kind][level, :rows], narrow_factors[kind][level]], axis=0)
         return jnp.concatenate([full, rest], axis=1)
 
-    def step(height, _, carry):
+    def step(height, kept, _, carry):
         y = w = jnp.zeros((height, plan.window), F32)
         for level in range(levels):
             y = lam[level, :height] * factor(0, level, height) + factor(1, level, height) * y
             lam[level, :height] = y
         for level in range(levels - 1, -1, -1):
             w = lam[level, :height] + factor(2, level, height) * w
-            up, down = pltpu.roll(w, height - 1, 0), pltpu.roll(w, 1, 0)
-            v = w + lat_e[level, :height] * (up - w) + lat_w[level, :height] * (w - down)
+            up, down, v = pltpu.roll(w, height - 1, 0)[:kept], pltpu.roll(w, 1, 0)[:kept], w[:kept]
+            v = v + lat_e[level, :kept] * (up - v) + lat_w[level, :kept] * (v - down)
             east, west = pltpu.roll(v, plan.window - 1, 1), pltpu.roll(v, 1, 1)
-            face_e = jnp.concatenate([own_e[level], halo_e[level, : height - rows]], axis=0)
-            face_w = jnp.concatenate([own_w[level], halo_w[level, : height - rows]], axis=0)
-            lam[level, :height] = v + face_e * (east - v) + face_w * (v - west)
+            face_e, face_w = own_e[level], own_w[level]
+            if kept > rows:
+                face_e = jnp.concatenate([face_e, halo_e[level, : kept - rows]], axis=0)
+                face_w = jnp.concatenate([face_w, halo_w[level, : kept - rows]], axis=0)
+            lam[level, :kept] = v + face_e * (east - v) + face_w * (v - west)
         flux[...] += w[:rows, : plan.chunk]
         return carry
 
     wide = max(0, HALO - rows // 2)
-    lax.fori_loop(0, wide, functools.partial(step, 3 * rows), 0)
+    lax.fori_loop(0, wide, functools.partial(step, 3 * rows, 3 * rows), 0)
     for level in range(levels):
         for ref, begin in ((lam, rows), (lat_e, rows), (lat_w, rows), (halo_e, 0), (halo_w, 0), *((f, 0) for f in rest_factors)):
             north, south = ref[level, begin : begin + rows], ref[level, begin + rows : begin + 2 * rows]
             ref[level, begin : begin + rows] = near_rows(plan, north, south)
-    lax.fori_loop(wide, STEPS, functools.partial(step, 2 * rows), 0)
+    lax.fori_loop(wide, STEPS - 1, functools.partial(step, 2 * rows, 2 * rows), 0)
+    step(2 * rows, rows, 0, 0)
     flux[...] = flux[...] / STEPS
     for turn in range(plan.devices):
         base = (partner_of(me, turn, plan.devices) if turn else me) * plan.count
@@ -536,9 +541,9 @@
 
     early = plan.packed(plan.own_size)
     late = plan.packed(plan.sent_size) * (devices - 1)
-    own, early_a, early_b, *sent = call(
+    own, *sent = call(
         functools.partial(pack_body, plan),
-        [(plan.own_size,) + tile] + [(early,) + tile] * 2 + [(plan.sent_size,) + tile] * (devices - 1),
+        [(plan.own_size,) + tile] + [(plan.sent_size,) + tile] * (devices - 1),
         field,
         courant,
         diffusion,
@@ -547,6 +552,7 @@
         inputs=pltpu.HBM,
     )
     got = [lax.ppermute(part, "lev", pairs) for part, pairs in zip(sent, rounds(devices))]
+    early_a, early_b = call(functools.partial(pack_rows_body, plan), [(early,) + tile] * 2, own)
     early_b = lax.ppermute(early_b, ("lat", "tr"), swaps_b)
     early_a = lax.ppermute(early_a, ("lat", "tr"), swaps_a)
     late_a, late_b = call(functools.partial(forward_rows_body, plan), [(late,) + tile] * 2, *got, keep=True)
@@ -563,7 +569,10 @@
     )
     buckets = bucket_tiles(tile_values[0], tile_region, tile_cell)
     late_a, late_b, state, buckets = lax.optimization_barrier((late_a, late_b, state, buckets))
-    buckets = [buckets[0]] + [lax.ppermute(part, "lat", pairs) for part, pairs in zip(buckets[1:], rounds(bands))]
+    crossing = {}
+    for turn in sorted(range(1, bands), key=lambda turn: (turn == bands - 1, -turn)):
+        crossing[turn] = lax.ppermute(buckets[turn], "lat", rounds(bands)[turn - 1])
+    buckets = [buckets[0]] + [crossing[turn] for turn in range(1, bands)]
 
     whole, halo = (plan.levels, 3 * rows, plan.window), (plan.levels, 2 * rows, plan.window)
     *outs, flux = call(

time: 36.7 us -> 36.5 us (level)
    ppermute x3, waiting for transfers between devices: 0.09 us -> 0.53 us  [local(): crossing[turn] = lax.ppermute(buckets[turn], 'lat', rounds(bands)[turn - 1])]
    ppermute x2, waiting for transfers between devices: 8.7 us -> 8.26 us  [local(): lax.ppermute(part, 'lev', pairs)]
    pallas_call x7 -> x8, Pallas kernels: 9.82 us -> 9.6 us  [call(): pl.pallas_call(body, out_shape=[pltpu.VMEM(shape, F32) if keep else jax.S...]
where the time goes in v6:
time: 36.5 us; the launch traced here: 36.4 us
  starting transfers between devices  13 us (36%)
  waiting for transfers between devices  12.2 us (33%)
  Pallas kernels  9.6 us (26%)
  local copies, waits for them, and re-layouts  0.85 us (2%)
  between operations  0.68 us (2%)
    pallas_call x8, Pallas kernels, call(): pl.pallas_call(body, out_shape=[pltpu.VMEM(shape, F32) if keep else jax.S...  9.6 us
    ppermute x2, waiting for transfers between devices, local(): lax.ppermute(part, 'lev', pairs)  8.26 us
    ppermute x3, starting transfers between devices, local(): crossing[turn] = lax.ppermute(buckets[turn], 'lat', rounds(bands)[turn - 1])  5.26 us
    ppermute x2, starting transfers between devices, local(): lax.ppermute(part, 'lev', pairs)  4.3 us
    ppermute x1, waiting for transfers between devices, local(): late_a = lax.ppermute(late_a, ('lat', 'tr'), swaps_a)  3.42 us
    ppermute x1, starting transfers between devices, local(): late_a = lax.ppermute(late_a, ('lat', 'tr'), swaps_a)  1.82 us
    ppermute x1, starting transfers between devices, local(): early_a = lax.ppermute(early_a, ('lat', 'tr'), swaps_a)  1.64 us
    reshape x1, local copies, waits for them, and re-layouts, bucket_tiles(): tile_cell.reshape(tiles, 1)  0.74 us
  transfers between devices with their start and end apart: 9, of which 4 were waited for; matrix products, arithmetic and copies ran while one was open for 2% of the time, Pallas kernels for 21%

profile of v6, /device:TPU:0, one launch (start us, length us, event | category | flops | bytes accessed | tf_op | source)
XLA Modules:
  0.0 36.4 jit_solution(9145458242103358947)
XLA Ops:
  0.6 1.4 %shard_map.77 = (f32[123,8,128]{2,1,0:T(8,128)S(1)}, f32[80,8,128]{2,1,0:T(8,128)S(1)}) custom-call(f32[12,8,512]{2,1,0:T(8,128)} %bitcast.8, f32[2,12,8,512]{3,2,1,0:T(8,128)} %refs_1_.1, f32[23,8,256]{2,1,0:T(8,128)} %refs_2_.1), custom_call_target="tpu_custom_call" | custom-call | tf_op jit(solution)/shard_map/pallas_call | solution.py:23
  2.1 3.0 %collective-permute-start = (f32[80,8,128]{2,1,0:T(8,128)S(1)}, f32[80,8,128]{2,1,0:T(8,128)S(1)}, u32[]{:S(2)}, u32[]{:S(2)}) collective-permute-start(f32[80,8,128]{2,1,0:T(8,128)S(1)} %get-tuple-element.55), channel_id=1, source_target_pairs={{0,2},{2,0},{1,3},{3,1},{4,6},{6,4},{5,7},{7,5},{8,10},{10,8},{9,1... | collective-permute-start | bytes 983048 | tf_op jit(solution)/shard_map/ppermute | solution.py:554
  5.1 0.0 copy-start
  5.1 0.1 shard_map.79
  5.2 1.6 %collective-permute-start.3 = (f32[93,8,128]{2,1,0:T(8,128)S(1)}, f32[93,8,128]{2,1,0:T(8,128)S(1)}, u32[]{:S(2)}, u32[]{:S(2)}) collective-permute-start(f32[93,8,128]{2,1,0:T(8,128)S(1)} %get-tuple-element.59), channel_id=1, source_target_pairs={{0,4},{1,5},{4,0},{5,1},{8,12},{9,13},{12,8},{13,9},{2,6},{3,7},{6... | collective-permute-start | bytes 1142792 | tf_op jit(solution)/shard_map/ppermute | solution.py:557
  6.8 0.0 collective-permute-start.4
  6.8 6.0 %collective-permute-done.refs_0_.refs_3_ = f32[80,8,128]{2,1,0:T(8,128)S(1)} collective-permute-done((f32[80,8,128]{2,1,0:T(8,128)S(1)}, f32[80,8,128]{2,1,0:T(8,128)S(1)}, u32[]{:S(2)}, u32[]{:S(2)}) %collective-permute-start) | collective-permute-done | bytes 327712 | tf_op jit(solution)/shard_map/ppermute | solution.py:554
  12.8 0.7 %shard_map.78 = (f32[60,8,128]{2,1,0:T(8,128)}, f32[60,8,128]{2,1,0:T(8,128)S(1)}) custom-call(f32[80,8,128]{2,1,0:T(8,128)S(1)} %collective-permute-done.refs_0_.refs_3_), custom_call_target="tpu_custom_call" | custom-call | tf_op jit(solution)/shard_map/pallas_call | solution.py:23
  13.5 0.0 copy-start.1
  13.5 1.8 %collective-permute-start.1 = (f32[60,8,128]{2,1,0:T(8,128)}, f32[60,8,128]{2,1,0:T(8,128)S(1)}, u32[]{:S(2)}, u32[]{:S(2)}) collective-permute-start(f32[60,8,128]{2,1,0:T(8,128)} %get-tuple-element.56), channel_id=1, source_target_pairs={{0,4},{1,5},{4,0},{5,1},{8,12},{9,13},{12,8},{13,9},{2,6},{3,7},{6... | collective-permute-start | bytes 737288 | tf_op jit(solution)/shard_map/ppermute | solution.py:560
  15.3 0.0 collective-permute-start.2
  15.4 0.0 copy-done.1
  15.4 0.1 copy.8.region_column
  15.5 0.7 %copy.9.cell_column = s32[64,1]{1,0:T(8,128)S(1)} copy(s32[64,1]{0,1:T(1,128)} %bitcast.10) | data formatting | bytes 512 | tf_op jit(solution)/shard_map/reshape | solution.py:529
  16.2 0.0 copy-done
  16.2 0.6 %shard_map.81 = (f32[13,16,128]{2,1,0:T(8,128)S(1)}, f32[13,16,128]{2,1,0:T(8,128)S(1)}, f32[13,16,128]{2,1,0:T(8,128)S(1)}, f32[13,16,128]{2,1,0:T(8,128)S(1)}) custom-call(f32[12,64,128]{2,1,0:T(8,128)S(1)} %bitcast.6, s32[64,1]{1,0:T(8,128)S(1)} %copy.8.region_column, s32[1,64]{1,0:T(1,128)S(1)} %bitcast.7, s32[64,1]{1,0:T(8,128)S(1)} %copy.9.cell_column), custom_call_target="tpu_custom_call" | custom-call | tf_op jit(solution)/shard_map/pallas_call | solution.py:23
  16.8 0.0 collective-permute-done.3.refs_1_
  16.8 0.0 collective-permute-done.4.refs_2_
  16.8 0.7 %shard_map.80 = (f32[24,8,384]{2,1,0:T(8,128)S(1)}, f32[24,8,384]{2,1,0:T(8,128)S(1)}, f32[24,8,384]{2,1,0:T(8,128)S(1)}, f32[24,8,384]{2,1,0:T(8,128)S(1)}, f32...) custom-call(f32[123,8,128]{2,1,0:T(8,128)S(1)} %get-tuple-element.58, ...), custom_call_target="tpu_custom_call" | custom-call | tf_op jit(solution)/shard_map/pallas_call | solution.py:23
  17.5 3.4 %collective-permute-done.1.refs_17_ = f32[60,8,128]{2,1,0:T(8,128)S(1)} collective-permute-done((f32[60,8,128]{2,1,0:T(8,128)}, f32[60,8,128]{2,1,0:T(8,128)S(1)}, u32[]{:S(2)}, u32[]{:S(2)}) %collective-permute-start.1) | collective-permute-done | bytes 245792 | tf_op jit(solution)/shard_map/ppermute | solution.py:560
  20.9 0.0 collective-permute-done.2.refs_18_
  20.9 2.6 %collective-permute-start.6 = (f32[13,16,128]{2,1,0:T(8,128)S(1)}, f32[13,16,128]{2,1,0:T(8,128)S(1)}, u32[]{:S(2)}, u32[]{:S(2)}) collective-permute-start(f32[13,16,128]{2,1,0:T(8,128)S(1)} %get-tuple-element.104), channel_id=1, source_target_pairs={{0,4},{4,0},{8,12},{12,8},{1,5},{5,1},{9,13},{13,9},{2,6},{6,2},{1... | collective-permute-start | bytes 319496 | tf_op jit(solution)/shard_map/ppermute | solution.py:574
  23.5 1.5 %collective-permute-start.7 = (f32[13,16,128]{2,1,0:T(8,128)S(1)}, f32[13,16,128]{2,1,0:T(8,128)S(1)}, u32[]{:S(2)}, u32[]{:S(2)}) collective-permute-start(f32[13,16,128]{2,1,0:T(8,128)S(1)} %get-tuple-element.105), channel_id=1, source_target_pairs={{0,8},{4,12},{8,0},{12,4},{1,9},{5,13},{9,1},{13,5},{2,10},{6,14},... | collective-permute-start | bytes 319496 | tf_op jit(solution)/shard_map/ppermute | solution.py:574
  25.0 1.2 %collective-permute-start.8 = (f32[13,16,128]{2,1,0:T(8,128)S(1)}, f32[13,16,128]{2,1,0:T(8,128)S(1)}, u32[]{:S(2)}, u32[]{:S(2)}) collective-permute-start(f32[13,16,128]{2,1,0:T(8,128)S(1)} %get-tuple-element.106), channel_id=1, source_target_pairs={{0,12},{4,8},{8,4},{12,0},{1,13},{5,9},{9,5},{13,1},{2,14},{6,10},... | collective-permute-start | bytes 319496 | tf_op jit(solution)/shard_map/ppermute | solution.py:574
  26.1 4.9 %shard_map.82 = (f32[12,8,256]{2,1,0:T(8,128)S(1)}, f32[12,8,256]{2,1,0:T(8,128)S(1)}, f32[8,256]{1,0:T(8,128)}) custom-call(f32[24,8,384]{2,1,0:T(8,128)S(1)} %get-tuple-element.82.refs_0_, f32[24,8,384]{2,1,0:T(8,128)S(1)} %get-tuple-element.83.refs_1_, f32[24,8,384]{2,1,0:T(8,128)S(1)} %get-tuple-element.84.refs_2_, ...), custom_call_target="tpu_custom_call" | custom-call | tf_op jit(solution)/shard_map/pallas_call | solution.py:23
  31.1 1.3 %collective-permute-start.5 = (f32[12,8,256]{2,1,0:T(8,128)S(1)}, f32[12,8,256]{2,1,0:T(8,128)S(1)}, u32[]{:S(2)}, u32[]{:S(2)}) collective-permute-start(f32[12,8,256]{2,1,0:T(8,128)S(1)} %get-tuple-element.102), channel_id=1, source_target_pairs={{0,2},{2,0},{1,3},{3,1},{4,6},{6,4},{5,7},{7,5},{8,10},{10,8},{9,1... | collective-permute-start | bytes 294920 | tf_op jit(solution)/shard_map/ppermute | solution.py:588
  32.3 0.0 collective-permute-done.6.refs_1_
  32.3 0.5 %collective-permute-done.7.refs_2_ = f32[13,16,128]{2,1,0:T(8,128)S(1)} collective-permute-done((f32[13,16,128]{2,1,0:T(8,128)S(1)}, f32[13,16,128]{2,1,0:T(8,128)S(1)}, u32[]{:S(2)}, u32[]{:S(2)}) %collective-permute-start.7) | collective-permute-done | bytes 106528 | tf_op jit(solution)/shard_map/ppermute | solution.py:574
  32.9 0.0 collective-permute-done.8.refs_3_
  32.9 0.5 %shard_map.83.refs_2_ = f32[12,8,512]{2,1,0:T(8,128)S(1)} custom-call(f32[13,16,128]{2,1,0:T(8,128)S(1)} %get-tuple-element.103.refs_0_, f32[13,16,128]{2,1,0:T(8,128)S(1)} %collective-permute-done.6.refs_1_, f32[13,16,128]{2,1,0:T(8,128)S(1)} %collective-permute-done.7.refs_2_, f32[13,16,128]{2,1,0:T(8,128)S(1)} %collective-permute-done.8.refs_3_), custom_call_target="tpu_custom_call" | custom-call | tf_op jit(solution)/shard_map/pallas_call | solution.py:23
  33.4 2.3 %collective-permute-done.5.refs_1_ = f32[12,8,256]{2,1,0:T(8,128)S(1)} collective-permute-done((f32[12,8,256]{2,1,0:T(8,128)S(1)}, f32[12,8,256]{2,1,0:T(8,128)S(1)}, u32[]{:S(2)}, u32[]{:S(2)}) %collective-permute-start.5) | collective-permute-done | bytes 98336 | tf_op jit(solution)/shard_map/ppermute | solution.py:588
  35.7 0.7 %shard_map.84 = f32[12,8,512]{2,1,0:T(8,128)} custom-call(f32[12,8,256]{2,1,0:T(8,128)S(1)} %get-tuple-element.101.refs_0_, f32[12,8,256]{2,1,0:T(8,128)S(1)} %collective-permute-done.5.refs_1_, f32[12,8,512]{2,1,0:T(8,128)S(1)} %shard_map.83.refs_2_), custom_call_target="tpu_custom_call" | custom-call | tf_op jit(solution)/shard_map/pallas_call | solution.py:23
Async XLA Ops:
  2.1 10.7 %collective-permute-start = (f32[80,8,128]{2,1,0:T(8,128)S(1)}, f32[80,8,128]{2,1,0:T(8,128)S(1)}, u32[]{:S(2)}, u32[]{:S(2)}) collective-permute-start(f32[80,8,128]{2,1,0:T(8,128)S(1)} %get-tuple-element.55), channel_id=1, source_target_pairs={{0,2},{2,0},{1,3},{3,1},{4,6},{6,4},{5,7},{7,5},{8,10},{10,8},{9,1... | collective-permute-start | bytes 983048 | tf_op jit(solution)/shard_map/ppermute | solution.py:554
  5.1 11.1 %copy-start = (f32[1,12,64,128]{3,2,1,0:T(8,128)S(1)}, f32[1,12,64,128]{3,2,1,0:T(8,128)}, u32[]{:S(2)}) copy-start(f32[1,12,64,128]{3,2,1,0:T(8,128)} %param.9) | copy-start | bytes 1179652
  5.2 11.6 %collective-permute-start.3 = (f32[93,8,128]{2,1,0:T(8,128)S(1)}, f32[93,8,128]{2,1,0:T(8,128)S(1)}, u32[]{:S(2)}, u32[]{:S(2)}) collective-permute-start(f32[93,8,128]{2,1,0:T(8,128)S(1)} %get-tuple-element.59), channel_id=1, source_target_pairs={{0,4},{1,5},{4,0},{5,1},{8,12},{9,13},{12,8},{13,9},{2,6},{3,7},{6... | collective-permute-start | bytes 1142792 | tf_op jit(solution)/shard_map/ppermute | solution.py:557
  6.8 10.0 %collective-permute-start.4 = (f32[93,8,128]{2,1,0:T(8,128)S(1)}, f32[93,8,128]{2,1,0:T(8,128)S(1)}, u32[]{:S(2)}, u32[]{:S(2)}) collective-permute-start(f32[93,8,128]{2,1,0:T(8,128)S(1)} %get-tuple-element.60), channel_id=1, source_target_pairs={{0,1},{1,0},{4,8},{5,9},{8,4},{9,5},{12,13},{13,12},{2,3},{3,2},{6... | collective-permute-start | bytes 1142792 | tf_op jit(solution)/shard_map/ppermute | solution.py:556
  13.5 1.8 %copy-start.1 = (s32[64,1]{0,1:T(1,128)S(1)}, s32[64,1]{0,1:T(1,128)}, u32[]{:S(2)}) copy-start(s32[64,1]{0,1:T(1,128)} %param.10) | copy-start | bytes 772
  13.5 7.4 %collective-permute-start.1 = (f32[60,8,128]{2,1,0:T(8,128)}, f32[60,8,128]{2,1,0:T(8,128)S(1)}, u32[]{:S(2)}, u32[]{:S(2)}) collective-permute-start(f32[60,8,128]{2,1,0:T(8,128)} %get-tuple-element.56), channel_id=1, source_target_pairs={{0,4},{1,5},{4,0},{5,1},{8,12},{9,13},{12,8},{13,9},{2,6},{3,7},{6... | collective-permute-start | bytes 737288 | tf_op jit(solution)/shard_map/ppermute | solution.py:560
  15.3 5.5 %collective-permute-start.2 = (f32[60,8,128]{2,1,0:T(8,128)S(1)}, f32[60,8,128]{2,1,0:T(8,128)S(1)}, u32[]{:S(2)}, u32[]{:S(2)}) collective-permute-start(f32[60,8,128]{2,1,0:T(8,128)S(1)} %get-tuple-element.57), channel_id=1, source_target_pairs={{0,1},{1,0},{4,8},{5,9},{8,4},{9,5},{12,13},{13,12},{2,3},{3,2},{6... | collective-permute-start | bytes 737288 | tf_op jit(solution)/shard_map/ppermute | solution.py:559
  20.9 11.5 %collective-permute-start.6 = (f32[13,16,128]{2,1,0:T(8,128)S(1)}, f32[13,16,128]{2,1,0:T(8,128)S(1)}, u32[]{:S(2)}, u32[]{:S(2)}) collective-permute-start(f32[13,16,128]{2,1,0:T(8,128)S(1)} %get-tuple-element.104), channel_id=1, source_target_pairs={{0,4},{4,0},{8,12},{12,8},{1,5},{5,1},{9,13},{13,9},{2,6},{6,2},{1... | collective-permute-start | bytes 319496 | tf_op jit(solution)/shard_map/ppermute | solution.py:574
  23.5 9.4 %collective-permute-start.7 = (f32[13,16,128]{2,1,0:T(8,128)S(1)}, f32[13,16,128]{2,1,0:T(8,128)S(1)}, u32[]{:S(2)}, u32[]{:S(2)}) collective-permute-start(f32[13,16,128]{2,1,0:T(8,128)S(1)} %get-tuple-element.105), channel_id=1, source_target_pairs={{0,8},{4,12},{8,0},{12,4},{1,9},{5,13},{9,1},{13,5},{2,10},{6,14},... | collective-permute-start | bytes 319496 | tf_op jit(solution)/shard_map/ppermute | solution.py:574
  25.0 7.9 %collective-permute-start.8 = (f32[13,16,128]{2,1,0:T(8,128)S(1)}, f32[13,16,128]{2,1,0:T(8,128)S(1)}, u32[]{:S(2)}, u32[]{:S(2)}) collective-permute-start(f32[13,16,128]{2,1,0:T(8,128)S(1)} %get-tuple-element.106), channel_id=1, source_target_pairs={{0,12},{4,8},{8,4},{12,0},{1,13},{5,9},{9,5},{13,1},{2,14},{6,10},... | collective-permute-start | bytes 319496 | tf_op jit(solution)/shard_map/ppermute | solution.py:574
  31.1 4.6 %collective-permute-start.5 = (f32[12,8,256]{2,1,0:T(8,128)S(1)}, f32[12,8,256]{2,1,0:T(8,128)S(1)}, u32[]{:S(2)}, u32[]{:S(2)}) collective-permute-start(f32[12,8,256]{2,1,0:T(8,128)S(1)} %get-tuple-element.102), channel_id=1, source_target_pairs={{0,2},{2,0},{1,3},{3,1},{4,6},{6,4},{5,7},{7,5},{8,10},{10,8},{9,1... | collective-permute-start | bytes 294920 | tf_op jit(solution)/shard_map/ppermute | solution.py:588

commit v7 on v6

--- a/solution.py
+++ b/solution.py
@@ -13,7 +13,7 @@
 F32 = jnp.float32
 
 
-def call(body, out_shapes, *args, scratch=(), semaphores=0, inputs=pltpu.VMEM, keep=False):
+def call(body, out_shapes, *args, scratch=(), semaphores=0, inputs=pltpu.VMEM):
     spec = pl.BlockSpec(memory_space=pltpu.VMEM)
     if inputs == pltpu.HBM:
         args = [pltpu.with_memory_space_constraint(arg, pltpu.HBM) for arg in args]
@@ -22,7 +22,7 @@
         shapes.append(pltpu.SemaphoreType.DMA((semaphores,)))
     return pl.pallas_call(
         body,
-        out_shape=[pltpu.VMEM(shape, F32) if keep else jax.ShapeDtypeStruct(shape, F32) for shape in out_shapes],
+        out_shape=[jax.ShapeDtypeStruct(shape, F32) for shape in out_shapes],
         in_specs=[pl.BlockSpec(memory_space=inputs)] * len(args),
         out_specs=[spec] * len(out_shapes),
         scratch_shapes=shapes,
@@ -231,18 +231,16 @@
     by_parity(rows)
 
 
-def forward_rows_body(plan, *refs):
-    turns = plan.devices - 1
-    got, swap_a, swap_b = refs[:turns], refs[turns], refs[turns + 1]
+def forward_rows_body(plan, first_swap, *refs):
+    got, swap = refs[:-1], refs[-1]
     size = plan.packed(plan.sent_size)
 
     def rows(even):
-        for north, swap in ((even, swap_a), (not even, swap_b)):
-            for turn in range(turns):
-                def store(index, tile, base=turn * size, swap=swap):
-                    swap[base + index] = tile
-
-                pack_rows(plan, lambda i, turn=turn: got[turn][i], plan.sent_size, north, store)
+        for turn, part in enumerate(got):
+            def store(index, tile, base=turn * size):
+                swap[base + index] = tile
+
+            pack_rows(plan, part.__getitem__, plan.sent_size, even == first_swap, store)
 
     by_parity(rows)
 
@@ -555,7 +553,8 @@
     early_a, early_b = call(functools.partial(pack_rows_body, plan), [(early,) + tile] * 2, own)
     early_b = lax.ppermute(early_b, ("lat", "tr"), swaps_b)
     early_a = lax.ppermute(early_a, ("lat", "tr"), swaps_a)
-    late_a, late_b = call(functools.partial(forward_rows_body, plan), [(late,) + tile] * 2, *got, keep=True)
+    (late_b,) = call(functools.partial(forward_rows_body, plan, False), [(late,) + tile], *got)
+    (late_a,) = call(functools.partial(forward_rows_body, plan, True), [(late,) + tile], *got)
     late_b = lax.ppermute(late_b, ("lat", "tr"), swaps_b)
     late_a = lax.ppermute(late_a, ("lat", "tr"), swaps_a)
     state = call(

time: 36.5 us -> 37.5 us (1.027)
  waiting for transfers between devices: 12.2 us -> 13.6 us
  starting transfers between devices: 13 us -> 12.2 us
    ppermute x1, waiting for transfers between devices: 0.01 us -> 1.62 us  [local(): early_a = lax.ppermute(early_a, ('lat', 'tr'), swaps_a)]
    ppermute x3, waiting for transfers between devices: 0.53 us -> 1.65 us  [local(): crossing[turn] = lax.ppermute(buckets[turn], 'lat', rounds(bands)[turn - 1])]
    ppermute x2, waiting for transfers between devices: 8.26 us -> 7.23 us  [local(): lax.ppermute(part, 'lev', pairs)]
    ppermute x2, starting transfers between devices: 4.3 us -> 3.54 us  [local(): lax.ppermute(part, 'lev', pairs)]
    unnamed x5 -> x7, local copies, waits for them, and re-layouts: 0.1 us -> 0.76 us
    reshape x1, local copies, waits for them, and re-layouts: 0.74 us -> 0.1 us  [bucket_tiles(): tile_cell.reshape(tiles, 1)]
    pallas_call x8 -> x9, Pallas kernels: 9.6 us -> 9.94 us  [call(): pl.pallas_call(body, out_shape=[jax.ShapeDtypeStruct(shape, F32) for shap...]
  transfers between devices with their start and end apart: 9 -> 9, of which waited for: 4 -> 5; matrix products, arithmetic and copies ran while one was open for 2% -> 1% of each run, Pallas kernels for 21% -> 21%
where the time goes in v7:
time: 37.5 us; the launch traced here: 37.3 us
  waiting for transfers between devices  13.6 us (36%)
  starting transfers between devices  12.2 us (33%)
  Pallas kernels  9.94 us (27%)
  local copies, waits for them, and re-layouts  0.86 us (2%)
  between operations  0.7 us (2%)
    pallas_call x9, Pallas kernels, call(): pl.pallas_call(body, out_shape=[jax.ShapeDtypeStruct(shape, F32) for shap...  9.94 us
    ppermute x2, waiting for transfers between devices, local(): lax.ppermute(part, 'lev', pairs)  7.23 us
    ppermute x3, starting transfers between devices, local(): crossing[turn] = lax.ppermute(buckets[turn], 'lat', rounds(bands)[turn - 1])  5.14 us
    ppermute x2, starting transfers between devices, local(): lax.ppermute(part, 'lev', pairs)  3.54 us
    ppermute x1, waiting for transfers between devices, local(): late_a = lax.ppermute(late_a, ('lat', 'tr'), swaps_a)  3.11 us
    ppermute x1, starting transfers between devices, local(): late_a = lax.ppermute(late_a, ('lat', 'tr'), swaps_a)  1.89 us
    ppermute x3, waiting for transfers between devices, local(): crossing[turn] = lax.ppermute(buckets[turn], 'lat', rounds(bands)[turn - 1])  1.65 us
    ppermute x1, waiting for transfers between devices, local(): early_a = lax.ppermute(early_a, ('lat', 'tr'), swaps_a)  1.62 us
  transfers between devices with their start and end apart: 9, of which 5 were waited for; matrix products, arithmetic and copies ran while one was open for 1% of the time, Pallas kernels for 21%

profile of v7, /device:TPU:0, one launch (start us, length us, event | category | flops | bytes accessed | tf_op | source)
XLA Modules:
  0.0 37.3 jit_solution(13762476052749236761)
XLA Ops:
  0.6 1.4 %shard_map.77 = (f32[123,8,128]{2,1,0:T(8,128)S(1)}, f32[80,8,128]{2,1,0:T(8,128)S(1)}) custom-call(f32[12,8,512]{2,1,0:T(8,128)} %bitcast.8, f32[2,12,8,512]{3,2,1,0:T(8,128)} %refs_1_.1, f32[23,8,256]{2,1,0:T(8,128)} %refs_2_.1), custom_call_target="tpu_custom_call" | custom-call | tf_op jit(solution)/shard_map/pallas_call | solution.py:23
  2.1 3.0 %collective-permute-start = (f32[80,8,128]{2,1,0:T(8,128)S(1)}, f32[80,8,128]{2,1,0:T(8,128)S(1)}, u32[]{:S(2)}, u32[]{:S(2)}) collective-permute-start(f32[80,8,128]{2,1,0:T(8,128)S(1)} %get-tuple-element.53), channel_id=1, source_target_pairs={{0,2},{2,0},{1,3},{3,1},{4,6},{6,4},{5,7},{7,5},{8,10},{10,8},{9,1... | collective-permute-start | bytes 983048 | tf_op jit(solution)/shard_map/ppermute | solution.py:552
  5.1 0.8 %shard_map.80 = (f32[93,8,128]{2,1,0:T(8,128)}, f32[93,8,128]{2,1,0:T(8,128)S(1)}) custom-call(f32[123,8,128]{2,1,0:T(8,128)S(1)} %get-tuple-element.54.own.refs_0_), custom_call_target="tpu_custom_call" | custom-call | tf_op jit(solution)/shard_map/pallas_call | solution.py:23
  5.9 1.6 %collective-permute-start.3 = (f32[93,8,128]{2,1,0:T(8,128)}, f32[93,8,128]{2,1,0:T(8,128)S(1)}, u32[]{:S(2)}, u32[]{:S(2)}) collective-permute-start(f32[93,8,128]{2,1,0:T(8,128)} %get-tuple-element.55), channel_id=1, source_target_pairs={{0,4},{1,5},{4,0},{5,1},{8,12},{9,13},{12,8},{13,9},{2,6},{3,7},{6... | collective-permute-start | bytes 1142792 | tf_op jit(solution)/shard_map/ppermute | solution.py:555
  7.5 0.0 collective-permute-start.4
  7.5 5.3 %collective-permute-done.refs_0_.refs_3_ = f32[80,8,128]{2,1,0:T(8,128)S(1)} collective-permute-done((f32[80,8,128]{2,1,0:T(8,128)S(1)}, f32[80,8,128]{2,1,0:T(8,128)S(1)}, u32[]{:S(2)}, u32[]{:S(2)}) %collective-permute-start) | collective-permute-done | bytes 327712 | tf_op jit(solution)/shard_map/ppermute | solution.py:552
  12.8 0.0 copy-start.1
  12.8 0.0 copy-start
  12.8 1.9 %collective-permute-start.1 = (f32[60,8,128]{2,1,0:T(8,128)S(1)}, f32[60,8,128]{2,1,0:T(8,128)S(1)}, u32[]{:S(2)}, u32[]{:S(2)}) collective-permute-start(f32[60,8,128]{2,1,0:T(8,128)S(1)} %shard_map.78), channel_id=1, source_target_pairs={{0,4},{1,5},{4,0},{5,1},{8,12},{9,13},{12,8},{13,9},{2,6},{3,7},{6... | collective-permute-start | bytes 737288 | tf_op jit(solution)/shard_map/ppermute | solution.py:559
  14.8 0.1 collective-permute-start.2
  14.8 0.0 copy-done.1
  14.8 0.1 copy.8.region_column
  14.9 0.7 %copy-done.2 = s32[64]{0:T(128)S(1)} copy-done((s32[64]{0:T(128)S(1)}, s32[64]{0:T(128)}, u32[]{:S(2)}) %copy-start.2) | copy-done | bytes 280
  15.6 0.1 copy.9.cell_column
  15.7 0.0 copy-done
  15.7 0.6 %shard_map.82 = (f32[13,16,128]{2,1,0:T(8,128)S(1)}, f32[13,16,128]{2,1,0:T(8,128)S(1)}, f32[13,16,128]{2,1,0:T(8,128)S(1)}, f32[13,16,128]{2,1,0:T(8,128)S(1)}) custom-call(f32[12,64,128]{2,1,0:T(8,128)S(1)} %bitcast.6, s32[64,1]{1,0:T(8,128)S(1)} %copy.8.region_column, s32[1,64]{1,0:T(1,128)S(1)} %bitcast.7, s32[64,1]{1,0:T(8,128)S(1)} %copy.9.cell_column), custom_call_target="tpu_custom_call" | custom-call | tf_op jit(solution)/shard_map/pallas_call | solution.py:23
  16.3 1.6 %collective-permute-done.3.refs_1_ = f32[93,8,128]{2,1,0:T(8,128)S(1)} collective-permute-done((f32[93,8,128]{2,1,0:T(8,128)}, f32[93,8,128]{2,1,0:T(8,128)S(1)}, u32[]{:S(2)}, u32[]{:S(2)}) %collective-permute-start.3) | collective-permute-done | bytes 380960 | tf_op jit(solution)/shard_map/ppermute | solution.py:555
  17.9 0.0 collective-permute-done.4.refs_2_
  17.9 0.7 %shard_map.81 = (f32[24,8,384]{2,1,0:T(8,128)S(1)}, f32[24,8,384]{2,1,0:T(8,128)S(1)}, f32[24,8,384]{2,1,0:T(8,128)S(1)}, f32[24,8,384]{2,1,0:T(8,128)S(1)}, f32...) custom-call(f32[123,8,128]{2,1,0:T(8,128)S(1)} %get-tuple-element.54, ...), custom_call_target="tpu_custom_call" | custom-call | tf_op jit(solution)/shard_map/pallas_call | solution.py:23
  18.6 3.1 %collective-permute-done.1.refs_17_ = f32[60,8,128]{2,1,0:T(8,128)S(1)} collective-permute-done((f32[60,8,128]{2,1,0:T(8,128)S(1)}, f32[60,8,128]{2,1,0:T(8,128)S(1)}, u32[]{:S(2)}, u32[]{:S(2)}) %collective-permute-start.1) | collective-permute-done | bytes 245792 | tf_op jit(solution)/shard_map/ppermute | solution.py:559
  21.7 0.0 collective-permute-done.2.refs_18_
  21.7 2.5 %collective-permute-start.6 = (f32[13,16,128]{2,1,0:T(8,128)S(1)}, f32[13,16,128]{2,1,0:T(8,128)S(1)}, u32[]{:S(2)}, u32[]{:S(2)}) collective-permute-start(f32[13,16,128]{2,1,0:T(8,128)S(1)} %get-tuple-element.100), channel_id=1, source_target_pairs={{0,4},{4,0},{8,12},{12,8},{1,5},{5,1},{9,13},{13,9},{2,6},{6,2},{1... | collective-permute-start | bytes 319496 | tf_op jit(solution)/shard_map/ppermute | solution.py:573
  24.2 1.7 %collective-permute-start.7 = (f32[13,16,128]{2,1,0:T(8,128)S(1)}, f32[13,16,128]{2,1,0:T(8,128)S(1)}, u32[]{:S(2)}, u32[]{:S(2)}) collective-permute-start(f32[13,16,128]{2,1,0:T(8,128)S(1)} %get-tuple-element.101), channel_id=1, source_target_pairs={{0,8},{4,12},{8,0},{12,4},{1,9},{5,13},{9,1},{13,5},{2,10},{6,14},... | collective-permute-start | bytes 319496 | tf_op jit(solution)/shard_map/ppermute | solution.py:573
  25.8 1.0 %collective-permute-start.8 = (f32[13,16,128]{2,1,0:T(8,128)S(1)}, f32[13,16,128]{2,1,0:T(8,128)S(1)}, u32[]{:S(2)}, u32[]{:S(2)}) collective-permute-start(f32[13,16,128]{2,1,0:T(8,128)S(1)} %get-tuple-element.102), channel_id=1, source_target_pairs={{0,12},{4,8},{8,4},{12,0},{1,13},{5,9},{9,5},{13,1},{2,14},{6,10},... | collective-permute-start | bytes 319496 | tf_op jit(solution)/shard_map/ppermute | solution.py:573
  26.8 5.2 %shard_map.83 = (f32[12,8,256]{2,1,0:T(8,128)S(1)}, f32[12,8,256]{2,1,0:T(8,128)S(1)}, f32[8,256]{1,0:T(8,128)}) custom-call(f32[24,8,384]{2,1,0:T(8,128)S(1)} %get-tuple-element.78.refs_0_, f32[24,8,384]{2,1,0:T(8,128)S(1)} %get-tuple-element.79.refs_1_, f32[24,8,384]{2,1,0:T(8,128)S(1)} %get-tuple-element.80.refs_2_, ...), custom_call_target="tpu_custom_call" | custom-call | tf_op jit(solution)/shard_map/pallas_call | solution.py:23
  32.0 0.5 %collective-permute-start.5 = (f32[12,8,256]{2,1,0:T(8,128)S(1)}, f32[12,8,256]{2,1,0:T(8,128)S(1)}, u32[]{:S(2)}, u32[]{:S(2)}) collective-permute-start(f32[12,8,256]{2,1,0:T(8,128)S(1)} %get-tuple-element.98), channel_id=1, source_target_pairs={{0,2},{2,0},{1,3},{3,1},{4,6},{6,4},{5,7},{7,5},{8,10},{10,8},{9,1... | collective-permute-start | bytes 294920 | tf_op jit(solution)/shard_map/ppermute | solution.py:587
  32.5 0.0 collective-permute-done.6.refs_1_
  32.5 1.6 %collective-permute-done.7.refs_2_ = f32[13,16,128]{2,1,0:T(8,128)S(1)} collective-permute-done((f32[13,16,128]{2,1,0:T(8,128)S(1)}, f32[13,16,128]{2,1,0:T(8,128)S(1)}, u32[]{:S(2)}, u32[]{:S(2)}) %collective-permute-start.7) | collective-permute-done | bytes 106528 | tf_op jit(solution)/shard_map/ppermute | solution.py:573
  34.2 0.0 collective-permute-done.8.refs_3_
  34.2 0.5 %shard_map.84.refs_2_ = f32[12,8,512]{2,1,0:T(8,128)S(1)} custom-call(f32[13,16,128]{2,1,0:T(8,128)S(1)} %get-tuple-element.99.refs_0_, f32[13,16,128]{2,1,0:T(8,128)S(1)} %collective-permute-done.6.refs_1_, f32[13,16,128]{2,1,0:T(8,128)S(1)} %collective-permute-done.7.refs_2_, f32[13,16,128]{2,1,0:T(8,128)S(1)} %collective-permute-done.8.refs_3_), custom_call_target="tpu_custom_call" | custom-call | tf_op jit(solution)/shard_map/pallas_call | solution.py:23
  34.7 1.9 %collective-permute-done.5.refs_1_ = f32[12,8,256]{2,1,0:T(8,128)S(1)} collective-permute-done((f32[12,8,256]{2,1,0:T(8,128)S(1)}, f32[12,8,256]{2,1,0:T(8,128)S(1)}, u32[]{:S(2)}, u32[]{:S(2)}) %collective-permute-start.5) | collective-permute-done | bytes 98336 | tf_op jit(solution)/shard_map/ppermute | solution.py:587
  36.6 0.7 %shard_map.85 = f32[12,8,512]{2,1,0:T(8,128)} custom-call(f32[12,8,256]{2,1,0:T(8,128)S(1)} %get-tuple-element.97.refs_0_, f32[12,8,256]{2,1,0:T(8,128)S(1)} %collective-permute-done.5.refs_1_, f32[12,8,512]{2,1,0:T(8,128)S(1)} %shard_map.84.refs_2_), custom_call_target="tpu_custom_call" | custom-call | tf_op jit(solution)/shard_map/pallas_call | solution.py:23
  (3 shorter events, 0.0 us)
Async XLA Ops:
  2.1 10.7 %collective-permute-start = (f32[80,8,128]{2,1,0:T(8,128)S(1)}, f32[80,8,128]{2,1,0:T(8,128)S(1)}, u32[]{:S(2)}, u32[]{:S(2)}) collective-permute-start(f32[80,8,128]{2,1,0:T(8,128)S(1)} %get-tuple-element.53), channel_id=1, source_target_pairs={{0,2},{2,0},{1,3},{3,1},{4,6},{6,4},{5,7},{7,5},{8,10},{10,8},{9,1... | collective-permute-start | bytes 983048 | tf_op jit(solution)/shard_map/ppermute | solution.py:552
  5.9 12.0 %collective-permute-start.3 = (f32[93,8,128]{2,1,0:T(8,128)}, f32[93,8,128]{2,1,0:T(8,128)S(1)}, u32[]{:S(2)}, u32[]{:S(2)}) collective-permute-start(f32[93,8,128]{2,1,0:T(8,128)} %get-tuple-element.55), channel_id=1, source_target_pairs={{0,4},{1,5},{4,0},{5,1},{8,12},{9,13},{12,8},{13,9},{2,6},{3,7},{6... | collective-permute-start | bytes 1142792 | tf_op jit(solution)/shard_map/ppermute | solution.py:555
  7.5 10.4 %collective-permute-start.4 = (f32[93,8,128]{2,1,0:T(8,128)S(1)}, f32[93,8,128]{2,1,0:T(8,128)S(1)}, u32[]{:S(2)}, u32[]{:S(2)}) collective-permute-start(f32[93,8,128]{2,1,0:T(8,128)S(1)} %get-tuple-element.56), channel_id=1, source_target_pairs={{0,1},{1,0},{4,8},{5,9},{8,4},{9,5},{12,13},{13,12},{2,3},{3,2},{6... | collective-permute-start | bytes 1142792 | tf_op jit(solution)/shard_map/ppermute | solution.py:554
  12.8 2.0 %copy-start.1 = (s32[64,1]{0,1:T(1,128)S(1)}, s32[64,1]{0,1:T(1,128)}, u32[]{:S(2)}) copy-start(s32[64,1]{0,1:T(1,128)} %param.10) | copy-start | bytes 772
  12.8 2.9 %copy-start = (f32[1,12,64,128]{3,2,1,0:T(8,128)S(1)}, f32[1,12,64,128]{3,2,1,0:T(8,128)}, u32[]{:S(2)}) copy-start(f32[1,12,64,128]{3,2,1,0:T(8,128)} %param.9) | copy-start | bytes 1179652
  12.8 8.8 %collective-permute-start.1 = (f32[60,8,128]{2,1,0:T(8,128)S(1)}, f32[60,8,128]{2,1,0:T(8,128)S(1)}, u32[]{:S(2)}, u32[]{:S(2)}) collective-permute-start(f32[60,8,128]{2,1,0:T(8,128)S(1)} %shard_map.78), channel_id=1, source_target_pairs={{0,4},{1,5},{4,0},{5,1},{8,12},{9,13},{12,8},{13,9},{2,6},{3,7},{6... | collective-permute-start | bytes 737288 | tf_op jit(solution)/shard_map/ppermute | solution.py:559
  14.8 6.9 %collective-permute-start.2 = (f32[60,8,128]{2,1,0:T(8,128)S(1)}, f32[60,8,128]{2,1,0:T(8,128)S(1)}, u32[]{:S(2)}, u32[]{:S(2)}) collective-permute-start(f32[60,8,128]{2,1,0:T(8,128)S(1)} %shard_map.79), channel_id=1, source_target_pairs={{0,1},{1,0},{4,8},{5,9},{8,4},{9,5},{12,13},{13,12},{2,3},{3,2},{6... | collective-permute-start | bytes 737288 | tf_op jit(solution)/shard_map/ppermute | solution.py:558
  14.9 0.7 %copy-start.2 = (s32[64]{0:T(128)S(1)}, s32[64]{0:T(128)}, u32[]{:S(2)}) copy-start(s32[64]{0:T(128)} %param.11) | copy-start | bytes 772
  21.7 10.9 %collective-permute-start.6 = (f32[13,16,128]{2,1,0:T(8,128)S(1)}, f32[13,16,128]{2,1,0:T(8,128)S(1)}, u32[]{:S(2)}, u32[]{:S(2)}) collective-permute-start(f32[13,16,128]{2,1,0:T(8,128)S(1)} %get-tuple-element.100), channel_id=1, source_target_pairs={{0,4},{4,0},{8,12},{12,8},{1,5},{5,1},{9,13},{13,9},{2,6},{6,2},{1... | collective-permute-start | bytes 319496 | tf_op jit(solution)/shard_map/ppermute | solution.py:573
  24.2 10.0 %collective-permute-start.7 = (f32[13,16,128]{2,1,0:T(8,128)S(1)}, f32[13,16,128]{2,1,0:T(8,128)S(1)}, u32[]{:S(2)}, u32[]{:S(2)}) collective-permute-start(f32[13,16,128]{2,1,0:T(8,128)S(1)} %get-tuple-element.101), channel_id=1, source_target_pairs={{0,8},{4,12},{8,0},{12,4},{1,9},{5,13},{9,1},{13,5},{2,10},{6,14},... | collective-permute-start | bytes 319496 | tf_op jit(solution)/shard_map/ppermute | solution.py:573
  25.8 8.4 %collective-permute-start.8 = (f32[13,16,128]{2,1,0:T(8,128)S(1)}, f32[13,16,128]{2,1,0:T(8,128)S(1)}, u32[]{:S(2)}, u32[]{:S(2)}) collective-permute-start(f32[13,16,128]{2,1,0:T(8,128)S(1)} %get-tuple-element.102), channel_id=1, source_target_pairs={{0,12},{4,8},{8,4},{12,0},{1,13},{5,9},{9,5},{13,1},{2,14},{6,10},... | collective-permute-start | bytes 319496 | tf_op jit(solution)/shard_map/ppermute | solution.py:573
  32.0 4.6 %collective-permute-start.5 = (f32[12,8,256]{2,1,0:T(8,128)S(1)}, f32[12,8,256]{2,1,0:T(8,128)S(1)}, u32[]{:S(2)}, u32[]{:S(2)}) collective-permute-start(f32[12,8,256]{2,1,0:T(8,128)S(1)} %get-tuple-element.98), channel_id=1, source_target_pairs={{0,2},{2,0},{1,3},{3,1},{4,6},{6,4},{5,7},{7,5},{8,10},{10,8},{9,1... | collective-permute-start | bytes 294920 | tf_op jit(solution)/shard_map/ppermute | solution.py:587
